TPU v7x, 32 devices: a whole 2x2x4 slice. The times are simulated.
32 devices in a mesh: dom: 8 (over z, x), feat: 4 (over y, core).
Axes of the slice: x: 2, y: 2, z: 4, core: 2. Of those that a mesh axis runs over, the one named last changes fastest.
Arguments:
- feats: bfloat16 [16384, 768], P('dom', 'feat'), may hold values from -6 to 6
- tile_vals: bfloat16 [1536, 128, 128], P('dom'), may hold values from 0 to 1
- tile_dst: int32 [1536], P('dom'), may hold values from 0 to 15
- tile_src: int32 [1536], P('dom'), may hold values from 0 to 79
- tile_count: int32 [8], P('dom'), may hold values from 96 to 192, as said below
- send_blocks: int32 [8, 8, 8], P('dom'), may hold values from 0 to 15
- send_count: int32 [8, 8], P('dom'), may hold values from 1 to 8, as said below
- w_self: bfloat16 [3, 768, 768], replicated, may hold values from -0.21875 to 0.21875
- w_nbr: bfloat16 [3, 768, 768], replicated, may hold values from -0.21875 to 0.21875
- bias: float32 [3, 768], replicated, may hold values from -3 to 3
Outputs:
- hidden: bfloat16 [16384, 768], P('dom', 'feat')
Inputs may be any that keep to these rules, and one draw needn't show every extreme that they name: `tile_count`: some partition has exactly 192 live tiles. `send_count`: some partition sends exactly 8 blocks to some peer.
All inputs are finite; a program needn't handle non-finite values.
Results may differ from a plain program's by a relative error of at most 0.0085.
Values may be sent and summed in bfloat16 or wider, within the bound.
No kernel may reach another device: no remote copies, remote signals or barrier semaphores. Data moves between devices by JAX's collectives and lax.ppermute only.
A program may use at most 128 MiB of HBM per device.

v0:
```python
import jax
import jax.numpy as jnp
from jax import lax
from jax.sharding import PartitionSpec as P

LAYERS = 3
BLK = 128
PEERS = 8
SLOTS = 8


def from_behind(block, axis, distance):
    devices = range(lax.axis_size(axis))
    route = [((i - distance) % len(devices), i) for i in devices]
    return lax.ppermute(block, axis, route)


def per_device(
    feats, tile_vals, tile_dst, tile_src, tile_count, send_blocks, send_count, w_self, w_nbr, bias
):
    node_rows, cols = feats.shape
    blk_dev = node_rows // BLK
    tiles_here = tile_vals.shape[0]
    column_start = lax.axis_index("feat") * cols
    offsets = [(d // 2 + 1) * (1 if d % 2 == 0 else -1) for d in range(PEERS)]
    live = (jnp.arange(tiles_here, dtype=jnp.int32) < tile_count[0]).astype(jnp.bfloat16)
    masked = tile_vals * live[:, None, None]
    onehot = (tile_dst[None, :] == jnp.arange(blk_dev, dtype=jnp.int32)[:, None]).astype(
        jnp.float32
    )
    row_sums = jnp.sum(masked.astype(jnp.float32), axis=2)
    degree = 1.0 + jnp.dot(onehot, row_sums, preferred_element_type=jnp.float32)
    slot_ids = jnp.arange(SLOTS, dtype=jnp.int32)
    hidden = feats
    for layer in range(LAYERS):
        blocks_here = hidden.reshape(blk_dev, BLK, cols)
        outgoing = []
        for d in range(PEERS):
            filled = (slot_ids < send_count[0, d]).astype(jnp.bfloat16)
            outgoing.append(blocks_here[send_blocks[0, d]] * filled[:, None, None])
        incoming = [None] * PEERS
        for d in range(PEERS):
            incoming[d] = from_behind(outgoing[d], "dom", offsets[d])
        received = jnp.stack(incoming).reshape(PEERS * SLOTS, BLK, cols)
        source_list = jnp.concatenate([blocks_here, received], axis=0)
        picked = source_list[tile_src]
        contrib = jnp.einsum("tij,tjf->tif", masked, picked, preferred_element_type=jnp.float32)
        summed = jnp.einsum("bt,tif->bif", onehot, contrib, preferred_element_type=jnp.float32)
        agg_blocks = (summed / degree[:, :, None]).astype(jnp.bfloat16)
        agg = agg_blocks.reshape(node_rows, cols)
        last_layer = layer == LAYERS - 1
        bias_here = lax.dynamic_slice_in_dim(bias[layer], column_start, cols, 0)
        self_cols = lax.dynamic_slice_in_dim(w_self[layer], column_start, cols, 1)
        nbr_cols = lax.dynamic_slice_in_dim(w_nbr[layer], column_start, cols, 1)
        total = jnp.dot(
            lax.all_gather(hidden, "feat", axis=1, tiled=True),
            self_cols,
            preferred_element_type=jnp.float32,
        )
        pre = total + jnp.dot(
            lax.all_gather(agg, "feat", axis=1, tiled=True),
            nbr_cols,
            preferred_element_type=jnp.float32,
        )
        pre = pre + bias_here[None, :]
        if not last_layer:
            pre = jax.nn.relu(pre)
        hidden = pre.astype(jnp.bfloat16)
    return hidden


def solution(mesh):
    in_specs = (
        P("dom", "feat"),
        P("dom", None, None),
        P("dom"),
        P("dom"),
        P("dom"),
        P("dom", None, None),
        P("dom", None),
        P(),
        P(),
        P(),
    )
    out_specs = P("dom", "feat")
    return jax.shard_map(
        per_device, mesh=mesh, in_specs=in_specs, out_specs=out_specs, check_vma=False
    )
```

profile of v0, /device:TPU:0, one launch (start us, length us, event | category | flops | bytes accessed | tf_op | source)
XLA Modules:
  0.0 529.6 jit_solution(4964081315004327278)
XLA Ops:
  7.3 1.3 copy_bitcast_fusion.5
  9.6 1.6 fusion.68
  13.4 2.9 collective-permute-start
  18.4 3.0 collective-permute-start.1
  25.9 3.8 collective-permute-start.3
  36.9 6.4 %convert_reduce_fusion = bf16[192,128]{1,0:T(8,128)(2,1)S(1)} fusion(bf16[192,128,128]{2,1,0:T(8,128)(2,1)} %param.11, bf16[192]{0:T(256)(128)(2,1)S(1)} %compare_convert_fusion.8), kind=kLoop, calls=%fused_computation.33 | loop fusion | flops 15704064 | bytes 6340992 | tf_op jit(solution)/shard_map/reduce_sum | solution.py:31
  43.5 3.9 collective-permute-start.5
  47.5 3.0 collective-permute-start.7
  50.6 12.8 %collective-permute-done.4 = bf16[8,128,192]{1,2,0:T(8,128)(2,1)} collective-permute-done((bf16[8,128,192]{1,2,0:T(8,128)(2,1)}, bf16[8,128,192]{1,2,0:T(8,128)(2,1)}, u32[]{:S(2)}, u32[]{:S(2)}) %collective-permute-start.4) | collective-permute-done | bytes 393248 | tf_op jit(solution)/shard_map/ppermute | solution.py:15
  65.1 35.0 %collective-permute-done.6 = bf16[8,128,192]{1,2,0:T(8,128)(2,1)S(1)} collective-permute-done((bf16[8,128,192]{1,2,0:T(8,128)(2,1)S(1)}, bf16[8,128,192]{1,2,0:T(8,128)(2,1)S(1)}, u32[]{:S(2)}, u32[]{:S(2)}) %collective-permute-start.6) | collective-permute-done | bytes 393248 | tf_op jit(solution)/shard_map/ppermute | solution.py:15
  100.2 6.9 %collective-permute-done.7 = bf16[8,128,192]{1,2,0:T(8,128)(2,1)S(1)} collective-permute-done((bf16[8,128,192]{1,2,0:T(8,128)(2,1)S(1)}, bf16[8,128,192]{1,2,0:T(8,128)(2,1)S(1)}, u32[]{:S(2)}, u32[]{:S(2)}) %collective-permute-start.7) | collective-permute-done | bytes 393248 | tf_op jit(solution)/shard_map/ppermute | solution.py:15
  107.2 2.3 pad_maximum_fusion
  109.5 12.0 %gather_fusion.8 = bf16[192,128,192]{1,2,0:T(8,128)(2,1)} fusion(bf16[80,128,192]{1,2,0:T(8,128)(2,1)} %pad_maximum_fusion, s32[1024]{0:T(1024)S(1)} %pad_clamp_fusion), kind=kCustom, calls=%fused_computation.8 | custom fusion | bytes 18875136 | tf_op jit(solution)/shard_map/gather | solution.py:46
  121.5 15.7 %fusion.10 = bf16[192,128,192]{1,2,0:T(8,128)(2,1)} fusion(bf16[192,128,192]{1,2,0:T(8,128)(2,1)} %gather_fusion.8, bf16[192,128,128]{2,1,0:T(8,128)(2,1)} %param.11, bf16[192]{0:T(256)(128)(2,1)S(1)} %compare_convert_fusion.8), kind=kOutput, calls=%fused_computation.38 | convolution fusion | flops 1211105280 | bytes 25166208 | tf_op jit(solution)/shard_map/tij,tjf->tif/dot_general | solution.py:47
  137.3 8.9 %divide_convert_fusion.2 = bf16[16,128,192]{1,0,2:T(8,128)(2,1)S(1)} fusion(bf16[192,128,192]{1,2,0:T(8,128)(2,1)} %fusion.10, f32[16,128]{1,0:T(8,128)S(1)} %convolution_add_fusion.3, s32[192]{0:T(256)} %param.12), kind=kOutput, calls=%fused_computation.60 | convolution fusion | flops 151784448 | bytes 10232576 | tf_op jit(solution)/shard_map/bt,tif->bif/dot_general | solution.py:48
  147.8 1.4 fusion.67
  149.3 1.9 fusion.66
  151.2 1.4 copy-done.1
  152.6 1.7 fusion.65
  154.3 3.5 convolution_bitcast_fusion
  157.8 18.0 %all-gather.9.cloned.1.call-done = bf16[2048,768]{0,1:T(8,128)(2,1)} async-done(((bf16[2048,192]{0,1:T(8,128)(2,1)}), bf16[2048,768]{0,1:T(8,128)(2,1)}) %all-gather.9.cloned.1.call-update) | async-done | bytes 3145744 | tf_op jit(solution)/shard_map/all_gather | solution.py:61
  175.8 3.7 fusion.21
  179.5 1.3 copy_bitcast_fusion.4
  180.9 1.5 gather_fusion.9
  187.7 1.1 broadcast_multiply_fusion.22
  188.8 1.5 collective-permute-start.8
  190.5 3.3 collective-permute-start.9
  195.4 3.9 collective-permute-start.11
  201.0 6.7 %collective-permute-done.8 = bf16[8,128,192]{1,2,0:T(8,128)(2,1)S(1)} collective-permute-done((bf16[8,128,192]{1,2,0:T(8,128)(2,1)S(1)}, bf16[8,128,192]{1,2,0:T(8,128)(2,1)S(1)}, u32[]{:S(2)}, u32[]{:S(2)}) %collective-permute-start.8) | collective-permute-done | bytes 393248 | tf_op jit(solution)/shard_map/ppermute | solution.py:15
  207.6 4.3 collective-permute-start.13
  212.6 1.1 collective-permute-done.10
  213.8 1.4 collective-permute-start.15
  215.2 5.0 collective-permute-done.11
  220.2 17.0 %collective-permute-done.12 = bf16[8,128,192]{1,2,0:T(8,128)(2,1)S(1)} collective-permute-done((bf16[8,128,192]{1,2,0:T(8,128)(2,1)S(1)}, bf16[8,128,192]{1,2,0:T(8,128)(2,1)S(1)}, u32[]{:S(2)}, u32[]{:S(2)}) %collective-permute-start.12) | collective-permute-done | bytes 393248 | tf_op jit(solution)/shard_map/ppermute | solution.py:15
  237.4 34.4 %collective-permute-done.14 = bf16[8,128,192]{1,2,0:T(8,128)(2,1)S(1)} collective-permute-done((bf16[8,128,192]{1,2,0:T(8,128)(2,1)S(1)}, bf16[8,128,192]{1,2,0:T(8,128)(2,1)S(1)}, u32[]{:S(2)}, u32[]{:S(2)}) %collective-permute-start.14) | collective-permute-done | bytes 393248 | tf_op jit(solution)/shard_map/ppermute | solution.py:15
  271.8 7.4 %collective-permute-done.15 = bf16[8,128,192]{1,2,0:T(8,128)(2,1)S(1)} collective-permute-done((bf16[8,128,192]{1,2,0:T(8,128)(2,1)S(1)}, bf16[8,128,192]{1,2,0:T(8,128)(2,1)S(1)}, u32[]{:S(2)}, u32[]{:S(2)}) %collective-permute-start.15) | collective-permute-done | bytes 393248 | tf_op jit(solution)/shard_map/ppermute | solution.py:15
  279.3 2.3 pad_maximum_fusion.1
  281.7 11.8 %gather_fusion.17 = bf16[192,128,192]{1,2,0:T(8,128)(2,1)} fusion(bf16[80,128,192]{1,2,0:T(8,128)(2,1)} %pad_maximum_fusion.1, s32[1024]{0:T(1024)S(1)} %pad_clamp_fusion), kind=kCustom, calls=%fused_computation.17 | custom fusion | bytes 18875136 | tf_op jit(solution)/shard_map/gather | solution.py:46
  293.5 15.8 %fusion.8 = bf16[192,128,192]{1,2,0:T(8,128)(2,1)} fusion(bf16[192,128,192]{1,2,0:T(8,128)(2,1)} %gather_fusion.17, bf16[192,128,128]{2,1,0:T(8,128)(2,1)} %param.11, bf16[192]{0:T(256)(128)(2,1)S(1)} %compare_convert_fusion.8), kind=kOutput, calls=%fused_computation.36 | convolution fusion | flops 1211105280 | bytes 25166208 | tf_op jit(solution)/shard_map/tij,tjf->tif/dot_general | solution.py:47
  309.3 8.8 %divide_convert_fusion.1 = bf16[16,128,192]{1,0,2:T(8,128)(2,1)S(1)} fusion(bf16[192,128,192]{1,2,0:T(8,128)(2,1)} %fusion.8, f32[16,128]{1,0:T(8,128)S(1)} %copy-done.3, s32[192]{0:T(256)S(1)} %copy-done.27), kind=kOutput, calls=%fused_computation.59 | convolution fusion | flops 151784448 | bytes 10232576 | tf_op jit(solution)/shard_map/bt,tif->bif/dot_general | solution.py:48
  320.2 2.9 fusion.33
  323.1 23.7 %all-gather.13.cloned.1.call-done = bf16[2048,768]{0,1:T(8,128)(2,1)} async-done(((bf16[2048,192]{0,1:T(8,128)(2,1)}), bf16[2048,768]{0,1:T(8,128)(2,1)}) %all-gather.13.cloned.1.call-update) | async-done | bytes 3145744 | tf_op jit(solution)/shard_map/all_gather | solution.py:61
  346.8 3.8 fusion.20
  350.7 1.3 copy_bitcast_fusion.3
  352.0 1.5 gather_fusion.18
  358.8 1.2 broadcast_multiply_fusion.21
  359.9 1.5 collective-permute-start.16
  362.2 3.3 collective-permute-start.17
  367.1 3.9 collective-permute-start.19
  372.7 5.9 %collective-permute-done.16 = bf16[8,128,192]{1,2,0:T(8,128)(2,1)S(1)} collective-permute-done((bf16[8,128,192]{1,2,0:T(8,128)(2,1)S(1)}, bf16[8,128,192]{1,2,0:T(8,128)(2,1)S(1)}, u32[]{:S(2)}, u32[]{:S(2)}) %collective-permute-start.16) | collective-permute-done | bytes 393248 | tf_op jit(solution)/shard_map/ppermute | solution.py:15
  378.7 4.3 collective-permute-start.21
  383.7 1.8 collective-permute-done.18
  385.5 1.4 collective-permute-start.23
  387.0 5.0 collective-permute-done.19
  392.0 16.4 %collective-permute-done.20 = bf16[8,128,192]{1,2,0:T(8,128)(2,1)S(1)} collective-permute-done((bf16[8,128,192]{1,2,0:T(8,128)(2,1)S(1)}, bf16[8,128,192]{1,2,0:T(8,128)(2,1)S(1)}, u32[]{:S(2)}, u32[]{:S(2)}) %collective-permute-start.20) | collective-permute-done | bytes 393248 | tf_op jit(solution)/shard_map/ppermute | solution.py:15
  408.9 34.6 %collective-permute-done.22 = bf16[8,128,192]{1,2,0:T(8,128)(2,1)S(1)} collective-permute-done((bf16[8,128,192]{1,2,0:T(8,128)(2,1)S(1)}, bf16[8,128,192]{1,2,0:T(8,128)(2,1)S(1)}, u32[]{:S(2)}, u32[]{:S(2)}) %collective-permute-start.22) | collective-permute-done | bytes 393248 | tf_op jit(solution)/shard_map/ppermute | solution.py:15
  443.6 7.4 %collective-permute-done.23 = bf16[8,128,192]{1,2,0:T(8,128)(2,1)S(1)} collective-permute-done((bf16[8,128,192]{1,2,0:T(8,128)(2,1)S(1)}, bf16[8,128,192]{1,2,0:T(8,128)(2,1)S(1)}, u32[]{:S(2)}, u32[]{:S(2)}) %collective-permute-start.23) | collective-permute-done | bytes 393248 | tf_op jit(solution)/shard_map/ppermute | solution.py:15
  451.1 2.3 pad_maximum_fusion.2
  453.4 11.8 %gather_fusion.26 = bf16[192,128,192]{1,2,0:T(8,128)(2,1)} fusion(bf16[80,128,192]{1,2,0:T(8,128)(2,1)} %pad_maximum_fusion.2, s32[1024]{0:T(1024)S(1)} %pad_clamp_fusion), kind=kCustom, calls=%fused_computation.26 | custom fusion | bytes 18875136 | tf_op jit(solution)/shard_map/gather | solution.py:46
  465.2 15.9 %fusion.6 = bf16[192,128,192]{1,2,0:T(8,128)(2,1)} fusion(bf16[192,128,192]{1,2,0:T(8,128)(2,1)} %gather_fusion.26, bf16[192,128,128]{2,1,0:T(8,128)(2,1)} %param.11, bf16[192]{0:T(256)(128)(2,1)S(1)} %compare_convert_fusion.8), kind=kOutput, calls=%fused_computation.34 | convolution fusion | flops 1211105280 | bytes 25166208 | tf_op jit(solution)/shard_map/tij,tjf->tif/dot_general | solution.py:47
  481.2 8.8 %divide_convert_fusion = bf16[16,128,192]{1,0,2:T(8,128)(2,1)S(1)} fusion(bf16[192,128,192]{1,2,0:T(8,128)(2,1)} %fusion.6, f32[16,128]{1,0:T(8,128)S(1)} %copy-done.3, s32[192]{0:T(256)S(1)} %copy-done.28), kind=kOutput, calls=%fused_computation.58 | convolution fusion | flops 151784448 | bytes 10232576 | tf_op jit(solution)/shard_map/bt,tif->bif/dot_general | solution.py:48
  491.8 2.9 fusion.30
  494.7 24.0 %all-gather.17.cloned.1.call-done = bf16[2048,768]{0,1:T(8,128)(2,1)} async-done(((bf16[2048,192]{0,1:T(8,128)(2,1)}), bf16[2048,768]{0,1:T(8,128)(2,1)}) %all-gather.17.cloned.1.call-update) | async-done | bytes 3145744 | tf_op jit(solution)/shard_map/all_gather | solution.py:61
  518.7 3.8 fusion.22
  (183 shorter events, 44.7 us)
Async XLA Ops:
  6.5 147.7 %all-gather.7.cloned.1.call-start = ((), (), s32[]{:S(2)}) async-start(), calls=%async_computation | async-start | bytes 3932160 | tf_op jit(solution)/shard_map/all_gather | solution.py:56
  7.3 168.5 %all-gather.9.cloned.1.call-start = ((), (), s32[]{:S(2)}) async-start(), calls=%async_computation.1 | async-start | bytes 3932160 | tf_op jit(solution)/shard_map/all_gather | solution.py:61
  11.9 9.6 %copy-start.12 = (bf16[8]{0:T(256)(128)(2,1)}, bf16[8]{0:T(256)(128)(2,1)S(1)}, u32[]{:S(2)}) copy-start(bf16[8]{0:T(256)(128)(2,1)S(1)} %compare_convert_fusion.7) | copy-start | bytes 52
  11.9 12.4 %copy-start.4 = (s32[1024]{0:T(1024)}, s32[1024]{0:T(1024)S(1)}, u32[]{:S(2)}) copy-start(s32[1024]{0:T(1024)S(1)} %get-tuple-element.36) | copy-start | bytes 12292
  11.9 12.4 %copy-start.5 = (s32[1024]{0:T(1024)}, s32[1024]{0:T(1024)S(1)}, u32[]{:S(2)}) copy-start(s32[1024]{0:T(1024)S(1)} %get-tuple-element.37) | copy-start | bytes 12292
  13.4 30.0 %collective-permute-start = (bf16[8,128,192]{1,2,0:T(8,128)(2,1)}, bf16[8,128,192]{1,2,0:T(8,128)(2,1)S(1)}, u32[]{:S(2)}, u32[]{:S(2)}) collective-permute-start(bf16[8,128,192]{1,2,0:T(8,128)(2,1)} %broadcast_multiply_fusion.23), channel_id=1, source_target_pairs={{28,0},{0,4},{4,8},{8,12},{12,16},{16,20},{20,24},{24,28},{29,1},{... | collective-permute-start | bytes 1179656 | tf_op jit(solution)/shard_map/ppermute | solution.py:15
  17.6 3.9 copy-start.14
  18.4 28.9 %collective-permute-start.1 = (bf16[8,128,192]{1,2,0:T(8,128)(2,1)}, bf16[8,128,192]{1,2,0:T(8,128)(2,1)S(1)}, u32[]{:S(2)}, u32[]{:S(2)}) collective-permute-start(bf16[8,128,192]{1,2,0:T(8,128)(2,1)} %broadcast_multiply_fusion.20), channel_id=1, source_target_pairs={{4,0},{8,4},{12,8},{16,12},{20,16},{24,20},{28,24},{0,28},{5,1},{9... | collective-permute-start | bytes 1179656 | tf_op jit(solution)/shard_map/ppermute | solution.py:15
  21.5 11.0 %copy-start.6 = (s32[1024]{0:T(1024)}, s32[1024]{0:T(1024)S(1)}, u32[]{:S(2)}) copy-start(s32[1024]{0:T(1024)S(1)} %get-tuple-element.34) | copy-start | bytes 12292
  21.5 11.0 %copy-start.7 = (s32[1024]{0:T(1024)}, s32[1024]{0:T(1024)S(1)}, u32[]{:S(2)}) copy-start(s32[1024]{0:T(1024)S(1)} %get-tuple-element.35) | copy-start | bytes 12292
  22.8 10.4 %copy-start.16 = (bf16[8]{0:T(256)(128)(2,1)}, bf16[8]{0:T(256)(128)(2,1)S(1)}, u32[]{:S(2)}) copy-start(bf16[8]{0:T(256)(128)(2,1)S(1)} %compare_convert_fusion.5) | copy-start | bytes 52
  23.7 23.9 %collective-permute-start.2 = (bf16[8,128,192]{1,2,0:T(8,128)(2,1)}, bf16[8,128,192]{1,2,0:T(8,128)(2,1)S(1)}, u32[]{:S(2)}, u32[]{:S(2)}) collective-permute-start(bf16[8,128,192]{1,2,0:T(8,128)(2,1)} %broadcast_multiply_fusion.17), channel_id=1, source_target_pairs={{24,0},{28,4},{0,8},{4,12},{8,16},{12,20},{16,24},{20,28},{25,1},{... | collective-permute-start | bytes 1179656 | tf_op jit(solution)/shard_map/ppermute | solution.py:15
  25.0 4.7 copy-start.17
  25.9 24.7 %collective-permute-start.3 = (bf16[8,128,192]{1,2,0:T(8,128)(2,1)}, bf16[8,128,192]{1,2,0:T(8,128)(2,1)S(1)}, u32[]{:S(2)}, u32[]{:S(2)}) collective-permute-start(bf16[8,128,192]{1,2,0:T(8,128)(2,1)} %broadcast_multiply_fusion.14), channel_id=1, source_target_pairs={{8,0},{12,4},{16,8},{20,12},{24,16},{28,20},{0,24},{4,28},{9,1},{1... | collective-permute-start | bytes 1179656 | tf_op jit(solution)/shard_map/ppermute | solution.py:15
  29.7 3.5 copy-start.8
  29.7 3.5 copy-start.9
  31.0 2.2 copy-start.18
  31.9 31.6 %collective-permute-start.4 = (bf16[8,128,192]{1,2,0:T(8,128)(2,1)}, bf16[8,128,192]{1,2,0:T(8,128)(2,1)}, u32[]{:S(2)}, u32[]{:S(2)}) collective-permute-start(bf16[8,128,192]{1,2,0:T(8,128)(2,1)} %broadcast_multiply_fusion.11), channel_id=1, source_target_pairs={{20,0},{24,4},{28,8},{0,12},{4,16},{8,20},{12,24},{16,28},{21,1},{... | collective-permute-start | bytes 1179656 | tf_op jit(solution)/shard_map/ppermute | solution.py:15
  33.2 10.1 %copy-start.19 = (bf16[8]{0:T(256)(128)(2,1)}, bf16[8]{0:T(256)(128)(2,1)S(1)}, u32[]{:S(2)}) copy-start(bf16[8]{0:T(256)(128)(2,1)S(1)} %compare_convert_fusion.2) | copy-start | bytes 52
  33.3 1.3 copy-start.11
  33.3 3.3 copy-start.10
  34.6 2.3 copy-start.20
  35.9 7.4 %copy-start.23 = (bf16[8]{0:T(256)(128)(2,1)}, bf16[8]{0:T(256)(128)(2,1)S(1)}, u32[]{:S(2)}) copy-start(bf16[8]{0:T(256)(128)(2,1)S(1)} %compare_convert_fusion) | copy-start | bytes 52
  36.9 6.4 %copy-start.26 = (s32[192]{0:T(256)S(1)}, s32[192]{0:T(256)}, u32[]{:S(2)}) copy-start(s32[192]{0:T(256)} %param.12) | copy-start | bytes 2308
  36.9 6.5 %copy-start.29 = (s32[192]{0:T(256)S(1)}, s32[192]{0:T(256)}, u32[]{:S(2)}) copy-start(s32[192]{0:T(256)} %param.13) | copy-start | bytes 2308
  43.4 93.8 %copy-start.2 = (f32[16,128]{1,0:T(8,128)}, f32[16,128]{1,0:T(8,128)S(1)}, u32[]{:S(2)}) copy-start(f32[16,128]{1,0:T(8,128)S(1)} %convolution_add_fusion.3) | copy-start | bytes 24580
  43.5 21.6 %collective-permute-start.5 = (bf16[8,128,192]{1,2,0:T(8,128)(2,1)S(1)}, bf16[8,128,192]{1,2,0:T(8,128)(2,1)S(1)}, u32[]{:S(2)}, u32[]{:S(2)}) collective-permute-start(bf16[8,128,192]{1,2,0:T(8,128)(2,1)S(1)} %broadcast_multiply_fusion.8), channel_id=1, source_target_pairs={{12,0},{16,4},{20,8},{24,12},{28,16},{0,20},{4,24},{8,28},{13,1},{... | collective-permute-start | bytes 1179656 | tf_op jit(solution)/shard_map/ppermute | solution.py:15
  47.4 52.7 %collective-permute-start.6 = (bf16[8,128,192]{1,2,0:T(8,128)(2,1)S(1)}, bf16[8,128,192]{1,2,0:T(8,128)(2,1)S(1)}, u32[]{:S(2)}, u32[]{:S(2)}) collective-permute-start(bf16[8,128,192]{1,2,0:T(8,128)(2,1)S(1)} %broadcast_multiply_fusion.5), channel_id=1, source_target_pairs={{16,0},{20,4},{24,8},{28,12},{0,16},{4,20},{8,24},{12,28},{17,1},{... | collective-permute-start | bytes 1179656 | tf_op jit(solution)/shard_map/ppermute | solution.py:15
  47.5 59.6 %collective-permute-start.7 = (bf16[8,128,192]{1,2,0:T(8,128)(2,1)S(1)}, bf16[8,128,192]{1,2,0:T(8,128)(2,1)S(1)}, u32[]{:S(2)}, u32[]{:S(2)}) collective-permute-start(bf16[8,128,192]{1,2,0:T(8,128)(2,1)S(1)} %broadcast_multiply_fusion.2), channel_id=1, source_target_pairs={{16,0},{20,4},{24,8},{28,12},{0,16},{4,20},{8,24},{12,28},{17,1},{... | collective-permute-start | bytes 1179656 | tf_op jit(solution)/shard_map/ppermute | solution.py:15
  137.3 12.0 %copy-start = (bf16[3,768,768]{2,1,0:T(8,128)(2,1)S(1)}, bf16[3,768,768]{2,1,0:T(8,128)(2,1)}, u32[]{:S(2)}) copy-start(bf16[3,768,768]{2,1,0:T(8,128)(2,1)} %param.17) | copy-start | bytes 10616836
  147.3 172.8 %all-gather.11.cloned.1.call-start = ((), (), s32[]{:S(2)}) async-start(), calls=%async_computation.2 | async-start | bytes 3932160 | tf_op jit(solution)/shard_map/all_gather | solution.py:56
  149.3 3.3 copy-start.1
  179.5 167.3 %all-gather.13.cloned.1.call-start = ((), (), s32[]{:S(2)}) async-start(), calls=%async_computation.3 | async-start | bytes 3932160 | tf_op jit(solution)/shard_map/all_gather | solution.py:61
  183.1 4.5 copy-start.13
  183.9 6.5 %copy-start.15 = (bf16[8]{0:T(256)(128)(2,1)S(1)}, bf16[8]{0:T(256)(128)(2,1)}, u32[]{:S(2)}) copy-start(bf16[8]{0:T(256)(128)(2,1)} %copy-done.14) | copy-start | bytes 52
  187.7 13.1 %copy-start.21 = (bf16[8]{0:T(256)(128)(2,1)S(1)}, bf16[8]{0:T(256)(128)(2,1)}, u32[]{:S(2)}) copy-start(bf16[8]{0:T(256)(128)(2,1)} %copy-done.20) | copy-start | bytes 52
  187.7 13.2 %copy-start.24 = (bf16[8]{0:T(256)(128)(2,1)S(1)}, bf16[8]{0:T(256)(128)(2,1)}, u32[]{:S(2)}) copy-start(bf16[8]{0:T(256)(128)(2,1)} %copy-done.23) | copy-start | bytes 52
  188.8 18.8 %collective-permute-start.8 = (bf16[8,128,192]{1,2,0:T(8,128)(2,1)S(1)}, bf16[8,128,192]{1,2,0:T(8,128)(2,1)S(1)}, u32[]{:S(2)}, u32[]{:S(2)}) collective-permute-start(bf16[8,128,192]{1,2,0:T(8,128)(2,1)S(1)} %broadcast_multiply_fusion.22), channel_id=1, source_target_pairs={{28,0},{0,4},{4,8},{8,12},{12,16},{16,20},{20,24},{24,28},{29,1},{... | collective-permute-start | bytes 1179656 | tf_op jit(solution)/shard_map/ppermute | solution.py:15
  190.5 21.5 %collective-permute-start.9 = (bf16[8,128,192]{1,2,0:T(8,128)(2,1)S(1)}, bf16[8,128,192]{1,2,0:T(8,128)(2,1)S(1)}, u32[]{:S(2)}, u32[]{:S(2)}) collective-permute-start(bf16[8,128,192]{1,2,0:T(8,128)(2,1)S(1)} %broadcast_multiply_fusion.19), channel_id=1, source_target_pairs={{4,0},{8,4},{12,8},{16,12},{20,16},{24,20},{28,24},{0,28},{5,1},{9... | collective-permute-start | bytes 1179656 | tf_op jit(solution)/shard_map/ppermute | solution.py:15
  194.5 19.2 %collective-permute-start.10 = (bf16[8,128,192]{1,2,0:T(8,128)(2,1)S(1)}, bf16[8,128,192]{1,2,0:T(8,128)(2,1)S(1)}, u32[]{:S(2)}, u32[]{:S(2)}) collective-permute-start(bf16[8,128,192]{1,2,0:T(8,128)(2,1)S(1)} %broadcast_multiply_fusion.16), channel_id=1, source_target_pairs={{24,0},{28,4},{0,8},{4,12},{8,16},{12,20},{16,24},{20,28},{25,1},{... | collective-permute-start | bytes 1179656 | tf_op jit(solution)/shard_map/ppermute | solution.py:15
  195.4 24.8 %collective-permute-start.11 = (bf16[8,128,192]{1,2,0:T(8,128)(2,1)S(1)}, bf16[8,128,192]{1,2,0:T(8,128)(2,1)S(1)}, u32[]{:S(2)}, u32[]{:S(2)}) collective-permute-start(bf16[8,128,192]{1,2,0:T(8,128)(2,1)S(1)} %broadcast_multiply_fusion.13), channel_id=1, source_target_pairs={{8,0},{12,4},{16,8},{20,12},{24,16},{28,20},{0,24},{4,28},{9,1},{1... | collective-permute-start | bytes 1179656 | tf_op jit(solution)/shard_map/ppermute | solution.py:15
  199.9 37.3 %collective-permute-start.12 = (bf16[8,128,192]{1,2,0:T(8,128)(2,1)S(1)}, bf16[8,128,192]{1,2,0:T(8,128)(2,1)S(1)}, u32[]{:S(2)}, u32[]{:S(2)}) collective-permute-start(bf16[8,128,192]{1,2,0:T(8,128)(2,1)S(1)} %broadcast_multiply_fusion.10), channel_id=1, source_target_pairs={{20,0},{24,4},{28,8},{0,12},{4,16},{8,20},{12,24},{16,28},{21,1},{... | collective-permute-start | bytes 1179656 | tf_op jit(solution)/shard_map/ppermute | solution.py:15
  207.6 29.7 %collective-permute-start.13 = (bf16[8,128,192]{1,2,0:T(8,128)(2,1)S(1)}, bf16[8,128,192]{1,2,0:T(8,128)(2,1)S(1)}, u32[]{:S(2)}, u32[]{:S(2)}) collective-permute-start(bf16[8,128,192]{1,2,0:T(8,128)(2,1)S(1)} %broadcast_multiply_fusion.7), channel_id=1, source_target_pairs={{12,0},{16,4},{20,8},{24,12},{28,16},{0,20},{4,24},{8,28},{13,1},{... | collective-permute-start | bytes 1179656 | tf_op jit(solution)/shard_map/ppermute | solution.py:15
  212.0 59.8 %collective-permute-start.14 = (bf16[8,128,192]{1,2,0:T(8,128)(2,1)S(1)}, bf16[8,128,192]{1,2,0:T(8,128)(2,1)S(1)}, u32[]{:S(2)}, u32[]{:S(2)}) collective-permute-start(bf16[8,128,192]{1,2,0:T(8,128)(2,1)S(1)} %broadcast_multiply_fusion.4), channel_id=1, source_target_pairs={{16,0},{20,4},{24,8},{28,12},{0,16},{4,20},{8,24},{12,28},{17,1},{... | collective-permute-start | bytes 1179656 | tf_op jit(solution)/shard_map/ppermute | solution.py:15
  213.8 65.5 %collective-permute-start.15 = (bf16[8,128,192]{1,2,0:T(8,128)(2,1)S(1)}, bf16[8,128,192]{1,2,0:T(8,128)(2,1)S(1)}, u32[]{:S(2)}, u32[]{:S(2)}) collective-permute-start(bf16[8,128,192]{1,2,0:T(8,128)(2,1)S(1)} %broadcast_multiply_fusion.1), channel_id=1, source_target_pairs={{16,0},{20,4},{24,8},{28,12},{0,16},{4,20},{8,24},{12,28},{17,1},{... | collective-permute-start | bytes 1179656 | tf_op jit(solution)/shard_map/ppermute | solution.py:15
  293.5 15.8 %copy-start.3 = (f32[16,128]{1,0:T(8,128)S(1)}, f32[16,128]{1,0:T(8,128)}, u32[]{:S(2)}) copy-start(f32[16,128]{1,0:T(8,128)} %copy-done.2) | copy-start | bytes 24580
  293.5 15.8 %copy-start.27 = (s32[192]{0:T(256)S(1)}, s32[192]{0:T(256)}, u32[]{:S(2)}) copy-start(s32[192]{0:T(256)} %param.12) | copy-start | bytes 2308
  319.2 172.7 %all-gather.15.cloned.1.call-start = ((), (), s32[]{:S(2)}) async-start(), calls=%async_computation.4 | async-start | bytes 3932160 | tf_op jit(solution)/shard_map/all_gather | solution.py:56
  350.6 168.1 %all-gather.17.cloned.1.call-start = ((), (), s32[]{:S(2)}) async-start(), calls=%async_computation.5 | async-start | bytes 3932160 | tf_op jit(solution)/shard_map/all_gather | solution.py:61
  358.7 13.8 %copy-start.22 = (bf16[8]{0:T(256)(128)(2,1)S(1)}, bf16[8]{0:T(256)(128)(2,1)}, u32[]{:S(2)}) copy-start(bf16[8]{0:T(256)(128)(2,1)} %copy-done.20) | copy-start | bytes 52
  358.8 13.9 %copy-start.25 = (bf16[8]{0:T(256)(128)(2,1)S(1)}, bf16[8]{0:T(256)(128)(2,1)}, u32[]{:S(2)}) copy-start(bf16[8]{0:T(256)(128)(2,1)} %copy-done.23) | copy-start | bytes 52
  359.9 18.8 %collective-permute-start.16 = (bf16[8,128,192]{1,2,0:T(8,128)(2,1)S(1)}, bf16[8,128,192]{1,2,0:T(8,128)(2,1)S(1)}, u32[]{:S(2)}, u32[]{:S(2)}) collective-permute-start(bf16[8,128,192]{1,2,0:T(8,128)(2,1)S(1)} %broadcast_multiply_fusion.21), channel_id=1, source_target_pairs={{28,0},{0,4},{4,8},{8,12},{12,16},{16,20},{20,24},{24,28},{29,1},{... | collective-permute-start | bytes 1179656 | tf_op jit(solution)/shard_map/ppermute | solution.py:15
  362.2 20.8 %collective-permute-start.17 = (bf16[8,128,192]{1,2,0:T(8,128)(2,1)S(1)}, bf16[8,128,192]{1,2,0:T(8,128)(2,1)S(1)}, u32[]{:S(2)}, u32[]{:S(2)}) collective-permute-start(bf16[8,128,192]{1,2,0:T(8,128)(2,1)S(1)} %broadcast_multiply_fusion.18), channel_id=1, source_target_pairs={{4,0},{8,4},{12,8},{16,12},{20,16},{24,20},{28,24},{0,28},{5,1},{9... | collective-permute-start | bytes 1179656 | tf_op jit(solution)/shard_map/ppermute | solution.py:15
  366.3 19.2 %collective-permute-start.18 = (bf16[8,128,192]{1,2,0:T(8,128)(2,1)S(1)}, bf16[8,128,192]{1,2,0:T(8,128)(2,1)S(1)}, u32[]{:S(2)}, u32[]{:S(2)}) collective-permute-start(bf16[8,128,192]{1,2,0:T(8,128)(2,1)S(1)} %broadcast_multiply_fusion.15), channel_id=1, source_target_pairs={{24,0},{28,4},{0,8},{4,12},{8,16},{12,20},{16,24},{20,28},{25,1},{... | collective-permute-start | bytes 1179656 | tf_op jit(solution)/shard_map/ppermute | solution.py:15
  367.1 24.8 %collective-permute-start.19 = (bf16[8,128,192]{1,2,0:T(8,128)(2,1)S(1)}, bf16[8,128,192]{1,2,0:T(8,128)(2,1)S(1)}, u32[]{:S(2)}, u32[]{:S(2)}) collective-permute-start(bf16[8,128,192]{1,2,0:T(8,128)(2,1)S(1)} %broadcast_multiply_fusion.12), channel_id=1, source_target_pairs={{8,0},{12,4},{16,8},{20,12},{24,16},{28,20},{0,24},{4,28},{9,1},{1... | collective-permute-start | bytes 1179656 | tf_op jit(solution)/shard_map/ppermute | solution.py:15
  371.7 36.7 %collective-permute-start.20 = (bf16[8,128,192]{1,2,0:T(8,128)(2,1)S(1)}, bf16[8,128,192]{1,2,0:T(8,128)(2,1)S(1)}, u32[]{:S(2)}, u32[]{:S(2)}) collective-permute-start(bf16[8,128,192]{1,2,0:T(8,128)(2,1)S(1)} %broadcast_multiply_fusion.9), channel_id=1, source_target_pairs={{20,0},{24,4},{28,8},{0,12},{4,16},{8,20},{12,24},{16,28},{21,1},{... | collective-permute-start | bytes 1179656 | tf_op jit(solution)/shard_map/ppermute | solution.py:15
  378.7 30.2 %collective-permute-start.21 = (bf16[8,128,192]{1,2,0:T(8,128)(2,1)S(1)}, bf16[8,128,192]{1,2,0:T(8,128)(2,1)S(1)}, u32[]{:S(2)}, u32[]{:S(2)}) collective-permute-start(bf16[8,128,192]{1,2,0:T(8,128)(2,1)S(1)} %broadcast_multiply_fusion.6), channel_id=1, source_target_pairs={{12,0},{16,4},{20,8},{24,12},{28,16},{0,20},{4,24},{8,28},{13,1},{... | collective-permute-start | bytes 1179656 | tf_op jit(solution)/shard_map/ppermute | solution.py:15
  383.0 60.5 %collective-permute-start.22 = (bf16[8,128,192]{1,2,0:T(8,128)(2,1)S(1)}, bf16[8,128,192]{1,2,0:T(8,128)(2,1)S(1)}, u32[]{:S(2)}, u32[]{:S(2)}) collective-permute-start(bf16[8,128,192]{1,2,0:T(8,128)(2,1)S(1)} %broadcast_multiply_fusion.3), channel_id=1, source_target_pairs={{16,0},{20,4},{24,8},{28,12},{0,16},{4,20},{8,24},{12,28},{17,1},{... | collective-permute-start | bytes 1179656 | tf_op jit(solution)/shard_map/ppermute | solution.py:15
  385.5 65.5 %collective-permute-start.23 = (bf16[8,128,192]{1,2,0:T(8,128)(2,1)S(1)}, bf16[8,128,192]{1,2,0:T(8,128)(2,1)S(1)}, u32[]{:S(2)}, u32[]{:S(2)}) collective-permute-start(bf16[8,128,192]{1,2,0:T(8,128)(2,1)S(1)} %broadcast_multiply_fusion), channel_id=1, source_target_pairs={{16,0},{20,4},{24,8},{28,12},{0,16},{4,20},{8,24},{12,28},{17,1},{... | collective-permute-start | bytes 1179656 | tf_op jit(solution)/shard_map/ppermute | solution.py:15
  465.2 15.9 %copy-start.28 = (s32[192]{0:T(256)S(1)}, s32[192]{0:T(256)}, u32[]{:S(2)}) copy-start(s32[192]{0:T(256)} %param.12) | copy-start | bytes 2308
Sparse Core Ops, SparseCore 0:
  8.9 31.2 all-gather.6
  147.4 28.3 all-gather.8
  179.6 28.5 all-gather.10
  319.3 27.4 all-gather.12
  350.7 28.5 all-gather.14
  491.2 27.4 all-gather.16
where the time goes:
time: 536 us; the launch traced here: 530 us
  waiting for transfers between devices  265 us (49%)
  matrix products  94.6 us (18%)
  local copies, waits for them, and re-layouts  73.2 us (14%)
  starting transfers between devices  47.7 us (9%)
  other arithmetic  33.6 us (6%)
  between operations  15.4 us (3%)
    ppermute x24, waiting for transfers between devices, from_behind(): return lax.ppermute(block, axis, route)  199 us
    all_gather x3, waiting for transfers between devices, per_device(): lax.all_gather(agg, 'feat', axis=1, tiled=True)  65.8 us
    dot_general x3, matrix products, per_device(): jnp.einsum('tij,tjf->tif', masked, picked, preferred_element_type=jnp.flo...  47.4 us
    ppermute x24, starting transfers between devices, from_behind(): return lax.ppermute(block, axis, route)  47 us
    gather x3, local copies, waits for them, and re-layouts, per_device(): picked = source_list[tile_src]  35.7 us
    dot_general x3, matrix products, per_device(): jnp.einsum('bt,tif->bif', onehot, contrib, preferred_element_type=jnp.flo...  26.5 us
    gather x24, local copies, waits for them, and re-layouts, per_device(): outgoing.append(blocks_here[send_blocks[0, d]] * filled[:, None, None])  18.4 us
    mul x24, other arithmetic, per_device(): outgoing.append(blocks_here[send_blocks[0, d]] * filled[:, None, None])  14.1 us
  transfers between devices with their start and end apart: 30, of which 20 were waited for; matrix products, arithmetic and copies ran while one was open for 36% of the time, Pallas kernels for 0%

commit v1 on v0

v1 whole, which is shorter than its diff:
```python
import functools

import jax
import jax.numpy as jnp
from jax import lax
from jax.experimental import pallas as pl
from jax.experimental.pallas import tpu as pltpu
from jax.sharding import PartitionSpec as P

BLK = 128
GROUP = 4
SIDE = 8
CHUNKS = 2
VMEM = pl.BlockSpec(memory_space=pltpu.VMEM)
SMEM = pl.BlockSpec(memory_space=pltpu.SMEM)


def params():
    return pltpu.CompilerParams(vmem_limit_bytes=40 * 2**20)


def cost(us):
    return pl.CostEstimate(
        flops=int(us * 1e9), bytes_accessed=int(us * 3e6), transcendentals=0
    )


def offset_of(d):
    return (d // 2 + 1) * (1 if d % 2 == 0 else -1)


def peer_of(offset):
    return 2 * (offset - 1) if offset > 0 else 2 * (-offset - 1) + 1


def from_behind(x, distance):
    n = lax.axis_size("dom")
    return lax.ppermute(x, "dom", [(i, (i + distance) % n) for i in range(n)])


def from_partner(x):
    n = lax.axis_size("dom")
    return lax.ppermute(x, "dom", [(i, i ^ 1) for i in range(n)])


def from_feat(x, bit):
    n = lax.axis_size("feat")
    return lax.ppermute(x, "feat", [(i, i ^ bit) for i in range(n)])


def plan_kernel(count, dst, src, place, starts, order, srcs, cursor, *, pad):
    blocks = starts.shape[0] - 1
    live = count[0]

    def clear(b, _):
        cursor[b] = 0
        return 0

    lax.fori_loop(0, blocks, clear, 0)

    def tally(t, _):
        cursor[dst[t]] = cursor[dst[t]] + 1
        return 0

    lax.fori_loop(0, live, tally, 0)

    def begin(b, at):
        starts[b] = at
        groups = (cursor[b] + GROUP - 1) // GROUP
        cursor[b] = at * GROUP
        return at + groups

    starts[blocks] = lax.fori_loop(0, blocks, begin, 0)

    def fill(p, _):
        order[p] = 0
        srcs[p] = pad
        return 0

    lax.fori_loop(0, order.shape[0], fill, 0)

    def put(t, _):
        p = cursor[dst[t]]
        order[p] = t
        srcs[p] = place[src[t]]
        cursor[dst[t]] = p + 1
        return 0

    lax.fori_loop(0, live, put, 0)


def side_by_side(starts, first, rows, product):
    lows = [starts[first + u] for u in range(SIDE)]
    highs = [starts[first + u + 1] for u in range(SIDE)]
    steps = functools.reduce(jnp.maximum, [h - l for h, l in zip(highs, lows)])

    def step(g, sums):
        out = []
        for u in range(SIDE):
            inside = lows[u] + g < highs[u]
            at = jnp.where(inside, lows[u] + g, 0) * GROUP
            out.append(sums[u] + product(at, inside))
        return tuple(out)

    zeros = tuple(jnp.zeros((rows, BLK), jnp.float32) for _ in range(SIDE))
    return lax.fori_loop(0, steps, step, zeros)


def across(left, tiles, order, at):
    right = jnp.concatenate([tiles[order[at + k]] for k in range(GROUP)], axis=1)
    return lax.dot_general(
        left, right, (((1,), (1,)), ((), ())), preferred_element_type=jnp.float32
    )


def degree_kernel(starts, order, srcs, tiles, inverse, *, pad):
    def product(at, inside):
        ones = [
            jnp.full(
                (8, BLK),
                jnp.where(inside & (srcs[at + k] != pad), 1.0, 0.0),
                jnp.float32,
            )
            for k in range(GROUP)
        ]
        left = jnp.concatenate(ones, axis=1).astype(jnp.bfloat16)
        return across(left, tiles, order, at)

    for first in range(0, inverse.shape[0], SIDE):
        sums = side_by_side(starts, first, 8, product)
        for u in range(SIDE):
            inverse[first + u] = 1.0 / (1.0 + sums[u])


def aggregate_kernel(starts, order, srcs, tiles, inverse, *rest, pad):
    *sources, out, held = rest
    at_block = 0
    for ref in sources:

        def copy(i, _, ref=ref, base=at_block):
            held[base + i] = ref[i]
            return 0

        lax.fori_loop(0, ref.shape[0], copy, 0)
        at_block += ref.shape[0]
    rows = held.shape[1]
    held[pad - 1] = jnp.zeros((rows, BLK), held.dtype)
    held[pad] = jnp.zeros((rows, BLK), held.dtype)

    def product(at, inside):
        left = [held[jnp.where(inside, srcs[at + k], pad)] for k in range(GROUP)]
        return across(jnp.concatenate(left, axis=1), tiles, order, at)

    for first in range(0, out.shape[0], SIDE):
        sums = side_by_side(starts, first, rows, product)
        for u in range(SIDE):
            out[first + u] = (sums[u] * inverse[first + u][:1]).astype(out.dtype)


def pair_of(ref, b):
    return jnp.concatenate([ref[b], ref[b + 1]], axis=1)


def self_kernel(weights, bias, full, out, *, feats):
    blocks = out.shape[0]

    def body(q, _):
        parts = [pair_of(full, f * blocks + 2 * q) for f in range(feats)]
        sums = lax.dot_general(
            weights[...],
            jnp.concatenate(parts, axis=0),
            (((1,), (0,)), ((), ())),
            preferred_element_type=jnp.float32,
        )
        sums = sums + bias[...]
        out[2 * q] = sums[:, :BLK]
        out[2 * q + 1] = sums[:, BLK:]
        return 0

    lax.fori_loop(0, blocks // 2, body, 0)


def update_kernel(weights, own, *rest, whole, gathered, feats, last):
    parts = rest[: len(gathered)]
    outs = rest[len(gathered) :]
    blocks = own.shape[0]

    def body(q, _):
        rows = []
        for ref, full in zip(parts, gathered):
            if full:
                rows += [pair_of(ref, f * blocks + 2 * q) for f in range(feats)]
            else:
                rows.append(pair_of(ref, 2 * q))
        sums = lax.dot_general(
            weights[...],
            jnp.concatenate(rows, axis=0),
            (((1,), (0,)), ((), ())),
            preferred_element_type=jnp.float32,
        )
        for k in range(2):
            pre = sums[:, k * BLK : (k + 1) * BLK] + own[2 * q + k]
            if last:
                outs[0][2 * q + k] = pre.astype(jnp.bfloat16)
                continue
            pre = jnp.maximum(pre, 0.0).astype(jnp.bfloat16)
            outs[0][2 * q + k] = pre
            size = pre.shape[0] // CHUNKS
            for c in range(CHUNKS):
                outs[1 + c][2 * q + k] = pre[c * size : (c + 1) * size]
        return 0

    lax.fori_loop(0, blocks // 2, body, 0)


def per_device(
    feats, tile_vals, tile_dst, tile_src, tile_count, send_blocks, send_count, w_self, w_nbr, bias
):
    n = lax.axis_size("dom")
    feat_size = lax.axis_size("feat")
    me = lax.axis_index("dom")
    feat_here = lax.axis_index("feat")
    odd = me % 2
    node_rows, cols = feats.shape
    blocks = node_rows // BLK
    tiles_here = tile_vals.shape[0]
    peers, slots = send_blocks.shape[1:]
    layers, width = bias.shape
    size = cols // CHUNKS
    round_trip = n == peers

    turned = feats.reshape(blocks, BLK, cols).transpose(0, 2, 1)
    chunks = [turned[:, c * size : (c + 1) * size] for c in range(CHUNKS)]

    mine = jnp.concatenate([send_blocks, send_count[:, :, None]], axis=2)
    table = lax.all_gather(mine, "dom", axis=0, tiled=True)

    def row(who, peer):
        sel = (jnp.arange(n) == who % n)[:, None] & (jnp.arange(peers) == peer)[None, :]
        return jnp.sum(jnp.where(sel[:, :, None], table, 0), axis=(0, 1))

    far = blocks if round_trip else 2 * blocks
    base_near, base_far = blocks, 3 * blocks
    base_x = base_far + far
    zero = base_x + 4 * slots
    pad = zero + 1
    place = [jnp.arange(blocks, dtype=jnp.int32)]
    for d in range(peers):
        o = offset_of(d)
        entry = row(me - o, d)
        if o % 2 == 0:
            at = {2: base_near, -2: base_near + blocks, 4: base_far, -4: base_x - blocks}[o]
            at = at + entry[:slots]
        else:
            even_set, odd_set = {1: (1, 0), -1: (0, 2), 3: (3, 1), -3: (2, 3)}[o]
            at = base_x + jnp.where(odd == 1, odd_set, even_set) * slots
            at = at + jnp.arange(slots, dtype=jnp.int32)
        place.append(jnp.where(jnp.arange(slots) < entry[slots], at, zero))
    place = jnp.concatenate(place).astype(jnp.int32)

    def ids(who, even_offset, odd_offset):
        peer = jnp.where(odd == 1, peer_of(odd_offset), peer_of(even_offset))
        return row(who, peer)[:slots]

    ids_own = lax.dynamic_index_in_dim(send_blocks[0], odd, 0, keepdims=False)
    ids_behind = ids(me - 2, 3, 1)
    ids_ahead = ids(me + 2, -1, -3)
    ids_far = ids(me + jnp.where(odd == 1, -4, 4), -3, 3)

    listed = tiles_here + blocks * (GROUP - 1)
    listed = -(-listed // GROUP) * GROUP
    starts, order, srcs = pl.pallas_call(
        functools.partial(plan_kernel, pad=pad),
        name="plan",
        in_specs=[SMEM] * 4,
        out_specs=[SMEM] * 3,
        out_shape=[
            jax.ShapeDtypeStruct((blocks + 1,), jnp.int32),
            jax.ShapeDtypeStruct((listed,), jnp.int32),
            jax.ShapeDtypeStruct((listed,), jnp.int32),
        ],
        scratch_shapes=[pltpu.SMEM((blocks,), jnp.int32)],
        cost_estimate=cost(5),
    )(tile_count, tile_dst, tile_src, place)

    inverse = pl.pallas_call(
        functools.partial(degree_kernel, pad=pad),
        name="degree",
        in_specs=[SMEM] * 3 + [VMEM],
        out_specs=VMEM,
        out_shape=jax.ShapeDtypeStruct((blocks, 8, BLK), jnp.float32),
        compiler_params=params(),
        cost_estimate=cost(8),
    )(starts, order, srcs, tile_vals)

    own_w = lax.dynamic_slice_in_dim(w_self, feat_here * cols, cols, 2).transpose(0, 2, 1)
    nbr_w = lax.dynamic_slice_in_dim(w_nbr, feat_here * cols, cols, 2)
    nbr_w = nbr_w.reshape(layers, feat_size, CHUNKS, size, cols)
    relative = feat_here ^ jnp.arange(feat_size)
    stacked = [
        (nbr_w if c < CHUNKS - 1 else jnp.take(nbr_w, relative, axis=1))[:, :, c]
        for c in range(CHUNKS)
    ]
    nbr_w = jnp.stack(stacked, axis=1).reshape(layers, width, cols).transpose(0, 2, 1)
    own_bias = lax.dynamic_slice_in_dim(bias, feat_here * cols, cols, 1)[:, :, None]

    def sources_of(part):
        x_own = from_partner(part[ids_own])
        behind = from_behind(part, 2)
        ahead = from_behind(part, -2)
        x_behind = from_partner(behind[ids_behind])
        x_ahead = from_partner(ahead[ids_ahead])
        if round_trip:
            half = blocks // 2
            far_parts = [from_behind(behind[:half], 2), from_behind(ahead[half:], -2)]
            from_far = jnp.concatenate(far_parts, axis=0)
        else:
            far_parts = [from_behind(behind, 2), from_behind(ahead, -2)]
            from_far = jnp.where(odd == 1, far_parts[0], far_parts[1])
        x_far = from_partner(from_far[ids_far])
        return [part, behind, ahead, *far_parts, x_own, x_behind, x_ahead, x_far]

    def aggregate(sources):
        rows = sources[0].shape[1]
        return pl.pallas_call(
            functools.partial(aggregate_kernel, pad=pad),
            name="aggregate",
            in_specs=[SMEM] * 3 + [VMEM] * (2 + len(sources)),
            out_specs=VMEM,
            out_shape=jax.ShapeDtypeStruct((blocks, rows, BLK), jnp.bfloat16),
            scratch_shapes=[pltpu.VMEM((pad + 1, rows, BLK), jnp.bfloat16)],
            compiler_params=params(),
            cost_estimate=cost(8),
        )(starts, order, srcs, tile_vals, inverse, *sources)

    for layer in range(layers):
        last = layer == layers - 1
        full = lax.all_gather(turned, "feat", axis=0, tiled=True)
        own = pl.pallas_call(
            functools.partial(self_kernel, feats=feat_size),
            name="own_product",
            in_specs=[VMEM] * 3,
            out_specs=VMEM,
            out_shape=jax.ShapeDtypeStruct((blocks, cols, BLK), jnp.float32),
            compiler_params=params(),
            cost_estimate=cost(4),
        )(own_w[layer], own_bias[layer], full)
        aggs = [aggregate(sources_of(part)) for part in chunks]
        parts, gathered = [], []
        for agg in aggs[:-1]:
            parts.append(lax.all_gather(agg, "feat", axis=0, tiled=True))
            gathered.append(True)
        agg = aggs[-1]
        across_y = from_feat(agg, 2)
        parts += [agg, from_feat(agg, 1), across_y, from_feat(across_y, 1)]
        gathered += [False] * feat_size
        shapes = [jax.ShapeDtypeStruct((blocks, cols, BLK), jnp.bfloat16)]
        if not last:
            shapes += [jax.ShapeDtypeStruct((blocks, size, BLK), jnp.bfloat16)] * CHUNKS
        outs = pl.pallas_call(
            functools.partial(
                update_kernel, whole=None, gathered=tuple(gathered), feats=feat_size, last=last
            ),
            name="update",
            in_specs=[VMEM] * (2 + len(parts)),
            out_specs=[VMEM] * len(shapes),
            out_shape=shapes,
            compiler_params=params(),
            cost_estimate=cost(4),
        )(nbr_w[layer], own, *parts)
        turned, chunks = outs[0], outs[1:]
    return turned.transpose(0, 2, 1).reshape(node_rows, cols)


def solution(mesh):
    in_specs = (
        P("dom", "feat"),
        P("dom", None, None),
        P("dom"),
        P("dom"),
        P("dom"),
        P("dom", None, None),
        P("dom", None),
        P(),
        P(),
        P(),
    )
    out_specs = P("dom", "feat")
    return jax.shard_map(
        per_device, mesh=mesh, in_specs=in_specs, out_specs=out_specs, check_vma=False
    )
```

time: 536 us -> 413 us (0.77); the launches traced: 530 us -> 413 us
  waiting for transfers between devices: 265 us -> 82.2 us
  matrix products: 94.6 us -> 0 us
  Pallas kernels: 0 us -> 62.5 us
  blocking collectives: 0 us -> 51.9 us
  local copies, waits for them, and re-layouts: 73.2 us -> 115 us
  starting transfers between devices: 47.7 us -> 74 us
  other arithmetic: 33.6 us -> 11.9 us
    ppermute x24 -> x57, waiting for transfers between devices: 199 us -> 82.1 us  [the longest x24 34.5 us: from_behind(): return lax.ppermute(x, 'dom', [(i, (i + distance) % n) for i in range(n)])]
    dot_general x13 -> x0, matrix products: 94.6 us -> none  [the longest x3 47.4 us: per_device(): jnp.einsum('tij,tjf->tif', masked, picked, preferred_element_type=jnp.flo...]
    all_gather x6, waiting for transfers between devices: 65.8 us -> 0.07 us  [the longest x3 0.06 us: per_device(): full = lax.all_gather(turned, 'feat', axis=0, tiled=True)]
    pallas_call x0 -> x14, Pallas kernels: none -> 62.5 us  [the longest x6 37.7 us: aggregate(): pl.pallas_call(functools.partial(aggregate_kernel, pad=pad), name='aggreg...]
    all_gather x0 -> x1, blocking collectives: none -> 51.9 us  [per_device(): table = lax.all_gather(mine, 'dom', axis=0, tiled=True)]
    unnamed x84 -> x109, local copies, waits for them, and re-layouts: 6.79 us -> 53.7 us
    ppermute x24 -> x57, starting transfers between devices: 47 us -> 73.7 us  [the longest x24 44.5 us: from_behind(): return lax.ppermute(x, 'dom', [(i, (i + distance) % n) for i in range(n)])]
    gather x27 -> x25, local copies, waits for them, and re-layouts: 54 us -> 34.1 us  [the longest x6 10.1 us: sources_of(): x_far = from_partner(from_far[ids_far])]
  transfers between devices with their start and end apart: 30 -> 63, of which waited for: 20 -> 23; matrix products, arithmetic and copies ran while one was open for 36% -> 18% of each run, Pallas kernels for 0% -> 13%
where the time goes in v1:
time: 413 us
  local copies, waits for them, and re-layouts  115 us (28%)
  waiting for transfers between devices  82.2 us (20%)
  starting transfers between devices  74 us (18%)
  Pallas kernels  62.5 us (15%)
  blocking collectives  51.9 us (13%)
  between operations  15.1 us (4%)
  other arithmetic  11.9 us (3%)
    unnamed x109, local copies, waits for them, and re-layouts  53.7 us
    all_gather x1, blocking collectives, per_device(): table = lax.all_gather(mine, 'dom', axis=0, tiled=True)  51.9 us
    ppermute x24, starting transfers between devices, from_behind(): return lax.ppermute(x, 'dom', [(i, (i + distance) % n) for i in range(n)])  44.5 us
    pallas_call x6, Pallas kernels, aggregate(): pl.pallas_call(functools.partial(aggregate_kernel, pad=pad), name='aggreg...  37.7 us
    ppermute x24, waiting for transfers between devices, from_behind(): return lax.ppermute(x, 'dom', [(i, (i + distance) % n) for i in range(n)])  34.5 us
    ppermute x24, waiting for transfers between devices, from_partner(): return lax.ppermute(x, 'dom', [(i, i ^ 1) for i in range(n)])  28.2 us
    ppermute x24, starting transfers between devices, from_partner(): return lax.ppermute(x, 'dom', [(i, i ^ 1) for i in range(n)])  24.4 us
    ppermute x9, waiting for transfers between devices, from_feat(): return lax.ppermute(x, 'feat', [(i, i ^ bit) for i in range(n)])  19.3 us
  transfers between devices with their start and end apart: 63, of which 23 were waited for; matrix products, arithmetic and copies ran while one was open for 18% of the time, Pallas kernels for 13%

profile of v1, /device:TPU:0, one launch (start us, length us, event | category | flops | bytes accessed | tf_op | source)
XLA Modules:
  0.0 412.6 jit_solution(12671562562975798995)
XLA Ops:
  9.9 3.1 collective-permute-start
  13.0 2.1 collective-permute-start.1
  15.1 3.8 collective-permute-start.9
  22.0 51.9 %all_gather.22 = s32[8,8,9]{2,1,0:T(8,128)S(1)} all-gather(s32[1,8,9]{2,1,0:T(8,128)S(1)} %pad_add_fusion), channel_id=1, replica_groups=mesh['dom'=8,'feat'=4] {'dom'}, dimensions={0}, use_global_device_ids=true | all-gather | bytes 2592 | tf_op jit(solution)/shard_map/all_gather | solution.py:236
  86.1 4.7 %constant_dynamic-slice_fusion.1 = (bf16[3,768,192]{2,1,0:T(8,128)(2,1)}, bf16[3,768,192]{2,1,0:T(8,128)(2,1)}) fusion(bf16[3,768,768]{2,1,0:T(8,128)(2,1)} %param.17, s32[]{:T(128)S(6)} %select_n.199, bf16[3,768,768]{2,1,0:T(8,128)(2,1)} %param.18), kind=kLoop, calls=%fused_computation.90 | loop fusion | bytes 3538948 | tf_op jit(solution)/shard_map/dynamic_slice | solution.py:296
  90.8 6.9 %plan.1 = (s32[17]{0:T(128)}, s32[240]{0:T(256)}, s32[240]{0:T(256)}) custom-call(s32[1]{0:T(128)S(6)} %copy.44.count, s32[192]{0:T(256)} %dst.1, s32[192]{0:T(256)} %src.1, s32[80]{0:T(128)} %concatenate.25.place), custom_call_target="tpu_custom_call" | custom-call | flops 5000000000 | bytes 15000000 | tf_op jit(solution)/shard_map/plan/pallas_call | solution.py:272
  97.7 2.8 copy-done.4
  102.4 4.1 degree.1.inverse
  107.8 2.9 gather_fusion
  110.9 3.9 collective-permute-start.3
  121.2 2.3 gather_fusion.4
  123.9 2.5 select_bitcast_fusion
  130.2 3.8 collective-permute-start.11
  134.0 2.8 copy-done.5
  137.7 6.8 %aggregate.6 = bf16[16,96,128]{2,1,0:T(8,128)(2,1)} custom-call(s32[17]{0:T(128)S(1)} %copy-done.43, s32[240]{0:T(256)S(1)} %copy-done.39, s32[240]{0:T(256)S(1)} %copy-done.41, bf16[192,128,128]{2,1,0:T(8,128)(2,1)S(1)} %copy-done.5, f32[16,8,128]{2,1,0:T(8,128)S(1)} %copy-done.32, bf16[16,96,128]{2,1,0:T(8,128)(2,1)S(1)} %get-tuple-element.41.rest_0_, ...), custom_call_target="tpu_custom_call" | custom-call | flops 8000000000 | bytes 24000000 | tf_op jit(solution)/shard_map/aggregate/pallas_call | solution.py:325
  147.9 2.0 collective-permute-start.14
  153.7 3.4 copy.27
  157.1 3.3 reshape.448
  160.4 2.4 copy.38
  162.8 2.8 copy-done.6
  165.6 5.7 %aggregate.7.rest_1_ = bf16[16,96,128]{2,1,0:T(8,128)(2,1)S(1)} custom-call(s32[17]{0:T(128)S(1)} %copy-done.43, s32[240]{0:T(256)S(1)} %copy-done.39, s32[240]{0:T(256)S(1)} %copy-done.41, bf16[192,128,128]{2,1,0:T(8,128)(2,1)S(1)} %copy-done.6, f32[16,8,128]{2,1,0:T(8,128)S(1)} %copy-done.33, bf16[16,96,128]{2,1,0:T(8,128)(2,1)S(1)} %get-tuple-element.40.rest_0_, ...), custom_call_target="tpu_custom_call" | custom-call | flops 8000000000 | bytes 24000000 | tf_op jit(solution)/shard_map/aggregate/pallas_call | solution.py:325
  173.1 6.0 %collective-permute-done.17.rest_3_ = bf16[16,96,128]{2,1,0:T(8,128)(2,1)S(1)} collective-permute-done((bf16[16,96,128]{2,1,0:T(8,128)(2,1)S(1)}, bf16[16,96,128]{2,1,0:T(8,128)(2,1)S(1)}, u32[]{:S(2)}, u32[]{:S(2)}) %collective-permute-start.17) | collective-permute-done | bytes 393248 | tf_op jit(solution)/shard_map/ppermute | solution.py:48
  180.7 1.9 copy-done.11
  182.6 2.0 own_product.3.own
  190.3 2.9 update.3
  193.3 3.8 collective-permute-start.20
  197.1 9.9 %collective-permute-done.19.rest_1_ = bf16[16,96,128]{2,1,0:T(8,128)(2,1)S(1)} collective-permute-done((bf16[16,96,128]{2,1,0:T(8,128)(2,1)S(1)}, bf16[16,96,128]{2,1,0:T(8,128)(2,1)S(1)}, u32[]{:S(2)}, u32[]{:S(2)}) %collective-permute-start.19) | collective-permute-done | bytes 393248 | tf_op jit(solution)/shard_map/ppermute | solution.py:38
  207.2 6.2 %collective-permute-done.20.rest_2_ = bf16[16,96,128]{2,1,0:T(8,128)(2,1)S(1)} collective-permute-done((bf16[16,96,128]{2,1,0:T(8,128)(2,1)S(1)}, bf16[16,96,128]{2,1,0:T(8,128)(2,1)S(1)}, u32[]{:S(2)}, u32[]{:S(2)}) %collective-permute-start.20) | collective-permute-done | bytes 393248 | tf_op jit(solution)/shard_map/ppermute | solution.py:38
  214.0 2.2 collective-permute-start.22
  226.5 3.3 collective-permute-start.28
  229.9 4.2 %collective-permute-done.25.rest_7_ = bf16[8,96,128]{2,1,0:T(8,128)(2,1)} collective-permute-done((bf16[8,96,128]{2,1,0:T(8,128)(2,1)}, bf16[8,96,128]{2,1,0:T(8,128)(2,1)}, u32[]{:S(2)}, u32[]{:S(2)}) %collective-permute-start.25) | collective-permute-done | bytes 196640 | tf_op jit(solution)/shard_map/ppermute | solution.py:43
  234.1 2.5 collective-permute-done.26.rest_8_
  237.6 2.8 copy-done.7
  241.3 7.0 %aggregate.8 = bf16[16,96,128]{2,1,0:T(8,128)(2,1)} custom-call(s32[17]{0:T(128)S(1)} %copy-done.43, s32[240]{0:T(256)S(1)} %copy-done.39, s32[240]{0:T(256)S(1)} %copy-done.41, bf16[192,128,128]{2,1,0:T(8,128)(2,1)S(1)} %copy-done.7, f32[16,8,128]{2,1,0:T(8,128)S(1)} %copy-done.34, bf16[16,96,128]{2,1,0:T(8,128)(2,1)S(1)} %copy-done.3, ...), custom_call_target="tpu_custom_call" | custom-call | flops 8000000000 | bytes 24000000 | tf_op jit(solution)/shard_map/aggregate/pallas_call | solution.py:325
  249.7 3.8 collective-permute-start.30
  255.6 2.0 collective-permute-start.32
  260.3 2.4 gather_fusion.16
  264.2 2.1 collective-permute-done.32.rest_6_
  266.3 3.3 collective-permute-done.33.rest_7_
  271.7 2.8 copy-done.8
  276.2 5.7 %aggregate.9.rest_1_ = bf16[16,96,128]{2,1,0:T(8,128)(2,1)S(1)} custom-call(s32[17]{0:T(128)S(1)} %copy-done.43, s32[240]{0:T(256)S(1)} %copy-done.39, s32[240]{0:T(256)S(1)} %copy-done.41, bf16[192,128,128]{2,1,0:T(8,128)(2,1)S(1)} %copy-done.8, f32[16,8,128]{2,1,0:T(8,128)S(1)} %copy-done.35, bf16[16,96,128]{2,1,0:T(8,128)(2,1)S(1)} %get-tuple-element.19.rest_0_, ...), custom_call_target="tpu_custom_call" | custom-call | flops 8000000000 | bytes 24000000 | tf_op jit(solution)/shard_map/aggregate/pallas_call | solution.py:325
  283.5 6.6 %collective-permute-done.36.rest_3_ = bf16[16,96,128]{2,1,0:T(8,128)(2,1)S(1)} collective-permute-done((bf16[16,96,128]{2,1,0:T(8,128)(2,1)S(1)}, bf16[16,96,128]{2,1,0:T(8,128)(2,1)S(1)}, u32[]{:S(2)}, u32[]{:S(2)}) %collective-permute-start.36) | collective-permute-done | bytes 393248 | tf_op jit(solution)/shard_map/ppermute | solution.py:48
  290.8 1.9 copy-done.13
  292.7 2.0 own_product.4.own
  300.4 2.9 update.4
  303.4 3.8 collective-permute-start.39
  307.2 9.9 %collective-permute-done.38.rest_1_ = bf16[16,96,128]{2,1,0:T(8,128)(2,1)S(1)} collective-permute-done((bf16[16,96,128]{2,1,0:T(8,128)(2,1)S(1)}, bf16[16,96,128]{2,1,0:T(8,128)(2,1)S(1)}, u32[]{:S(2)}, u32[]{:S(2)}) %collective-permute-start.38) | collective-permute-done | bytes 393248 | tf_op jit(solution)/shard_map/ppermute | solution.py:38
  317.2 6.2 %collective-permute-done.39.rest_2_ = bf16[16,96,128]{2,1,0:T(8,128)(2,1)S(1)} collective-permute-done((bf16[16,96,128]{2,1,0:T(8,128)(2,1)S(1)}, bf16[16,96,128]{2,1,0:T(8,128)(2,1)S(1)}, u32[]{:S(2)}, u32[]{:S(2)}) %collective-permute-start.39) | collective-permute-done | bytes 393248 | tf_op jit(solution)/shard_map/ppermute | solution.py:38
  323.4 2.3 collective-permute-start.41
  336.8 3.3 collective-permute-start.47
  340.0 2.6 collective-permute-done.44.rest_7_
  342.7 2.6 collective-permute-done.45.rest_8_
  345.3 2.8 copy-done.9
  348.9 6.9 %aggregate.10 = bf16[16,96,128]{2,1,0:T(8,128)(2,1)} custom-call(s32[17]{0:T(128)S(1)} %copy-done.43, s32[240]{0:T(256)S(1)} %copy-done.39, s32[240]{0:T(256)S(1)} %copy-done.41, bf16[192,128,128]{2,1,0:T(8,128)(2,1)S(1)} %copy-done.9, f32[16,8,128]{2,1,0:T(8,128)S(1)} %copy-done.36, bf16[16,96,128]{2,1,0:T(8,128)(2,1)S(1)} %get-tuple-element.21.rest_0_, ...), custom_call_target="tpu_custom_call" | custom-call | flops 8000000000 | bytes 24000000 | tf_op jit(solution)/shard_map/aggregate/pallas_call | solution.py:325
  356.0 3.9 collective-permute-start.49
  368.7 3.8 collective-permute-done.51.rest_6_
  372.6 3.4 collective-permute-done.52.rest_7_
  375.9 2.1 collective-permute-done.53.rest_8_
  378.0 2.8 copy-done.10
  380.8 5.7 %aggregate.11.rest_1_ = bf16[16,96,128]{2,1,0:T(8,128)(2,1)S(1)} custom-call(s32[17]{0:T(128)S(1)} %copy-done.43, s32[240]{0:T(256)S(1)} %copy-done.39, s32[240]{0:T(256)S(1)} %copy-done.41, bf16[192,128,128]{2,1,0:T(8,128)(2,1)S(1)} %copy-done.10, f32[16,8,128]{2,1,0:T(8,128)S(1)} %copy-done.37, bf16[16,96,128]{2,1,0:T(8,128)(2,1)S(1)} %get-tuple-element.22.rest_0_, ...), custom_call_target="tpu_custom_call" | custom-call | flops 8000000000 | bytes 24000000 | tf_op jit(solution)/shard_map/aggregate/pallas_call | solution.py:325
  388.1 6.7 %collective-permute-done.55.rest_3_ = bf16[16,96,128]{2,1,0:T(8,128)(2,1)S(1)} collective-permute-done((bf16[16,96,128]{2,1,0:T(8,128)(2,1)S(1)}, bf16[16,96,128]{2,1,0:T(8,128)(2,1)S(1)}, u32[]{:S(2)}, u32[]{:S(2)}) %collective-permute-start.55) | collective-permute-done | bytes 393248 | tf_op jit(solution)/shard_map/ppermute | solution.py:48
  394.9 1.9 copy-done.12
  396.8 2.0 own_product.5.own
  402.7 2.0 update.5
  (303 shorter events, 109.1 us)
Async XLA Ops:
  6.5 174.2 %all-gather.7.cloned.1.call-start = ((), (), s32[]{:S(2)}) async-start(), calls=%async_computation | async-start | bytes 3932160 | tf_op jit(solution)/shard_map/all_gather | solution.py:338
  8.8 177.7 %all-gather.9.cloned.1.call-start = ((), (), s32[]{:S(2)}) async-start(), calls=%async_computation.1 | async-start | bytes 1966080 | tf_op jit(solution)/shard_map/all_gather | solution.py:351
  9.9 100.8 %collective-permute-start = (bf16[16,96,128]{2,1,0:T(8,128)(2,1)S(1)}, bf16[16,96,128]{2,1,0:T(8,128)(2,1)S(1)}, u32[]{:S(2)}, u32[]{:S(2)}) collective-permute-start(bf16[16,96,128]{2,1,0:T(8,128)(2,1)S(1)} %get-tuple-element.41.rest_0_), channel_id=1, source_target_pairs={{0,8},{4,12},{8,16},{12,20},{16,24},{20,28},{24,0},{28,4},{1,9},{5... | collective-permute-start | bytes 1179656 | tf_op jit(solution)/shard_map/ppermute | solution.py:38
  13.0 97.8 %collective-permute-start.1 = (bf16[16,96,128]{2,1,0:T(8,128)(2,1)S(1)}, bf16[16,96,128]{2,1,0:T(8,128)(2,1)S(1)}, u32[]{:S(2)}, u32[]{:S(2)}) collective-permute-start(bf16[16,96,128]{2,1,0:T(8,128)(2,1)S(1)} %get-tuple-element.41.rest_0_), channel_id=1, source_target_pairs={{0,24},{4,28},{8,0},{12,4},{16,8},{20,12},{24,16},{28,20},{1,25},{... | collective-permute-start | bytes 1179656 | tf_op jit(solution)/shard_map/ppermute | solution.py:38
  15.1 108.4 %collective-permute-start.8 = (bf16[16,96,128]{2,1,0:T(8,128)(2,1)S(1)}, bf16[16,96,128]{2,1,0:T(8,128)(2,1)S(1)}, u32[]{:S(2)}, u32[]{:S(2)}) collective-permute-start(bf16[16,96,128]{2,1,0:T(8,128)(2,1)S(1)} %get-tuple-element.40.rest_0_), channel_id=1, source_target_pairs={{0,8},{4,12},{8,16},{12,20},{16,24},{20,28},{24,0},{28,4},{1,9},{5... | collective-permute-start | bytes 1179656 | tf_op jit(solution)/shard_map/ppermute | solution.py:38
  15.1 111.9 %collective-permute-start.9 = (bf16[16,96,128]{2,1,0:T(8,128)(2,1)S(1)}, bf16[16,96,128]{2,1,0:T(8,128)(2,1)S(1)}, u32[]{:S(2)}, u32[]{:S(2)}) collective-permute-start(bf16[16,96,128]{2,1,0:T(8,128)(2,1)S(1)} %get-tuple-element.40.rest_0_), channel_id=1, source_target_pairs={{0,24},{4,28},{8,0},{12,4},{16,8},{20,12},{24,16},{28,20},{1,25},{... | collective-permute-start | bytes 1179656 | tf_op jit(solution)/shard_map/ppermute | solution.py:38
  20.2 109.2 %collective-permute-start.4 = (bf16[8,96,128]{2,1,0:T(8,128)(2,1)}, bf16[8,96,128]{2,1,0:T(8,128)(2,1)S(1)}, u32[]{:S(2)}, u32[]{:S(2)}) collective-permute-start(bf16[8,96,128]{2,1,0:T(8,128)(2,1)} %gather_fusion.1), channel_id=1, source_target_pairs={{0,4},{4,0},{8,12},{12,8},{16,20},{20,16},{24,28},{28,24},{1,5},{5... | collective-permute-start | bytes 589832 | tf_op jit(solution)/shard_map/ppermute | solution.py:43
  110.8 7.6 %collective-permute-start.2 = (bf16[8,96,128]{2,1,0:T(8,128)(2,1)S(1)}, bf16[8,96,128]{2,1,0:T(8,128)(2,1)S(1)}, u32[]{:S(2)}, u32[]{:S(2)}) collective-permute-start(bf16[8,96,128]{2,1,0:T(8,128)(2,1)S(1)} %slice.222), channel_id=1, source_target_pairs={{0,8},{4,12},{8,16},{12,20},{16,24},{20,28},{24,0},{28,4},{1,9},{5... | collective-permute-start | bytes 589832 | tf_op jit(solution)/shard_map/ppermute | solution.py:38
  110.9 7.8 %collective-permute-start.3 = (bf16[8,96,128]{2,1,0:T(8,128)(2,1)S(1)}, bf16[8,96,128]{2,1,0:T(8,128)(2,1)S(1)}, u32[]{:S(2)}, u32[]{:S(2)}) collective-permute-start(bf16[8,96,128]{2,1,0:T(8,128)(2,1)S(1)} %slice.223), channel_id=1, source_target_pairs={{0,24},{4,28},{8,0},{12,4},{16,8},{20,12},{24,16},{28,20},{1,25},{... | collective-permute-start | bytes 589832 | tf_op jit(solution)/shard_map/ppermute | solution.py:38
  118.4 11.1 %collective-permute-start.5 = (bf16[8,96,128]{2,1,0:T(8,128)(2,1)}, bf16[8,96,128]{2,1,0:T(8,128)(2,1)S(1)}, u32[]{:S(2)}, u32[]{:S(2)}) collective-permute-start(bf16[8,96,128]{2,1,0:T(8,128)(2,1)} %gather_fusion.2), channel_id=1, source_target_pairs={{0,4},{4,0},{8,12},{12,8},{16,20},{20,16},{24,28},{28,24},{1,5},{5... | collective-permute-start | bytes 589832 | tf_op jit(solution)/shard_map/ppermute | solution.py:43
  118.7 15.3 %collective-permute-start.6 = (bf16[8,96,128]{2,1,0:T(8,128)(2,1)}, bf16[8,96,128]{2,1,0:T(8,128)(2,1)}, u32[]{:S(2)}, u32[]{:S(2)}) collective-permute-start(bf16[8,96,128]{2,1,0:T(8,128)(2,1)} %gather_fusion.3), channel_id=1, source_target_pairs={{0,4},{4,0},{8,12},{12,8},{16,20},{20,16},{24,28},{28,24},{1,5},{5... | collective-permute-start | bytes 589832 | tf_op jit(solution)/shard_map/ppermute | solution.py:43
  123.5 10.5 %collective-permute-start.7 = (bf16[8,96,128]{2,1,0:T(8,128)(2,1)}, bf16[8,96,128]{2,1,0:T(8,128)(2,1)S(1)}, u32[]{:S(2)}, u32[]{:S(2)}) collective-permute-start(bf16[8,96,128]{2,1,0:T(8,128)(2,1)} %gather_fusion.4), channel_id=1, source_target_pairs={{0,4},{4,0},{8,12},{12,8},{16,20},{20,16},{24,28},{28,24},{1,5},{5... | collective-permute-start | bytes 589832 | tf_op jit(solution)/shard_map/ppermute | solution.py:43
  127.1 35.7 %collective-permute-start.12 = (bf16[8,96,128]{2,1,0:T(8,128)(2,1)}, bf16[8,96,128]{2,1,0:T(8,128)(2,1)S(1)}, u32[]{:S(2)}, u32[]{:S(2)}) collective-permute-start(bf16[8,96,128]{2,1,0:T(8,128)(2,1)} %gather_fusion.5), channel_id=1, source_target_pairs={{0,4},{4,0},{8,12},{12,8},{16,20},{20,16},{24,28},{28,24},{1,5},{5... | collective-permute-start | bytes 589832 | tf_op jit(solution)/shard_map/ppermute | solution.py:43
  129.5 20.4 %collective-permute-start.10 = (bf16[8,96,128]{2,1,0:T(8,128)(2,1)}, bf16[8,96,128]{2,1,0:T(8,128)(2,1)S(1)}, u32[]{:S(2)}, u32[]{:S(2)}) collective-permute-start(bf16[8,96,128]{2,1,0:T(8,128)(2,1)} %slice.225), channel_id=1, source_target_pairs={{0,8},{4,12},{8,16},{12,20},{16,24},{20,28},{24,0},{28,4},{1,9},{5... | collective-permute-start | bytes 589832 | tf_op jit(solution)/shard_map/ppermute | solution.py:38
  130.2 19.7 %collective-permute-start.11 = (bf16[8,96,128]{2,1,0:T(8,128)(2,1)}, bf16[8,96,128]{2,1,0:T(8,128)(2,1)S(1)}, u32[]{:S(2)}, u32[]{:S(2)}) collective-permute-start(bf16[8,96,128]{2,1,0:T(8,128)(2,1)} %slice.226), channel_id=1, source_target_pairs={{0,24},{4,28},{8,0},{12,4},{16,8},{20,12},{24,16},{28,20},{1,25},{... | collective-permute-start | bytes 589832 | tf_op jit(solution)/shard_map/ppermute | solution.py:38
  144.6 146.2 %all-gather.11.cloned.1.call-start = ((), (), s32[]{:S(2)}) async-start(), calls=%async_computation.2 | async-start | bytes 3932160 | tf_op jit(solution)/shard_map/all_gather | solution.py:338
  146.4 16.4 %collective-permute-start.13 = (bf16[8,96,128]{2,1,0:T(8,128)(2,1)S(1)}, bf16[8,96,128]{2,1,0:T(8,128)(2,1)S(1)}, u32[]{:S(2)}, u32[]{:S(2)}) collective-permute-start(bf16[8,96,128]{2,1,0:T(8,128)(2,1)S(1)} %gather_fusion.6), channel_id=1, source_target_pairs={{0,4},{4,0},{8,12},{12,8},{16,20},{20,16},{24,28},{28,24},{1,5},{5... | collective-permute-start | bytes 589832 | tf_op jit(solution)/shard_map/ppermute | solution.py:43
  147.9 14.9 %collective-permute-start.14 = (bf16[8,96,128]{2,1,0:T(8,128)(2,1)}, bf16[8,96,128]{2,1,0:T(8,128)(2,1)S(1)}, u32[]{:S(2)}, u32[]{:S(2)}) collective-permute-start(bf16[8,96,128]{2,1,0:T(8,128)(2,1)} %gather_fusion.7), channel_id=1, source_target_pairs={{0,4},{4,0},{8,12},{12,8},{16,20},{20,16},{24,28},{28,24},{1,5},{5... | collective-permute-start | bytes 589832 | tf_op jit(solution)/shard_map/ppermute | solution.py:43
  151.3 11.5 %collective-permute-start.15 = (bf16[8,96,128]{2,1,0:T(8,128)(2,1)}, bf16[8,96,128]{2,1,0:T(8,128)(2,1)S(1)}, u32[]{:S(2)}, u32[]{:S(2)}) collective-permute-start(bf16[8,96,128]{2,1,0:T(8,128)(2,1)} %gather_fusion.8), channel_id=1, source_target_pairs={{0,4},{4,0},{8,12},{12,8},{16,20},{20,16},{24,28},{28,24},{1,5},{5... | collective-permute-start | bytes 589832 | tf_op jit(solution)/shard_map/ppermute | solution.py:43
  171.3 7.8 %collective-permute-start.17 = (bf16[16,96,128]{2,1,0:T(8,128)(2,1)S(1)}, bf16[16,96,128]{2,1,0:T(8,128)(2,1)S(1)}, u32[]{:S(2)}, u32[]{:S(2)}) collective-permute-start(bf16[16,96,128]{2,1,0:T(8,128)(2,1)S(1)} %aggregate.7.rest_1_), channel_id=1, source_target_pairs={{0,2},{1,3},{2,0},{3,1},{4,6},{5,7},{6,4},{7,5},{8,10},{9,11},{10,... | collective-permute-start | bytes 1179656 | tf_op jit(solution)/shard_map/ppermute | solution.py:48
  173.0 12.7 %collective-permute-start.16 = (bf16[16,96,128]{2,1,0:T(8,128)(2,1)S(1)}, bf16[16,96,128]{2,1,0:T(8,128)(2,1)S(1)}, u32[]{:S(2)}, u32[]{:S(2)}) collective-permute-start(bf16[16,96,128]{2,1,0:T(8,128)(2,1)S(1)} %aggregate.7.rest_1_), channel_id=1, source_target_pairs={{0,1},{1,0},{2,3},{3,2},{4,5},{5,4},{6,7},{7,6},{8,9},{9,8},{10,11... | collective-permute-start | bytes 1179656 | tf_op jit(solution)/shard_map/ppermute | solution.py:48
  179.1 6.6 %collective-permute-start.18 = (bf16[16,96,128]{2,1,0:T(8,128)(2,1)S(1)}, bf16[16,96,128]{2,1,0:T(8,128)(2,1)S(1)}, u32[]{:S(2)}, u32[]{:S(2)}) collective-permute-start(bf16[16,96,128]{2,1,0:T(8,128)(2,1)S(1)} %collective-permute-done.17.rest_3_), channel_id=1, source_target_pairs={{0,1},{1,0},{2,3},{3,2},{4,5},{5,4},{6,7},{7,6},{8,9},{9,8},{10,11... | collective-permute-start | bytes 1179656 | tf_op jit(solution)/shard_map/ppermute | solution.py:48
  193.2 103.3 %all-gather.13.cloned.1.call-start = ((), (), s32[]{:S(2)}) async-start(), calls=%async_computation.3 | async-start | bytes 1966080 | tf_op jit(solution)/shard_map/all_gather | solution.py:351
  193.3 13.8 %collective-permute-start.19 = (bf16[16,96,128]{2,1,0:T(8,128)(2,1)S(1)}, bf16[16,96,128]{2,1,0:T(8,128)(2,1)S(1)}, u32[]{:S(2)}, u32[]{:S(2)}) collective-permute-start(bf16[16,96,128]{2,1,0:T(8,128)(2,1)S(1)} %get-tuple-element.18.rest_0_), channel_id=1, source_target_pairs={{0,8},{4,12},{8,16},{12,20},{16,24},{20,28},{24,0},{28,4},{1,9},{5... | collective-permute-start | bytes 1179656 | tf_op jit(solution)/shard_map/ppermute | solution.py:38
  193.3 20.0 %collective-permute-start.20 = (bf16[16,96,128]{2,1,0:T(8,128)(2,1)S(1)}, bf16[16,96,128]{2,1,0:T(8,128)(2,1)S(1)}, u32[]{:S(2)}, u32[]{:S(2)}) collective-permute-start(bf16[16,96,128]{2,1,0:T(8,128)(2,1)S(1)} %get-tuple-element.18.rest_0_), channel_id=1, source_target_pairs={{0,24},{4,28},{8,0},{12,4},{16,8},{20,12},{24,16},{28,20},{1,25},{... | collective-permute-start | bytes 1179656 | tf_op jit(solution)/shard_map/ppermute | solution.py:38
  207.1 16.2 %collective-permute-start.21 = (bf16[8,96,128]{2,1,0:T(8,128)(2,1)S(1)}, bf16[8,96,128]{2,1,0:T(8,128)(2,1)S(1)}, u32[]{:S(2)}, u32[]{:S(2)}) collective-permute-start(bf16[8,96,128]{2,1,0:T(8,128)(2,1)S(1)} %slice.227), channel_id=1, source_target_pairs={{0,8},{4,12},{8,16},{12,20},{16,24},{20,28},{24,0},{28,4},{1,9},{5... | collective-permute-start | bytes 589832 | tf_op jit(solution)/shard_map/ppermute | solution.py:38
  214.0 9.5 %collective-permute-start.22 = (bf16[8,96,128]{2,1,0:T(8,128)(2,1)}, bf16[8,96,128]{2,1,0:T(8,128)(2,1)S(1)}, u32[]{:S(2)}, u32[]{:S(2)}) collective-permute-start(bf16[8,96,128]{2,1,0:T(8,128)(2,1)} %slice.228), channel_id=1, source_target_pairs={{0,24},{4,28},{8,0},{12,4},{16,8},{20,12},{24,16},{28,20},{1,25},{... | collective-permute-start | bytes 589832 | tf_op jit(solution)/shard_map/ppermute | solution.py:38
  217.5 9.0 %collective-permute-start.23 = (bf16[8,96,128]{2,1,0:T(8,128)(2,1)}, bf16[8,96,128]{2,1,0:T(8,128)(2,1)}, u32[]{:S(2)}, u32[]{:S(2)}) collective-permute-start(bf16[8,96,128]{2,1,0:T(8,128)(2,1)} %gather_fusion.9), channel_id=1, source_target_pairs={{0,4},{4,0},{8,12},{12,8},{16,20},{20,16},{24,28},{28,24},{1,5},{5... | collective-permute-start | bytes 589832 | tf_op jit(solution)/shard_map/ppermute | solution.py:43
  219.9 10.0 %collective-permute-start.24 = (bf16[8,96,128]{2,1,0:T(8,128)(2,1)}, bf16[8,96,128]{2,1,0:T(8,128)(2,1)}, u32[]{:S(2)}, u32[]{:S(2)}) collective-permute-start(bf16[8,96,128]{2,1,0:T(8,128)(2,1)} %gather_fusion.10), channel_id=1, source_target_pairs={{0,4},{4,0},{8,12},{12,8},{16,20},{20,16},{24,28},{28,24},{1,5},{5... | collective-permute-start | bytes 589832 | tf_op jit(solution)/shard_map/ppermute | solution.py:43
  222.3 11.8 %collective-permute-start.25 = (bf16[8,96,128]{2,1,0:T(8,128)(2,1)}, bf16[8,96,128]{2,1,0:T(8,128)(2,1)}, u32[]{:S(2)}, u32[]{:S(2)}) collective-permute-start(bf16[8,96,128]{2,1,0:T(8,128)(2,1)} %gather_fusion.11), channel_id=1, source_target_pairs={{0,4},{4,0},{8,12},{12,8},{16,20},{20,16},{24,28},{28,24},{1,5},{5... | collective-permute-start | bytes 589832 | tf_op jit(solution)/shard_map/ppermute | solution.py:43
  224.9 11.7 %collective-permute-start.26 = (bf16[8,96,128]{2,1,0:T(8,128)(2,1)}, bf16[8,96,128]{2,1,0:T(8,128)(2,1)S(1)}, u32[]{:S(2)}, u32[]{:S(2)}) collective-permute-start(bf16[8,96,128]{2,1,0:T(8,128)(2,1)} %gather_fusion.12), channel_id=1, source_target_pairs={{0,4},{4,0},{8,12},{12,8},{16,20},{20,16},{24,28},{28,24},{1,5},{5... | collective-permute-start | bytes 589832 | tf_op jit(solution)/shard_map/ppermute | solution.py:43
  226.0 22.4 %collective-permute-start.27 = (bf16[16,96,128]{2,1,0:T(8,128)(2,1)S(1)}, bf16[16,96,128]{2,1,0:T(8,128)(2,1)S(1)}, u32[]{:S(2)}, u32[]{:S(2)}) collective-permute-start(bf16[16,96,128]{2,1,0:T(8,128)(2,1)S(1)} %get-tuple-element.19.rest_0_), channel_id=1, source_target_pairs={{0,8},{4,12},{8,16},{12,20},{16,24},{20,28},{24,0},{28,4},{1,9},{5... | collective-permute-start | bytes 1179656 | tf_op jit(solution)/shard_map/ppermute | solution.py:38
  226.5 22.5 %collective-permute-start.28 = (bf16[16,96,128]{2,1,0:T(8,128)(2,1)S(1)}, bf16[16,96,128]{2,1,0:T(8,128)(2,1)S(1)}, u32[]{:S(2)}, u32[]{:S(2)}) collective-permute-start(bf16[16,96,128]{2,1,0:T(8,128)(2,1)S(1)} %get-tuple-element.19.rest_0_), channel_id=1, source_target_pairs={{0,24},{4,28},{8,0},{12,4},{16,8},{20,12},{24,16},{28,20},{1,25},{... | collective-permute-start | bytes 1179656 | tf_op jit(solution)/shard_map/ppermute | solution.py:38
  248.3 146.6 %all-gather.15.cloned.1.call-start = ((), (), s32[]{:S(2)}) async-start(), calls=%async_computation.4 | async-start | bytes 3932160 | tf_op jit(solution)/shard_map/all_gather | solution.py:338
  249.0 10.0 %collective-permute-start.29 = (bf16[8,96,128]{2,1,0:T(8,128)(2,1)}, bf16[8,96,128]{2,1,0:T(8,128)(2,1)S(1)}, u32[]{:S(2)}, u32[]{:S(2)}) collective-permute-start(bf16[8,96,128]{2,1,0:T(8,128)(2,1)} %slice.229), channel_id=1, source_target_pairs={{0,8},{4,12},{8,16},{12,20},{16,24},{20,28},{24,0},{28,4},{1,9},{5... | collective-permute-start | bytes 589832 | tf_op jit(solution)/shard_map/ppermute | solution.py:38
  249.7 9.8 %collective-permute-start.30 = (bf16[8,96,128]{2,1,0:T(8,128)(2,1)}, bf16[8,96,128]{2,1,0:T(8,128)(2,1)S(1)}, u32[]{:S(2)}, u32[]{:S(2)}) collective-permute-start(bf16[8,96,128]{2,1,0:T(8,128)(2,1)} %slice.230), channel_id=1, source_target_pairs={{0,24},{4,28},{8,0},{12,4},{16,8},{20,12},{24,16},{28,20},{1,25},{... | collective-permute-start | bytes 589832 | tf_op jit(solution)/shard_map/ppermute | solution.py:38
  254.2 10.0 %collective-permute-start.31 = (bf16[8,96,128]{2,1,0:T(8,128)(2,1)S(1)}, bf16[8,96,128]{2,1,0:T(8,128)(2,1)S(1)}, u32[]{:S(2)}, u32[]{:S(2)}) collective-permute-start(bf16[8,96,128]{2,1,0:T(8,128)(2,1)S(1)} %gather_fusion.13), channel_id=1, source_target_pairs={{0,4},{4,0},{8,12},{12,8},{16,20},{20,16},{24,28},{28,24},{1,5},{5... | collective-permute-start | bytes 589832 | tf_op jit(solution)/shard_map/ppermute | solution.py:43
  255.6 10.6 %collective-permute-start.32 = (bf16[8,96,128]{2,1,0:T(8,128)(2,1)}, bf16[8,96,128]{2,1,0:T(8,128)(2,1)S(1)}, u32[]{:S(2)}, u32[]{:S(2)}) collective-permute-start(bf16[8,96,128]{2,1,0:T(8,128)(2,1)} %gather_fusion.14), channel_id=1, source_target_pairs={{0,4},{4,0},{8,12},{12,8},{16,20},{20,16},{24,28},{28,24},{1,5},{5... | collective-permute-start | bytes 589832 | tf_op jit(solution)/shard_map/ppermute | solution.py:43
  259.0 10.6 %collective-permute-start.33 = (bf16[8,96,128]{2,1,0:T(8,128)(2,1)}, bf16[8,96,128]{2,1,0:T(8,128)(2,1)S(1)}, u32[]{:S(2)}, u32[]{:S(2)}) collective-permute-start(bf16[8,96,128]{2,1,0:T(8,128)(2,1)} %gather_fusion.15), channel_id=1, source_target_pairs={{0,4},{4,0},{8,12},{12,8},{16,20},{20,16},{24,28},{28,24},{1,5},{5... | collective-permute-start | bytes 589832 | tf_op jit(solution)/shard_map/ppermute | solution.py:43
  262.7 9.0 %collective-permute-start.34 = (bf16[8,96,128]{2,1,0:T(8,128)(2,1)}, bf16[8,96,128]{2,1,0:T(8,128)(2,1)S(1)}, u32[]{:S(2)}, u32[]{:S(2)}) collective-permute-start(bf16[8,96,128]{2,1,0:T(8,128)(2,1)} %gather_fusion.16), channel_id=1, source_target_pairs={{0,4},{4,0},{8,12},{12,8},{16,20},{20,16},{24,28},{28,24},{1,5},{5... | collective-permute-start | bytes 589832 | tf_op jit(solution)/shard_map/ppermute | solution.py:43
  281.9 8.1 %collective-permute-start.36 = (bf16[16,96,128]{2,1,0:T(8,128)(2,1)S(1)}, bf16[16,96,128]{2,1,0:T(8,128)(2,1)S(1)}, u32[]{:S(2)}, u32[]{:S(2)}) collective-permute-start(bf16[16,96,128]{2,1,0:T(8,128)(2,1)S(1)} %aggregate.9.rest_1_), channel_id=1, source_target_pairs={{0,2},{1,3},{2,0},{3,1},{4,6},{5,7},{6,4},{7,5},{8,10},{9,11},{10,... | collective-permute-start | bytes 1179656 | tf_op jit(solution)/shard_map/ppermute | solution.py:48
  283.5 12.4 %collective-permute-start.35 = (bf16[16,96,128]{2,1,0:T(8,128)(2,1)S(1)}, bf16[16,96,128]{2,1,0:T(8,128)(2,1)S(1)}, u32[]{:S(2)}, u32[]{:S(2)}) collective-permute-start(bf16[16,96,128]{2,1,0:T(8,128)(2,1)S(1)} %aggregate.9.rest_1_), channel_id=1, source_target_pairs={{0,1},{1,0},{2,3},{3,2},{4,5},{5,4},{6,7},{7,6},{8,9},{9,8},{10,11... | collective-permute-start | bytes 1179656 | tf_op jit(solution)/shard_map/ppermute | solution.py:48
  290.0 5.8 %collective-permute-start.37 = (bf16[16,96,128]{2,1,0:T(8,128)(2,1)S(1)}, bf16[16,96,128]{2,1,0:T(8,128)(2,1)S(1)}, u32[]{:S(2)}, u32[]{:S(2)}) collective-permute-start(bf16[16,96,128]{2,1,0:T(8,128)(2,1)S(1)} %collective-permute-done.36.rest_3_), channel_id=1, source_target_pairs={{0,1},{1,0},{2,3},{3,2},{4,5},{5,4},{6,7},{7,6},{8,9},{9,8},{10,11... | collective-permute-start | bytes 1179656 | tf_op jit(solution)/shard_map/ppermute | solution.py:48
  303.3 96.6 %all-gather.17.cloned.1.call-start = ((), (), s32[]{:S(2)}) async-start(), calls=%async_computation.5 | async-start | bytes 1966080 | tf_op jit(solution)/shard_map/all_gather | solution.py:351
  303.3 13.8 %collective-permute-start.38 = (bf16[16,96,128]{2,1,0:T(8,128)(2,1)S(1)}, bf16[16,96,128]{2,1,0:T(8,128)(2,1)S(1)}, u32[]{:S(2)}, u32[]{:S(2)}) collective-permute-start(bf16[16,96,128]{2,1,0:T(8,128)(2,1)S(1)} %get-tuple-element.21.rest_0_), channel_id=1, source_target_pairs={{0,8},{4,12},{8,16},{12,20},{16,24},{20,28},{24,0},{28,4},{1,9},{5... | collective-permute-start | bytes 1179656 | tf_op jit(solution)/shard_map/ppermute | solution.py:38
  303.4 20.0 %collective-permute-start.39 = (bf16[16,96,128]{2,1,0:T(8,128)(2,1)S(1)}, bf16[16,96,128]{2,1,0:T(8,128)(2,1)S(1)}, u32[]{:S(2)}, u32[]{:S(2)}) collective-permute-start(bf16[16,96,128]{2,1,0:T(8,128)(2,1)S(1)} %get-tuple-element.21.rest_0_), channel_id=1, source_target_pairs={{0,24},{4,28},{8,0},{12,4},{16,8},{20,12},{24,16},{28,20},{1,25},{... | collective-permute-start | bytes 1179656 | tf_op jit(solution)/shard_map/ppermute | solution.py:38
  317.2 15.8 %collective-permute-start.40 = (bf16[8,96,128]{2,1,0:T(8,128)(2,1)S(1)}, bf16[8,96,128]{2,1,0:T(8,128)(2,1)S(1)}, u32[]{:S(2)}, u32[]{:S(2)}) collective-permute-start(bf16[8,96,128]{2,1,0:T(8,128)(2,1)S(1)} %slice.231), channel_id=1, source_target_pairs={{0,8},{4,12},{8,16},{12,20},{16,24},{20,28},{24,0},{28,4},{1,9},{5... | collective-permute-start | bytes 589832 | tf_op jit(solution)/shard_map/ppermute | solution.py:38
  323.4 10.2 %collective-permute-start.41 = (bf16[8,96,128]{2,1,0:T(8,128)(2,1)S(1)}, bf16[8,96,128]{2,1,0:T(8,128)(2,1)S(1)}, u32[]{:S(2)}, u32[]{:S(2)}) collective-permute-start(bf16[8,96,128]{2,1,0:T(8,128)(2,1)S(1)} %slice.232), channel_id=1, source_target_pairs={{0,24},{4,28},{8,0},{12,4},{16,8},{20,12},{24,16},{28,20},{1,25},{... | collective-permute-start | bytes 589832 | tf_op jit(solution)/shard_map/ppermute | solution.py:38
  326.3 10.5 %collective-permute-start.42 = (bf16[8,96,128]{2,1,0:T(8,128)(2,1)S(1)}, bf16[8,96,128]{2,1,0:T(8,128)(2,1)S(1)}, u32[]{:S(2)}, u32[]{:S(2)}) collective-permute-start(bf16[8,96,128]{2,1,0:T(8,128)(2,1)S(1)} %gather_fusion.17), channel_id=1, source_target_pairs={{0,4},{4,0},{8,12},{12,8},{16,20},{20,16},{24,28},{28,24},{1,5},{5... | collective-permute-start | bytes 589832 | tf_op jit(solution)/shard_map/ppermute | solution.py:43
  329.6 10.5 %collective-permute-start.43 = (bf16[8,96,128]{2,1,0:T(8,128)(2,1)}, bf16[8,96,128]{2,1,0:T(8,128)(2,1)}, u32[]{:S(2)}, u32[]{:S(2)}) collective-permute-start(bf16[8,96,128]{2,1,0:T(8,128)(2,1)} %gather_fusion.18), channel_id=1, source_target_pairs={{0,4},{4,0},{8,12},{12,8},{16,20},{20,16},{24,28},{28,24},{1,5},{5... | collective-permute-start | bytes 589832 | tf_op jit(solution)/shard_map/ppermute | solution.py:43
  331.2 11.5 %collective-permute-start.44 = (bf16[8,96,128]{2,1,0:T(8,128)(2,1)}, bf16[8,96,128]{2,1,0:T(8,128)(2,1)}, u32[]{:S(2)}, u32[]{:S(2)}) collective-permute-start(bf16[8,96,128]{2,1,0:T(8,128)(2,1)} %gather_fusion.19), channel_id=1, source_target_pairs={{0,4},{4,0},{8,12},{12,8},{16,20},{20,16},{24,28},{28,24},{1,5},{5... | collective-permute-start | bytes 589832 | tf_op jit(solution)/shard_map/ppermute | solution.py:43
  335.0 10.3 %collective-permute-start.45 = (bf16[8,96,128]{2,1,0:T(8,128)(2,1)}, bf16[8,96,128]{2,1,0:T(8,128)(2,1)S(1)}, u32[]{:S(2)}, u32[]{:S(2)}) collective-permute-start(bf16[8,96,128]{2,1,0:T(8,128)(2,1)} %gather_fusion.20), channel_id=1, source_target_pairs={{0,4},{4,0},{8,12},{12,8},{16,20},{20,16},{24,28},{28,24},{1,5},{5... | collective-permute-start | bytes 589832 | tf_op jit(solution)/shard_map/ppermute | solution.py:43
  336.2 19.6 %collective-permute-start.46 = (bf16[16,96,128]{2,1,0:T(8,128)(2,1)S(1)}, bf16[16,96,128]{2,1,0:T(8,128)(2,1)S(1)}, u32[]{:S(2)}, u32[]{:S(2)}) collective-permute-start(bf16[16,96,128]{2,1,0:T(8,128)(2,1)S(1)} %get-tuple-element.22.rest_0_), channel_id=1, source_target_pairs={{0,8},{4,12},{8,16},{12,20},{16,24},{20,28},{24,0},{28,4},{1,9},{5... | collective-permute-start | bytes 1179656 | tf_op jit(solution)/shard_map/ppermute | solution.py:38
  336.8 19.2 %collective-permute-start.47 = (bf16[16,96,128]{2,1,0:T(8,128)(2,1)S(1)}, bf16[16,96,128]{2,1,0:T(8,128)(2,1)S(1)}, u32[]{:S(2)}, u32[]{:S(2)}) collective-permute-start(bf16[16,96,128]{2,1,0:T(8,128)(2,1)S(1)} %get-tuple-element.22.rest_0_), channel_id=1, source_target_pairs={{0,24},{4,28},{8,0},{12,4},{16,8},{20,12},{24,16},{28,20},{1,25},{... | collective-permute-start | bytes 1179656 | tf_op jit(solution)/shard_map/ppermute | solution.py:38
  355.9 9.8 %collective-permute-start.48 = (bf16[8,96,128]{2,1,0:T(8,128)(2,1)S(1)}, bf16[8,96,128]{2,1,0:T(8,128)(2,1)S(1)}, u32[]{:S(2)}, u32[]{:S(2)}) collective-permute-start(bf16[8,96,128]{2,1,0:T(8,128)(2,1)S(1)} %slice.233), channel_id=1, source_target_pairs={{0,8},{4,12},{8,16},{12,20},{16,24},{20,28},{24,0},{28,4},{1,9},{5... | collective-permute-start | bytes 589832 | tf_op jit(solution)/shard_map/ppermute | solution.py:38
  356.0 9.7 %collective-permute-start.49 = (bf16[8,96,128]{2,1,0:T(8,128)(2,1)S(1)}, bf16[8,96,128]{2,1,0:T(8,128)(2,1)S(1)}, u32[]{:S(2)}, u32[]{:S(2)}) collective-permute-start(bf16[8,96,128]{2,1,0:T(8,128)(2,1)S(1)} %slice.234), channel_id=1, source_target_pairs={{0,24},{4,28},{8,0},{12,4},{16,8},{20,12},{24,16},{28,20},{1,25},{... | collective-permute-start | bytes 589832 | tf_op jit(solution)/shard_map/ppermute | solution.py:38
  360.4 8.3 %collective-permute-start.50 = (bf16[8,96,128]{2,1,0:T(8,128)(2,1)S(1)}, bf16[8,96,128]{2,1,0:T(8,128)(2,1)S(1)}, u32[]{:S(2)}, u32[]{:S(2)}) collective-permute-start(bf16[8,96,128]{2,1,0:T(8,128)(2,1)S(1)} %gather_fusion.21), channel_id=1, source_target_pairs={{0,4},{4,0},{8,12},{12,8},{16,20},{20,16},{24,28},{28,24},{1,5},{5... | collective-permute-start | bytes 589832 | tf_op jit(solution)/shard_map/ppermute | solution.py:43
  362.3 10.3 %collective-permute-start.51 = (bf16[8,96,128]{2,1,0:T(8,128)(2,1)}, bf16[8,96,128]{2,1,0:T(8,128)(2,1)S(1)}, u32[]{:S(2)}, u32[]{:S(2)}) collective-permute-start(bf16[8,96,128]{2,1,0:T(8,128)(2,1)} %gather_fusion.22), channel_id=1, source_target_pairs={{0,4},{4,0},{8,12},{12,8},{16,20},{20,16},{24,28},{28,24},{1,5},{5... | collective-permute-start | bytes 589832 | tf_op jit(solution)/shard_map/ppermute | solution.py:43
  365.3 10.6 %collective-permute-start.52 = (bf16[8,96,128]{2,1,0:T(8,128)(2,1)}, bf16[8,96,128]{2,1,0:T(8,128)(2,1)S(1)}, u32[]{:S(2)}, u32[]{:S(2)}) collective-permute-start(bf16[8,96,128]{2,1,0:T(8,128)(2,1)} %gather_fusion.23), channel_id=1, source_target_pairs={{0,4},{4,0},{8,12},{12,8},{16,20},{20,16},{24,28},{28,24},{1,5},{5... | collective-permute-start | bytes 589832 | tf_op jit(solution)/shard_map/ppermute | solution.py:43
  365.8 29.0 %copy-start.50 = (f32[192,1]{0,1:T(1,128)S(1)}, f32[192,1]{0,1:T(1,128)}, u32[]{:S(2)}) copy-start(f32[192,1]{0,1:T(1,128)} %get-tuple-element.44) | copy-start | bytes 2308
  367.1 10.9 %collective-permute-start.53 = (bf16[8,96,128]{2,1,0:T(8,128)(2,1)}, bf16[8,96,128]{2,1,0:T(8,128)(2,1)S(1)}, u32[]{:S(2)}, u32[]{:S(2)}) collective-permute-start(bf16[8,96,128]{2,1,0:T(8,128)(2,1)} %gather_fusion.24), channel_id=1, source_target_pairs={{0,4},{4,0},{8,12},{12,8},{16,20},{20,16},{24,28},{28,24},{1,5},{5... | collective-permute-start | bytes 589832 | tf_op jit(solution)/shard_map/ppermute | solution.py:43
  386.5 8.2 %collective-permute-start.55 = (bf16[16,96,128]{2,1,0:T(8,128)(2,1)S(1)}, bf16[16,96,128]{2,1,0:T(8,128)(2,1)S(1)}, u32[]{:S(2)}, u32[]{:S(2)}) collective-permute-start(bf16[16,96,128]{2,1,0:T(8,128)(2,1)S(1)} %aggregate.11.rest_1_), channel_id=1, source_target_pairs={{0,2},{1,3},{2,0},{3,1},{4,6},{5,7},{6,4},{7,5},{8,10},{9,11},{10,... | collective-permute-start | bytes 1179656 | tf_op jit(solution)/shard_map/ppermute | solution.py:48
  388.1 11.8 %collective-permute-start.54 = (bf16[16,96,128]{2,1,0:T(8,128)(2,1)S(1)}, bf16[16,96,128]{2,1,0:T(8,128)(2,1)S(1)}, u32[]{:S(2)}, u32[]{:S(2)}) collective-permute-start(bf16[16,96,128]{2,1,0:T(8,128)(2,1)S(1)} %aggregate.11.rest_1_), channel_id=1, source_target_pairs={{0,1},{1,0},{2,3},{3,2},{4,5},{5,4},{6,7},{7,6},{8,9},{9,8},{10,11... | collective-permute-start | bytes 1179656 | tf_op jit(solution)/shard_map/ppermute | solution.py:48
  394.7 5.2 %collective-permute-start.56 = (bf16[16,96,128]{2,1,0:T(8,128)(2,1)S(1)}, bf16[16,96,128]{2,1,0:T(8,128)(2,1)S(1)}, u32[]{:S(2)}, u32[]{:S(2)}) collective-permute-start(bf16[16,96,128]{2,1,0:T(8,128)(2,1)S(1)} %collective-permute-done.55.rest_3_), channel_id=1, source_target_pairs={{0,1},{1,0},{2,3},{3,2},{4,5},{5,4},{6,7},{7,6},{8,9},{9,8},{10,11... | collective-permute-start | bytes 1179656 | tf_op jit(solution)/shard_map/ppermute | solution.py:48
  (53 other events, 214.3 us)
Sparse Core Ops, SparseCore 0:
  8.9 31.2 all-gather.6
  144.7 17.7 all-gather.8
  193.3 26.8 all-gather.10
  248.4 18.4 all-gather.12
  303.4 26.9 all-gather.14
  356.0 18.6 all-gather.16

commit v2 on v0

v2 whole, which is shorter than its diff:
```python
import functools

import jax
import jax.numpy as jnp
from jax import lax
from jax.experimental import pallas as pl
from jax.experimental.pallas import tpu as pltpu
from jax.sharding import PartitionSpec as P

BLK = 128
GROUP = 4
SIDE = 8
CHUNKS = 2
VMEM = pl.BlockSpec(memory_space=pltpu.VMEM)
SMEM = pl.BlockSpec(memory_space=pltpu.SMEM)


def params():
    return pltpu.CompilerParams(vmem_limit_bytes=18 * 2**20)


def cost(us):
    return pl.CostEstimate(
        flops=int(us * 1e9), bytes_accessed=int(us * 3e6), transcendentals=0
    )


def offset_of(d):
    return (d // 2 + 1) * (1 if d % 2 == 0 else -1)


def peer_of(offset):
    return 2 * (offset - 1) if offset > 0 else 2 * (-offset - 1) + 1


def peer_near(offset, n, peers=8):
    near = (offset + n // 2) % n - n // 2
    for d in range(peers):
        if offset_of(d) == near:
            return d
    return None


def from_behind(x, distance):
    n = lax.axis_size("dom")
    return lax.ppermute(x, "dom", [(i, (i + distance) % n) for i in range(n)])


def from_partner(x):
    n = lax.axis_size("dom")
    return lax.ppermute(x, "dom", [(i, i ^ 1) for i in range(n)])


def from_feat(x, bit):
    n = lax.axis_size("feat")
    return lax.ppermute(x, "feat", [(i, i ^ bit) for i in range(n)])


class Plan:
    def __init__(self, blocks, slots, tiles):
        self.blocks, self.slots = blocks, slots
        lists = 2 * blocks
        longest = tiles + lists * (GROUP - 1)
        self.longest = -(-longest // GROUP) * GROUP
        self.order_at = lists + 1
        self.srcs_at = self.order_at + self.longest
        self.size = self.srcs_at + self.longest

    def views(self, ref):
        return ref, Shifted(ref, self.order_at), Shifted(ref, self.srcs_at)


def picks_kernel(spot, mine, out):
    me = spot[0]
    odd = me % 2 == 1
    layers, _, width = mine.shape
    slots = width - 1
    for k in range(layers):
        peer_even = peer_near(1 + 2 * k, 2 * layers)
        peer_odd = peer_near(-1 + 2 * k, 2 * layers)
        for s in range(slots):
            even_one = 0 if peer_even is None else mine[k, peer_even, s]
            odd_one = 0 if peer_odd is None else mine[k, peer_odd, s]
            out[k, s] = jnp.where(odd, odd_one, even_one)
    low_end = me < 2
    for s in range(slots):
        up_from = jnp.where(odd, mine[0, peer_of(-3), s], mine[0, peer_of(-1), s])
        down_from = jnp.where(odd, mine[0, peer_of(1), s], mine[0, peer_of(3), s])
        out[layers, s] = jnp.where(low_end, up_from, down_from)
        out[layers + 1, s] = jnp.where(
            low_end, mine[0, peer_of(-2), s], mine[0, peer_of(2), s]
        )
        out[layers + 2, s] = me


class Shifted:
    def __init__(self, ref, at):
        self.ref, self.at = ref, at

    def __getitem__(self, i):
        return self.ref[self.at + i]

    def __setitem__(self, i, value):
        self.ref[self.at + i] = value


def plan_kernel(spot, count, dst, src, mine, theirs, out, place, cursor, *, bases, pad, late, plan):
    starts, order, srcs = plan.views(out)
    lists = 2 * plan.blocks
    blocks = plan.blocks
    me = spot[0]
    odd = me % 2 == 1
    layer_here = me // 2
    layers = mine.shape[0]
    peers, width = mine.shape[1:]
    slots = width - 1
    live = count[0]

    def own(b, _):
        place[b] = b
        return 0

    lax.fori_loop(0, blocks, own, 0)
    for d in range(peers):
        o = offset_of(d)
        if o % 2 == 0:
            k = (o // 2) % layers
            base, listed = bases(layer_here, k, False)

            def enter(s, _, d=d, k=k, base=base, listed=listed):
                at = base + jnp.where(listed, s, mine[k, d, s])
                place[blocks + d * slots + s] = jnp.where(s < mine[k, d, slots], at, pad - 1)
                return 0
        else:
            k = jnp.where(odd, ((o - 1) // 2) % layers, ((o + 1) // 2) % layers)
            base_even = bases(layer_here, ((o + 1) // 2) % layers, True)[0]
            base_odd = bases(layer_here, ((o - 1) // 2) % layers, True)[0]
            base = jnp.where(odd, base_odd, base_even)

            def enter(s, _, d=d, k=k, base=base):
                live_slot = s < theirs[k, d, slots]
                place[blocks + d * slots + s] = jnp.where(live_slot, base + s, pad - 1)
                return 0

        lax.fori_loop(0, slots, enter, 0)
    def clear(b, _):
        cursor[b] = 0
        return 0

    lax.fori_loop(0, lists, clear, 0)

    def list_of(t):
        at = place[src[t]]
        return dst[t] + jnp.where((at >= late) & (at < pad - 1), blocks, 0), at

    def tally(t, _):
        b, _at = list_of(t)
        cursor[b] = cursor[b] + 1
        return 0

    lax.fori_loop(0, live, tally, 0)

    def begin(b, at):
        starts[b] = at
        groups = (cursor[b] + GROUP - 1) // GROUP
        cursor[b] = at * GROUP
        return at + groups

    starts[lists] = lax.fori_loop(0, lists, begin, 0)

    def put(t, _):
        b, at = list_of(t)
        p = cursor[b]
        order[p] = t
        srcs[p] = at
        cursor[b] = p + 1
        return 0

    for p in range(GROUP):
        order[p] = 0
        srcs[p] = pad
    lax.fori_loop(0, live, put, 0)

    def fill_up(b, _):
        def fill(p, _):
            order[p] = 0
            srcs[p] = pad
            return 0

        lax.fori_loop(cursor[b], starts[b + 1] * GROUP, fill, 0)
        return 0

    lax.fori_loop(0, lists, fill_up, 0)


def side_by_side(starts, first, sums, product):
    lows = [starts[first + u] for u in range(SIDE)]
    highs = [starts[first + u + 1] for u in range(SIDE)]
    steps = functools.reduce(jnp.maximum, [h - l for h, l in zip(highs, lows)])

    def step(g, sums):
        out = []
        for u in range(SIDE):
            inside = lows[u] + g < highs[u]
            at = jnp.where(inside, lows[u] + g, 0) * GROUP
            out.append(sums[u] + product(at, inside))
        return tuple(out)

    return lax.fori_loop(0, steps, step, tuple(sums))


def zeros(rows):
    return [jnp.zeros((rows, BLK), jnp.float32) for _ in range(SIDE)]


def across(left, tiles, order, at):
    right = jnp.concatenate([tiles[order[at + k]] for k in range(GROUP)], axis=1)
    return lax.dot_general(
        left, right, (((1,), (1,)), ((), ())), preferred_element_type=jnp.float32
    )


def degree_kernel(index, tiles, inverse, kept, *, plan, pad):
    starts, order, srcs = plan.views(index)

    def keep(t, _):
        for k in range(4):
            kept[4 * t + k] = tiles[4 * t + k]
        return 0

    lax.fori_loop(0, tiles.shape[0] // 4, keep, 0)

    def product(at, inside):
        ones = [
            jnp.full(
                (8, BLK),
                jnp.where(inside & (srcs[at + k] != pad), 1.0, 0.0),
                jnp.float32,
            )
            for k in range(GROUP)
        ]
        left = jnp.concatenate(ones, axis=1).astype(jnp.bfloat16)
        return across(left, tiles, order, at)

    blocks = inverse.shape[0]
    for first in range(0, blocks, SIDE):
        sums = side_by_side(starts, first, zeros(8), product)
        sums = side_by_side(starts, blocks + first, sums, product)
        for u in range(SIDE):
            inverse[first + u] = 1.0 / (1.0 + sums[u])


def hold(held, refs):
    base = 0
    for ref in refs:

        def copy(i, _, ref=ref, base=base):
            for k in range(4):
                held[base + 4 * i + k] = ref[4 * i + k]
            return 0

        lax.fori_loop(0, ref.shape[0] // 4, copy, 0)
        base += ref.shape[0]
    held[base] = jnp.zeros(held.shape[1:], held.dtype)
    return base


def early_kernel(index, tiles, *rest, plan, pad):
    *sources, out, held = rest
    starts, order, srcs = plan.views(index)
    end = hold(held, sources)

    def product(at, inside):
        left = []
        for k in range(GROUP):
            src = jnp.where(inside, srcs[at + k], pad)
            left.append(held[jnp.minimum(src, end)])
        return across(jnp.concatenate(left, axis=1), tiles, order, at)

    for first in range(0, out.shape[0], SIDE):
        sums = side_by_side(starts, first, zeros(held.shape[1]), product)
        for u in range(SIDE):
            out[first + u] = sums[u]


def late_kernel(index, tiles, inverse, early, *rest, plan, pad, late, chunk):
    *sources, out, held = rest
    starts, order, srcs = plan.views(index)
    end = hold(held, sources)
    size = held.shape[1]
    cut = slice(chunk * size, (chunk + 1) * size)

    def product(at, inside):
        left = []
        for k in range(GROUP):
            src = jnp.where(inside, srcs[at + k], pad) - late
            left.append(held[jnp.clip(src, 0, end)])
        return across(jnp.concatenate(left, axis=1), tiles, order, at)

    blocks = out.shape[0]
    for first in range(0, blocks, SIDE):
        sums = [early[first + u, cut] for u in range(SIDE)]
        sums = side_by_side(starts, blocks + first, sums, product)
        for u in range(SIDE):
            out[first + u] = (sums[u] * inverse[first + u][:1]).astype(out.dtype)


def weights_kernel(spot, w, out, *, feats, chunks, relative):
    cols, width = out.shape
    here = spot[1]
    rows = []
    if relative:
        size = cols // chunks
        for c in range(chunks):
            for k in range(feats):
                at = pl.multiple_of((here ^ k) * cols + c * size, 16)
                rows.append(w[pl.ds(at, size), :])
        rows = jnp.concatenate(rows, axis=0)
    else:
        rows = w[...]
    column = lax.broadcasted_iota(jnp.int32, (cols, width), 1)
    wanted = lax.broadcasted_iota(jnp.int32, (cols, width), 0) + here * cols
    pick = jnp.where(column == wanted, 1.0, 0.0).astype(rows.dtype)
    turned = lax.dot_general(
        pick, rows, (((1,), (1,)), ((), ())), preferred_element_type=jnp.float32
    )
    out[...] = turned.astype(out.dtype)


def pick_kernel(picks, source, out, *, row):
    def copy(s, _):
        out[s] = source[picks[row, s]]
        return 0

    lax.fori_loop(0, out.shape[0], copy, 0)


def near_kernel(picks, own, below, above, x_out, *outs):
    layer_here = picks[picks.shape[0] - 1, 0] // 2
    slots, blocks = x_out.shape[0], own.shape[0]
    mixed, onward = outs[0::2], outs[1::2]
    size = mixed[0].shape[1]
    cuts = [slice(c * size, (c + 1) * size) for c in range(len(mixed))]

    def copy(s, _):
        x_out[s] = jnp.where(layer_here == 0, above[picks[3, s]], below[picks[1, s]])
        return 0

    lax.fori_loop(0, slots, copy, 0)

    @pl.when((layer_here == 0) | (layer_here == 3))
    def _():
        def copy(s, _):
            for c, cut in enumerate(cuts):
                mixed[c][s] = own[picks[4, s], cut]
                mixed[c][slots + s] = own[picks[5, s], cut]
            return 0

        lax.fori_loop(0, slots, copy, 0)

    def relay(through, back):
        def copy(i, _):
            for k in range(2):
                for c, cut in enumerate(cuts):
                    mixed[c][2 * i + k] = through[2 * i + k, cut]
                    onward[c][2 * i + k] = back[2 * i + k, cut]
            return 0

        lax.fori_loop(0, blocks // 2, copy, 0)

    @pl.when(layer_here == 1)
    def _():
        relay(below, above)

    @pl.when(layer_here == 2)
    def _():
        relay(above, below)


def far_kernel(picks, above, mixed, onward, out, *, chunk):
    layer_here = picks[picks.shape[0] - 1, 0] // 2
    slots, size = picks.shape[1], mixed.shape[1]
    cut = slice(chunk * size, (chunk + 1) * size)
    end = (layer_here == 0) | (layer_here == 3)

    @pl.when(end)
    def _():
        def copy(s, _):
            out[s] = onward[picks[2, s]]
            out[slots + s] = mixed[s]
            return 0

        lax.fori_loop(0, slots, copy, 0)

    @pl.when(jnp.logical_not(end))
    def _():
        def copy(s, _):
            out[s] = above[picks[3, s], cut]
            out[slots + s] = mixed[picks[2, s]]
            return 0

        lax.fori_loop(0, slots, copy, 0)


def pair_of(ref, b):
    return jnp.concatenate([ref[b], ref[b + 1]], axis=1)


def self_kernel(weights, bias, full, out, *, feats):
    blocks = out.shape[0]

    def body(q, _):
        parts = [pair_of(full, f * blocks + 2 * q) for f in range(feats)]
        sums = lax.dot_general(
            weights[...],
            jnp.concatenate(parts, axis=0),
            (((1,), (0,)), ((), ())),
            preferred_element_type=jnp.float32,
        )
        sums = sums + bias[...]
        out[2 * q] = sums[:, :BLK]
        out[2 * q + 1] = sums[:, BLK:]
        return 0

    lax.fori_loop(0, blocks // 2, body, 0)


def update_kernel(weights, before, *rest, count, low, kind):
    parts, out = rest[:count], rest[count]
    blocks = out.shape[0]

    def body(q, _):
        rows = jnp.concatenate([pair_of(ref, 2 * q) for ref in parts], axis=0)
        sums = lax.dot_general(
            weights[:, low : low + rows.shape[0]],
            rows,
            (((1,), (0,)), ((), ())),
            preferred_element_type=jnp.float32,
        )
        for k in range(2):
            pre = sums[:, k * BLK : (k + 1) * BLK] + before[2 * q + k]
            if kind == "relu":
                pre = jnp.maximum(pre, 0.0)
            out[2 * q + k] = pre.astype(out.dtype)
        return 0

    lax.fori_loop(0, blocks // 2, body, 0)


def tie(first, *others):
    return lax.optimization_barrier((tuple(first), *others))[0]


def line_base(blocks, slots):
    late = 3 * blocks + 2 * slots
    mixed, onward, x_far = late, late + blocks, late + 2 * blocks

    def base(layer_here, k, partner):
        middle = (layer_here == 1) | (layer_here == 2)
        lacking = layer_here == (0 if k == 1 else 3)
        if not partner:
            if k == 2:
                return jnp.where(middle, mixed, onward), False
            return jnp.where(lacking, mixed + slots, blocks + k // 2 * blocks), lacking
        if k == 0:
            return 3 * blocks, True
        if k == 2:
            return jnp.where(middle, x_far + slots, x_far), True
        here = 3 * blocks + slots
        if k == 3:
            here = jnp.where(layer_here == 0, here, x_far)
        return jnp.where(lacking, x_far + slots, here), True

    return base


def ring_base(blocks, slots, layers):
    def base(layer_here, k, partner):
        del layer_here
        if partner:
            if k in (2, layers - 2):
                return 5 * blocks + 3 * slots, True
            return 3 * blocks + {0: 0, 1: 1, layers - 1: 2}[k] * slots, True
        if k in (2, layers - 2):
            return 3 * blocks + 3 * slots + (0 if k == 2 else blocks), False
        return {1: 1, layers - 1: 2}[k] * blocks, False

    return base


def per_device(
    feats, tile_vals, tile_dst, tile_src, tile_count, send_blocks, send_count, w_self, w_nbr, bias
):
    n = lax.axis_size("dom")
    feat_size = lax.axis_size("feat")
    me = lax.axis_index("dom")
    feat_here = lax.axis_index("feat")
    node_rows, cols = feats.shape
    blocks = node_rows // BLK
    tiles_here = tile_vals.shape[0]
    peers, slots = send_blocks.shape[1:]
    layers, width = bias.shape
    depth = n // 2
    line = depth == 4
    chunks = CHUNKS if line else 1
    size = cols // chunks
    spot = jnp.stack([me, feat_here]).astype(jnp.int32)
    plan = Plan(blocks, slots, tiles_here)

    own_table = jnp.concatenate([send_blocks, send_count[:, :, None]], axis=2)
    near_by = {1: 2, 2: 4, depth - 2: -4, depth - 1: -2}
    far_tables = [
        from_behind(own_table, near_by[k]) if k in near_by else own_table for k in range(1, depth)
    ]
    mine = jnp.concatenate([own_table, *far_tables], axis=0)
    theirs = from_partner(mine)

    hidden = feats.reshape(blocks, BLK, cols).transpose(0, 2, 1)

    if line:
        late, pad = 3 * blocks + 2 * slots, 5 * blocks + 4 * slots + 1
        bases = line_base(blocks, slots)
    else:
        late, pad = 3 * blocks + 3 * slots, 5 * blocks + 4 * slots + 1
        bases = ring_base(blocks, slots, depth)

    picks = pl.pallas_call(
        picks_kernel,
        name="picks",
        in_specs=[SMEM] * 2,
        out_specs=SMEM,
        out_shape=jax.ShapeDtypeStruct((depth + 3, slots), jnp.int32),
        cost_estimate=cost(1),
    )(spot, mine)
    def call(kernel, name, out_shape, us, scalars, *args, held=None, **static):
        return pl.pallas_call(
            functools.partial(kernel, **static),
            name=name,
            in_specs=[SMEM] + [VMEM] * len(args),
            out_specs=jax.tree.map(lambda _: VMEM, out_shape),
            out_shape=out_shape,
            scratch_shapes=[] if held is None else [pltpu.VMEM(held, jnp.bfloat16)],
            compiler_params=params(),
            cost_estimate=cost(us),
        )(scalars, *args)

    made = {}

    made["index"] = pl.pallas_call(
        functools.partial(plan_kernel, bases=bases, pad=pad, late=late, plan=plan),
        name="plan",
        in_specs=[SMEM] * 6,
        out_specs=SMEM,
        out_shape=jax.ShapeDtypeStruct((plan.size,), jnp.int32),
        scratch_shapes=[
            pltpu.SMEM((blocks + peers * slots,), jnp.int32),
            pltpu.SMEM((2 * blocks,), jnp.int32),
        ],
        cost_estimate=cost(5),
    )(spot, tile_count, tile_dst, tile_src, mine, theirs)

    def degrees(*after):
        if "tiles" in made:
            return
        (tiles_in,) = tie((tile_vals,), *after)
        made["inverse"], made["tiles"] = call(
            degree_kernel,
            "degree",
            [
                pltpu.VMEM((blocks, 8, BLK), jnp.float32),
                pltpu.VMEM(tile_vals.shape, tile_vals.dtype),
            ],
            0.01,
            made["index"],
            tiles_in,
            plan=plan,
            pad=pad,
        )

    def turned_weights(w, relative):
        return pl.pallas_call(
            functools.partial(
                weights_kernel, feats=feat_size, chunks=chunks, relative=relative
            ),
            name="turn_weights",
            grid=(layers,),
            in_specs=[SMEM, pl.BlockSpec((None, width, width), lambda l: (l, 0, 0))],
            out_specs=pl.BlockSpec((None, cols, width), lambda l: (l, 0, 0)),
            out_shape=jax.ShapeDtypeStruct((layers, cols, width), w.dtype),
            compiler_params=params(),
            cost_estimate=cost(0.01),
        )(spot, w)

    own_w, nbr_w = turned_weights(w_self, False), turned_weights(w_nbr, True)
    own_bias = lax.dynamic_slice_in_dim(bias, feat_here * cols, cols, 1)[:, :, None]

    def parts_of(number, rows):
        return jax.ShapeDtypeStruct((number, rows, BLK), jnp.bfloat16)

    def pick(source, row):
        return call(pick_kernel, "pick", parts_of(slots, cols), 1, picks, source, row=row)

    def sum_early(sources):
        return call(
            early_kernel,
            "sum_early",
            pltpu.VMEM((blocks, cols, BLK), jnp.float32),
            6,
            made["index"],
            made["tiles"],
            *sources,
            held=(late + 1, cols, BLK),
            plan=plan,
            pad=pad,
        )

    def aggregate(early, sources, chunk):
        return call(
            late_kernel,
            "aggregate",
            parts_of(blocks, size),
            3,
            made["index"],
            made["tiles"],
            made["inverse"],
            early,
            *sources,
            held=(pad - late, size, BLK),
            plan=plan,
            pad=pad,
            late=late,
            chunk=chunk,
        )

    def own_product(layer, full):
        return pl.pallas_call(
            functools.partial(self_kernel, feats=feat_size),
            name="own_product",
            in_specs=[VMEM] * 3,
            out_specs=VMEM,
            out_shape=pltpu.VMEM((blocks, cols, BLK), jnp.float32),
            compiler_params=params(),
            cost_estimate=cost(2),
        )(own_w[layer], own_bias[layer], full)

    def update(weights, before, parts, low, kind):
        shapes = [pltpu.VMEM((blocks, cols, BLK), jnp.float32)]
        if kind != "sum":
            shapes = [parts_of(blocks, cols)]
        return pl.pallas_call(
            functools.partial(update_kernel, count=len(parts), low=low, kind=kind),
            name="update",
            in_specs=[VMEM] * (2 + len(parts)),
            out_specs=[VMEM] * len(shapes),
            out_shape=shapes,
            compiler_params=params(),
            cost_estimate=cost(3),
        )(weights, before, *parts)

    def send(x, pairs):
        return lax.ppermute(x, "dom", pairs)

    def from_line(hidden, state):
        up = [(i, i + 2) for i in range(n - 2)]
        down = [(i + 2, i) for i in range(n - 2)]
        mix = [(0, 6), (1, 7), (6, 0), (7, 1), (2, 4), (3, 5), (4, 2), (5, 3)]
        outward = [(2, 0), (3, 1), (4, 6), (5, 7)]
        below, above = send(hidden, up), send(hidden, down)
        x_own = from_partner(pick(hidden, 0))
        below, above, x_own, _ = lax.optimization_barrier((below, above, x_own, made["index"]))
        shapes = [parts_of(slots, cols)] + [parts_of(blocks, size)] * (2 * chunks)
        x_near, *onwards = call(near_kernel, "near", shapes, 2, picks, hidden, below, above)
        degrees(x_near)
        x_near = from_partner(x_near)
        far = [
            (send(onwards[2 * c], mix), send(onwards[2 * c + 1], outward)) for c in range(chunks)
        ]
        early = sum_early([hidden, below, above, x_own, x_near])
        listed = []
        for c, (mixed, onward) in enumerate(far):
            mixed, onward = far[c] = tie((mixed, onward), early, state, listed)
            shape = parts_of(2 * slots, size)
            listed.append(
                call(far_kernel, "far", shape, 1, picks, above, mixed, onward, chunk=c)
            )
        aggs = []
        for c, (mixed, onward) in enumerate(far):
            x_far = from_partner(listed[c])
            x_far, *_ = tie((x_far,), listed, aggs)
            aggs.append(aggregate(early, [mixed, onward, x_far], c))
        return aggs

    def from_ring(hidden):
        behind, ahead = from_behind(hidden, 2), from_behind(hidden, -2)
        behind_two, ahead_two = from_behind(behind, 2), from_behind(ahead, -2)
        x_own = from_partner(pick(hidden, 0))
        x_near = [from_partner(pick(behind, 1)), from_partner(pick(ahead, depth - 1))]
        degrees()
        odd = me % 2 == 1
        x_two = jnp.where(odd, pick(behind_two, 2), pick(ahead_two, depth - 2))
        early = sum_early([hidden, behind, ahead, x_own, *x_near])
        return [aggregate(early, [behind_two, ahead_two, from_partner(x_two)], 0)]

    for layer in range(layers):
        last = layer == layers - 1
        state = own_product(layer, lax.all_gather(hidden, "feat", axis=0, tiled=True))
        aggs = from_line(hidden, state) if line else from_ring(hidden)
        for c, agg in enumerate(aggs):
            other = from_feat(agg, 2)
            parts = [agg, from_feat(agg, 1), other, from_feat(other, 1)]
            kind = "sum" if c < chunks - 1 else "none" if last else "relu"
            (state,) = update(nbr_w[layer], state, parts, c * feat_size * size, kind)
        hidden = state
    return hidden.transpose(0, 2, 1).reshape(node_rows, cols)


def solution(mesh):
    in_specs = (
        P("dom", "feat"),
        P("dom", None, None),
        P("dom"),
        P("dom"),
        P("dom"),
        P("dom", None, None),
        P("dom", None),
        P(),
        P(),
        P(),
    )
    out_specs = P("dom", "feat")
    return jax.shard_map(
        per_device, mesh=mesh, in_specs=in_specs, out_specs=out_specs, check_vma=False
    )
```

time: 536 us -> 324 us (0.60); the launches traced: 530 us -> 324 us
  waiting for transfers between devices: 265 us -> 101 us
  Pallas kernels: 0 us -> 96 us
  matrix products: 94.6 us -> 0 us
  other arithmetic: 33.6 us -> 0.8 us
  local copies, waits for them, and re-layouts: 73.2 us -> 43.9 us
  starting transfers between devices: 47.7 us -> 68.2 us
    ppermute x24 -> x52, waiting for transfers between devices: 199 us -> 101 us  [the longest x13 36.4 us: from_partner(): return lax.ppermute(x, 'dom', [(i, i ^ 1) for i in range(n)])]
    pallas_call x0 -> x35, Pallas kernels: none -> 96 us  [the longest x22 62.5 us: call(): pl.pallas_call(functools.partial(kernel, **static), name=name, in_specs=[...]
    dot_general x13 -> x0, matrix products: 94.6 us -> none  [the longest x3 47.4 us: per_device(): jnp.einsum('tij,tjf->tif', masked, picked, preferred_element_type=jnp.flo...]
    all_gather x6 -> x3, waiting for transfers between devices: 65.8 us -> 0.01 us  [per_device(): lax.all_gather(hidden, 'feat', axis=0, tiled=True)]
    gather x27 -> x0, local copies, waits for them, and re-layouts: 54 us -> none  [the longest x3 35.7 us: per_device(): picked = source_list[tile_src]]
    unnamed x84 -> x98, local copies, waits for them, and re-layouts: 6.79 us -> 38.5 us
    ppermute x24 -> x52, starting transfers between devices: 47 us -> 68.1 us  [the longest x18 37.7 us: send(): return lax.ppermute(x, 'dom', pairs)]
    mul x24 -> x0, other arithmetic: 14.1 us -> none  [per_device(): outgoing.append(blocks_here[send_blocks[0, d]] * filled[:, None, None])]
  transfers between devices with their start and end apart: 30 -> 55, of which waited for: 20 -> 24; matrix products, arithmetic and copies ran while one was open for 36% -> 1% of each run, Pallas kernels for 0% -> 27%
where the time goes in v2:
time: 324 us
  waiting for transfers between devices  101 us (31%)
  Pallas kernels  96 us (30%)
  starting transfers between devices  68.2 us (21%)
  local copies, waits for them, and re-layouts  43.9 us (14%)
  between operations  14.5 us (4%)
    pallas_call x22, Pallas kernels, call(): pl.pallas_call(functools.partial(kernel, **static), name=name, in_specs=[...  62.5 us
    unnamed x98, local copies, waits for them, and re-layouts  38.5 us
    ppermute x18, starting transfers between devices, send(): return lax.ppermute(x, 'dom', pairs)  37.7 us
    ppermute x13, waiting for transfers between devices, from_partner(): return lax.ppermute(x, 'dom', [(i, i ^ 1) for i in range(n)])  36.4 us
    ppermute x18, waiting for transfers between devices, send(): return lax.ppermute(x, 'dom', pairs)  36.2 us
    ppermute x18, waiting for transfers between devices, from_feat(): return lax.ppermute(x, 'feat', [(i, i ^ bit) for i in range(n)])  28.4 us
    ppermute x13, starting transfers between devices, from_partner(): return lax.ppermute(x, 'dom', [(i, i ^ 1) for i in range(n)])  13.8 us
    pallas_call x6, Pallas kernels, update(): pl.pallas_call(functools.partial(update_kernel, count=len(parts), low=low...  11.9 us
  transfers between devices with their start and end apart: 55, of which 24 were waited for; matrix products, arithmetic and copies ran while one was open for 1% of the time, Pallas kernels for 27%

profile of v2, /device:TPU:0, one launch (start us, length us, event | category | flops | bytes accessed | tf_op | source)
XLA Modules:
  0.0 324.4 jit_solution(11665117303514908961)
XLA Ops:
  9.0 5.1 %collective-permute-start.2 = (s32[1,8,9]{2,1,0:T(8,128)S(1)}, s32[1,8,9]{2,1,0:T(8,128)S(1)}, u32[]{:S(2)}, u32[]{:S(2)}) collective-permute-start(s32[1,8,9]{2,1,0:T(8,128)S(1)} %pad_add_fusion.1), channel_id=1, source_target_pairs={{0,24},{4,28},{8,0},{12,4},{16,8},{20,12},{24,16},{28,20},{1,25},{... | collective-permute-start | bytes 872 | tf_op jit(solution)/shard_map/ppermute | solution.py:46
  16.3 5.1 %collective-permute-start.4 = (bf16[16,192,128]{2,1,0:T(8,128)(2,1)}, bf16[16,192,128]{2,1,0:T(8,128)(2,1)S(1)}, u32[]{:S(2)}, u32[]{:S(2)}) collective-permute-start(bf16[16,192,128]{2,1,0:T(8,128)(2,1)} %bitcast_bitcast_fusion.source.own.rest_0_), channel_id=1, source_target_pairs={{0,8},{4,12},{8,16},{12,20},{16,24},{20,28},{1,9},{5,13},{9,17},{1... | collective-permute-start | bytes 2359304 | tf_op jit(solution)/shard_map/ppermute | solution.py:661
  24.3 1.6 picks.1
  28.6 9.5 %plan.1.index = s32[609]{0:T(1024)} custom-call(s32[2]{0:T(128)} %pad_add_fusion.2.spot, s32[1]{0:T(128)S(6)} %copy.28.count, s32[192]{0:T(256)} %dst.1, s32[192]{0:T(256)} %src.1, s32[4,8,9]{2,1,0:T(8,128)} %copy-done.46, s32[4,8,9]{2,1,0:T(8,128)} %copy-done.48), custom_call_target="tpu_custom_call" | custom-call | flops 5000000000 | bytes 15000000 | tf_op jit(solution)/shard_map/plan/pallas_call | solution.py:549
  44.0 2.2 near.3
  50.5 2.2 turn_weights.3
  55.5 2.6 collective-permute-start.11
  59.4 2.8 copy-done.2
  62.2 5.4 %degree.1 = (f32[16,8,128]{2,1,0:T(8,128)S(1)}, bf16[192,128,128]{2,1,0:T(8,128)(2,1)S(1)}) custom-call(s32[609]{0:T(1024)S(1)} %copy-done.9, bf16[192,128,128]{2,1,0:T(8,128)(2,1)S(1)} %copy-done.2), custom_call_target="tpu_custom_call" | custom-call | flops 10000000 | bytes 30000 | tf_op jit(solution)/shard_map/degree/pallas_call | solution.py:536
  67.7 5.6 %sum_early.3.early = f32[16,192,128]{2,1,0:T(8,128)S(1)} custom-call(s32[609]{0:T(1024)S(1)} %copy-done.9, bf16[192,128,128]{2,1,0:T(8,128)(2,1)S(1)} %get-tuple-element.54.tiles, bf16[16,192,128]{2,1,0:T(8,128)(2,1)S(1)} %copy-done.7, bf16[16,192,128]{2,1,0:T(8,128)(2,1)S(1)} %copy-done.25, bf16[16,192,128]{2,1,0:T(8,128)(2,1)S(1)} %copy-done.22, ...), custom_call_target="tpu_custom_call" | custom-call | flops 6000000000 | bytes 18000000 | tf_op jit(solution)/shard_map/sum_early/pallas_call | solution.py:536
  73.3 2.6 copy-done.11
  77.0 1.9 copy-done.17
  78.9 2.0 own_product.3.before
  82.4 1.6 collective-permute-start.10
  84.0 5.3 %collective-permute-done.12.onward.rest_1_ = bf16[16,96,128]{2,1,0:T(8,128)(2,1)} collective-permute-done((bf16[16,96,128]{2,1,0:T(8,128)(2,1)}, bf16[16,96,128]{2,1,0:T(8,128)(2,1)}, u32[]{:S(2)}, u32[]{:S(2)}) %collective-permute-start.12) | collective-permute-done | bytes 393248 | tf_op jit(solution)/shard_map/ppermute | solution.py:661
  91.5 2.0 collective-permute-done.10.rest_2_
  93.5 3.9 %aggregate.6.rest_0_ = bf16[16,96,128]{2,1,0:T(8,128)(2,1)S(1)} custom-call(s32[609]{0:T(1024)S(1)} %copy-done.9, bf16[192,128,128]{2,1,0:T(8,128)(2,1)S(1)} %copy-done.12, f32[16,8,128]{2,1,0:T(8,128)S(1)} %get-tuple-element.55.inverse, f32[16,192,128]{2,1,0:T(8,128)S(1)} %copy-done.40, bf16[16,96,128]{2,1,0:T(8,128)(2,1)} %collective-permute-done.8.mixed.rest_0_, ...), custom_call_target="tpu_custom_call" | custom-call | flops 3000000000 | bytes 9000000 | tf_op jit(solution)/shard_map/aggregate/pallas_call | solution.py:536
  99.0 2.9 collective-permute-done.16.rest_2_
  101.8 4.0 %aggregate.7.rest_0_ = bf16[16,96,128]{2,1,0:T(8,128)(2,1)S(1)} custom-call(s32[609]{0:T(1024)S(1)} %copy-done.9, bf16[192,128,128]{2,1,0:T(8,128)(2,1)S(1)} %copy-done.12, f32[16,8,128]{2,1,0:T(8,128)S(1)} %get-tuple-element.55.inverse, f32[16,192,128]{2,1,0:T(8,128)S(1)} %copy-done.40, bf16[16,96,128]{2,1,0:T(8,128)(2,1)} %collective-permute-done.11.mixed.rest_0_, ...), custom_call_target="tpu_custom_call" | custom-call | flops 3000000000 | bytes 9000000 | tf_op jit(solution)/shard_map/aggregate/pallas_call | solution.py:536
  108.0 2.3 turn_weights.2
  110.3 6.0 %collective-permute-done.18.rest_2_ = bf16[16,96,128]{2,1,0:T(8,128)(2,1)S(1)} collective-permute-done((bf16[16,96,128]{2,1,0:T(8,128)(2,1)S(1)}, bf16[16,96,128]{2,1,0:T(8,128)(2,1)S(1)}, u32[]{:S(2)}, u32[]{:S(2)}) %collective-permute-start.18) | collective-permute-done | bytes 393248 | tf_op jit(solution)/shard_map/ppermute | solution.py:56
  116.4 1.7 update.6.before
  118.1 2.6 update.7.source.own.rest_0_
  122.0 4.6 %collective-permute-start.20 = (bf16[16,192,128]{2,1,0:T(8,128)(2,1)}, bf16[16,192,128]{2,1,0:T(8,128)(2,1)S(1)}, u32[]{:S(2)}, u32[]{:S(2)}) collective-permute-start(bf16[16,192,128]{2,1,0:T(8,128)(2,1)} %update.7.source.own.rest_0_), channel_id=1, source_target_pairs={{0,8},{4,12},{8,16},{12,20},{16,24},{20,28},{1,9},{5,13},{9,17},{1... | collective-permute-start | bytes 2359304 | tf_op jit(solution)/shard_map/ppermute | solution.py:661
  128.8 10.3 %collective-permute-done.22.rest_3_ = bf16[8,192,128]{2,1,0:T(8,128)(2,1)S(1)} collective-permute-done((bf16[8,192,128]{2,1,0:T(8,128)(2,1)S(1)}, bf16[8,192,128]{2,1,0:T(8,128)(2,1)S(1)}, u32[]{:S(2)}, u32[]{:S(2)}) %collective-permute-start.22) | collective-permute-done | bytes 393248 | tf_op jit(solution)/shard_map/ppermute | solution.py:51
  139.8 2.9 collective-permute-done.21.above.rest_2_
  144.1 2.2 near.4
  150.6 2.9 collective-permute-start.27
  154.8 3.0 collective-permute-done.23.rest_4_
  157.8 2.8 copy-done.13
  161.6 5.9 %sum_early.4.early = f32[16,192,128]{2,1,0:T(8,128)S(1)} custom-call(s32[609]{0:T(1024)S(1)} %copy-done.9, bf16[192,128,128]{2,1,0:T(8,128)(2,1)S(1)} %copy-done.13, bf16[16,192,128]{2,1,0:T(8,128)(2,1)} %update.7.source.own.rest_0_, bf16[16,192,128]{2,1,0:T(8,128)(2,1)S(1)} %collective-permute-done.20.below.rest_1_, ...), custom_call_target="tpu_custom_call" | custom-call | flops 6000000000 | bytes 18000000 | tf_op jit(solution)/shard_map/sum_early/pallas_call | solution.py:536
  168.7 1.9 copy-done.18
  170.5 2.0 own_product.4.before
  172.5 5.4 %collective-permute-done.25.onward.rest_1_ = bf16[16,96,128]{2,1,0:T(8,128)(2,1)} collective-permute-done((bf16[16,96,128]{2,1,0:T(8,128)(2,1)}, bf16[16,96,128]{2,1,0:T(8,128)(2,1)}, u32[]{:S(2)}, u32[]{:S(2)}) %collective-permute-start.25) | collective-permute-done | bytes 393248 | tf_op jit(solution)/shard_map/ppermute | solution.py:661
  180.0 6.2 %collective-permute-done.28.onward.rest_1_ = bf16[16,96,128]{2,1,0:T(8,128)(2,1)} collective-permute-done((bf16[16,96,128]{2,1,0:T(8,128)(2,1)}, bf16[16,96,128]{2,1,0:T(8,128)(2,1)}, u32[]{:S(2)}, u32[]{:S(2)}) %collective-permute-start.28) | collective-permute-done | bytes 393248 | tf_op jit(solution)/shard_map/ppermute | solution.py:661
  188.2 2.0 collective-permute-done.26.rest_2_
  190.2 2.8 copy-done.14
  193.0 3.9 %aggregate.8.rest_0_ = bf16[16,96,128]{2,1,0:T(8,128)(2,1)S(1)} custom-call(s32[609]{0:T(1024)S(1)} %copy-done.9, bf16[192,128,128]{2,1,0:T(8,128)(2,1)S(1)} %copy-done.14, f32[16,8,128]{2,1,0:T(8,128)S(1)} %get-tuple-element.55.inverse, f32[16,192,128]{2,1,0:T(8,128)S(1)} %copy-done.42, bf16[16,96,128]{2,1,0:T(8,128)(2,1)} %collective-permute-done.24.mixed.rest_0_, ...), custom_call_target="tpu_custom_call" | custom-call | flops 3000000000 | bytes 9000000 | tf_op jit(solution)/shard_map/aggregate/pallas_call | solution.py:536
  198.6 3.8 %aggregate.9.rest_0_ = bf16[16,96,128]{2,1,0:T(8,128)(2,1)S(1)} custom-call(s32[609]{0:T(1024)S(1)} %copy-done.9, bf16[192,128,128]{2,1,0:T(8,128)(2,1)S(1)} %copy-done.14, f32[16,8,128]{2,1,0:T(8,128)S(1)} %get-tuple-element.55.inverse, f32[16,192,128]{2,1,0:T(8,128)S(1)} %copy-done.42, bf16[16,96,128]{2,1,0:T(8,128)(2,1)S(1)} %collective-permute-done.27.mixed.rest_0_, ...), custom_call_target="tpu_custom_call" | custom-call | flops 3000000000 | bytes 9000000 | tf_op jit(solution)/shard_map/aggregate/pallas_call | solution.py:536
  203.9 5.1 %collective-permute-done.30.rest_2_ = bf16[16,96,128]{2,1,0:T(8,128)(2,1)S(1)} collective-permute-done((bf16[16,96,128]{2,1,0:T(8,128)(2,1)S(1)}, bf16[16,96,128]{2,1,0:T(8,128)(2,1)S(1)}, u32[]{:S(2)}, u32[]{:S(2)}) %collective-permute-start.30) | collective-permute-done | bytes 393248 | tf_op jit(solution)/shard_map/ppermute | solution.py:56
  209.5 5.9 %collective-permute-done.34.rest_2_ = bf16[16,96,128]{2,1,0:T(8,128)(2,1)S(1)} collective-permute-done((bf16[16,96,128]{2,1,0:T(8,128)(2,1)S(1)}, bf16[16,96,128]{2,1,0:T(8,128)(2,1)S(1)}, u32[]{:S(2)}, u32[]{:S(2)}) %collective-permute-start.34) | collective-permute-done | bytes 393248 | tf_op jit(solution)/shard_map/ppermute | solution.py:56
  215.4 1.7 update.8.before
  217.2 2.6 update.9.source.own.rest_0_
  221.1 4.6 %collective-permute-start.36 = (bf16[16,192,128]{2,1,0:T(8,128)(2,1)}, bf16[16,192,128]{2,1,0:T(8,128)(2,1)S(1)}, u32[]{:S(2)}, u32[]{:S(2)}) collective-permute-start(bf16[16,192,128]{2,1,0:T(8,128)(2,1)} %update.9.source.own.rest_0_), channel_id=1, source_target_pairs={{0,8},{4,12},{8,16},{12,20},{16,24},{20,28},{1,9},{5,13},{9,17},{1... | collective-permute-start | bytes 2359304 | tf_op jit(solution)/shard_map/ppermute | solution.py:661
  227.8 10.3 %collective-permute-done.38.rest_3_ = bf16[8,192,128]{2,1,0:T(8,128)(2,1)S(1)} collective-permute-done((bf16[8,192,128]{2,1,0:T(8,128)(2,1)S(1)}, bf16[8,192,128]{2,1,0:T(8,128)(2,1)S(1)}, u32[]{:S(2)}, u32[]{:S(2)}) %collective-permute-start.38) | collective-permute-done | bytes 393248 | tf_op jit(solution)/shard_map/ppermute | solution.py:51
  238.9 2.9 collective-permute-done.37.above.rest_2_
  243.1 2.6 near.5
  249.1 2.8 collective-permute-start.43
  253.1 3.2 collective-permute-done.39.rest_4_
  256.4 2.8 copy-done.15
  260.2 5.7 %sum_early.5.early = f32[16,192,128]{2,1,0:T(8,128)S(1)} custom-call(s32[609]{0:T(1024)S(1)} %copy-done.9, bf16[192,128,128]{2,1,0:T(8,128)(2,1)S(1)} %copy-done.15, bf16[16,192,128]{2,1,0:T(8,128)(2,1)} %update.9.source.own.rest_0_, bf16[16,192,128]{2,1,0:T(8,128)(2,1)S(1)} %collective-permute-done.36.below.rest_1_, ...), custom_call_target="tpu_custom_call" | custom-call | flops 6000000000 | bytes 18000000 | tf_op jit(solution)/shard_map/sum_early/pallas_call | solution.py:536
  267.0 1.9 copy-done.19
  268.9 2.0 own_product.5.before
  270.9 5.0 %collective-permute-done.41.onward.rest_1_ = bf16[16,96,128]{2,1,0:T(8,128)(2,1)} collective-permute-done((bf16[16,96,128]{2,1,0:T(8,128)(2,1)}, bf16[16,96,128]{2,1,0:T(8,128)(2,1)}, u32[]{:S(2)}, u32[]{:S(2)}) %collective-permute-start.41) | collective-permute-done | bytes 393248 | tf_op jit(solution)/shard_map/ppermute | solution.py:661
  278.4 5.7 %collective-permute-done.44.onward.rest_1_ = bf16[16,96,128]{2,1,0:T(8,128)(2,1)S(1)} collective-permute-done((bf16[16,96,128]{2,1,0:T(8,128)(2,1)}, bf16[16,96,128]{2,1,0:T(8,128)(2,1)S(1)}, u32[]{:S(2)}, u32[]{:S(2)}) %collective-permute-start.44) | collective-permute-done | bytes 393248 | tf_op jit(solution)/shard_map/ppermute | solution.py:661
  286.1 2.6 collective-permute-done.42.rest_2_
  288.8 2.8 copy-done.16
  291.5 3.9 %aggregate.10.rest_0_ = bf16[16,96,128]{2,1,0:T(8,128)(2,1)S(1)} custom-call(s32[609]{0:T(1024)S(1)} %copy-done.9, bf16[192,128,128]{2,1,0:T(8,128)(2,1)S(1)} %copy-done.16, f32[16,8,128]{2,1,0:T(8,128)S(1)} %get-tuple-element.55.inverse, f32[16,192,128]{2,1,0:T(8,128)S(1)} %copy-done.38, bf16[16,96,128]{2,1,0:T(8,128)(2,1)} %collective-permute-done.40.mixed.rest_0_, ...), custom_call_target="tpu_custom_call" | custom-call | flops 3000000000 | bytes 9000000 | tf_op jit(solution)/shard_map/aggregate/pallas_call | solution.py:536
  295.4 1.6 collective-permute-start.46
  297.0 3.4 %aggregate.11.rest_0_ = bf16[16,96,128]{2,1,0:T(8,128)(2,1)S(1)} custom-call(s32[609]{0:T(1024)S(1)} %copy-done.9, bf16[192,128,128]{2,1,0:T(8,128)(2,1)S(1)} %copy-done.16, f32[16,8,128]{2,1,0:T(8,128)S(1)} %get-tuple-element.55.inverse, f32[16,192,128]{2,1,0:T(8,128)S(1)} %copy-done.38, bf16[16,96,128]{2,1,0:T(8,128)(2,1)S(1)} %collective-permute-done.43.mixed.rest_0_, ...), custom_call_target="tpu_custom_call" | custom-call | flops 3000000000 | bytes 9000000 | tf_op jit(solution)/shard_map/aggregate/pallas_call | solution.py:536
  301.6 6.0 %collective-permute-done.46.rest_2_ = bf16[16,96,128]{2,1,0:T(8,128)(2,1)S(1)} collective-permute-done((bf16[16,96,128]{2,1,0:T(8,128)(2,1)S(1)}, bf16[16,96,128]{2,1,0:T(8,128)(2,1)S(1)}, u32[]{:S(2)}, u32[]{:S(2)}) %collective-permute-start.46) | collective-permute-done | bytes 393248 | tf_op jit(solution)/shard_map/ppermute | solution.py:56
  308.1 5.4 %collective-permute-done.50.rest_2_ = bf16[16,96,128]{2,1,0:T(8,128)(2,1)S(1)} collective-permute-done((bf16[16,96,128]{2,1,0:T(8,128)(2,1)S(1)}, bf16[16,96,128]{2,1,0:T(8,128)(2,1)S(1)}, u32[]{:S(2)}, u32[]{:S(2)}) %collective-permute-start.50) | collective-permute-done | bytes 393248 | tf_op jit(solution)/shard_map/ppermute | solution.py:56
  313.5 1.7 update.10.before
  315.2 1.7 update.11
  (194 shorter events, 73.0 us)
Async XLA Ops:
  6.5 70.5 %all-gather.4.cloned.1.call-start = ((), (), s32[]{:S(2)}) async-start(), calls=%async_computation | async-start | bytes 3932160 | tf_op jit(solution)/shard_map/all_gather | solution.py:706
  8.8 159.9 %all-gather.6.cloned.1.call-start = ((), (), s32[]{:S(2)}) async-start(), calls=%async_computation.1 | async-start | bytes 3932160 | tf_op jit(solution)/shard_map/all_gather | solution.py:706
  9.0 13.7 %collective-permute-start.2 = (s32[1,8,9]{2,1,0:T(8,128)S(1)}, s32[1,8,9]{2,1,0:T(8,128)S(1)}, u32[]{:S(2)}, u32[]{:S(2)}) collective-permute-start(s32[1,8,9]{2,1,0:T(8,128)S(1)} %pad_add_fusion.1), channel_id=1, source_target_pairs={{0,24},{4,28},{8,0},{12,4},{16,8},{20,12},{24,16},{28,20},{1,25},{... | collective-permute-start | bytes 872 | tf_op jit(solution)/shard_map/ppermute | solution.py:46
  14.1 8.7 %collective-permute-start.1 = (s32[1,8,9]{2,1,0:T(8,128)S(1)}, s32[1,8,9]{2,1,0:T(8,128)S(1)}, u32[]{:S(2)}, u32[]{:S(2)}) collective-permute-start(s32[1,8,9]{2,1,0:T(8,128)S(1)} %pad_add_fusion.1), channel_id=1, source_target_pairs={{0,16},{4,20},{8,24},{12,28},{16,0},{20,4},{24,8},{28,12},{1,17},{... | collective-permute-start | bytes 872 | tf_op jit(solution)/shard_map/ppermute | solution.py:46
  14.1 8.7 %collective-permute-start = (s32[1,8,9]{2,1,0:T(8,128)S(1)}, s32[1,8,9]{2,1,0:T(8,128)S(1)}, u32[]{:S(2)}, u32[]{:S(2)}) collective-permute-start(s32[1,8,9]{2,1,0:T(8,128)S(1)} %pad_add_fusion.1), channel_id=1, source_target_pairs={{0,8},{4,12},{8,16},{12,20},{16,24},{20,28},{24,0},{28,4},{1,9},{5... | collective-permute-start | bytes 872 | tf_op jit(solution)/shard_map/ppermute | solution.py:46
  15.1 23.7 %collective-permute-start.5 = (bf16[16,192,128]{2,1,0:T(8,128)(2,1)}, bf16[16,192,128]{2,1,0:T(8,128)(2,1)S(1)}, u32[]{:S(2)}, u32[]{:S(2)}) collective-permute-start(bf16[16,192,128]{2,1,0:T(8,128)(2,1)} %bitcast_bitcast_fusion.source.own.rest_0_), channel_id=1, source_target_pairs={{8,0},{12,4},{16,8},{20,12},{24,16},{28,20},{9,1},{13,5},{17,9},{2... | collective-permute-start | bytes 2359304 | tf_op jit(solution)/shard_map/ppermute | solution.py:661
  16.3 23.3 %collective-permute-start.4 = (bf16[16,192,128]{2,1,0:T(8,128)(2,1)}, bf16[16,192,128]{2,1,0:T(8,128)(2,1)S(1)}, u32[]{:S(2)}, u32[]{:S(2)}) collective-permute-start(bf16[16,192,128]{2,1,0:T(8,128)(2,1)} %bitcast_bitcast_fusion.source.own.rest_0_), channel_id=1, source_target_pairs={{0,8},{4,12},{8,16},{12,20},{16,24},{20,28},{1,9},{5,13},{9,17},{1... | collective-permute-start | bytes 2359304 | tf_op jit(solution)/shard_map/ppermute | solution.py:661
  22.8 5.1 %collective-permute-start.3 = (s32[4,8,9]{2,1,0:T(8,128)S(1)}, s32[4,8,9]{2,1,0:T(8,128)S(1)}, u32[]{:S(2)}, u32[]{:S(2)}) collective-permute-start(s32[4,8,9]{2,1,0:T(8,128)S(1)} %pad_add_fusion.mine), channel_id=1, source_target_pairs={{0,4},{4,0},{8,12},{12,8},{16,20},{20,16},{24,28},{28,24},{1,5},{5... | collective-permute-start | bytes 3464 | tf_op jit(solution)/shard_map/ppermute | solution.py:51
  27.3 13.3 %copy-start.44 = (s32[7,8]{1,0:T(8,128)S(1)}, s32[7,8]{1,0:T(8,128)}, u32[]{:S(2)}) copy-start(s32[7,8]{1,0:T(8,128)} %picks.1) | copy-start | bytes 676
  27.3 10.7 %collective-permute-start.6 = (bf16[8,192,128]{2,1,0:T(8,128)(2,1)S(1)}, bf16[8,192,128]{2,1,0:T(8,128)(2,1)S(1)}, u32[]{:S(2)}, u32[]{:S(2)}) collective-permute-start(bf16[8,192,128]{2,1,0:T(8,128)(2,1)S(1)} %pick.3), channel_id=1, source_target_pairs={{0,4},{4,0},{8,12},{12,8},{16,20},{20,16},{24,28},{28,24},{1,5},{5... | collective-permute-start | bytes 1179656 | tf_op jit(solution)/shard_map/ppermute | solution.py:51
  28.5 22.0 %copy-start.10 = (s32[2]{0:T(128)S(1)}, s32[2]{0:T(128)}, u32[]{:S(2)}) copy-start(s32[2]{0:T(128)} %pad_add_fusion.2.spot) | copy-start | bytes 28
  44.0 6.6 %copy-start.3 = (bf16[3,768,768]{2,1,0:T(8,128)(2,1)S(1)}, bf16[3,768,768]{2,1,0:T(8,128)(2,1)}, u32[]{:S(2)}) copy-start(bf16[3,768,768]{2,1,0:T(8,128)(2,1)} %w.3) | copy-start | bytes 10616836
  46.2 21.4 %collective-permute-start.7 = (bf16[8,192,128]{2,1,0:T(8,128)(2,1)}, bf16[8,192,128]{2,1,0:T(8,128)(2,1)}, u32[]{:S(2)}, u32[]{:S(2)}) collective-permute-start(bf16[8,192,128]{2,1,0:T(8,128)(2,1)} %get-tuple-element.52), channel_id=1, source_target_pairs={{0,4},{4,0},{8,12},{12,8},{16,20},{20,16},{24,28},{28,24},{1,5},{5... | collective-permute-start | bytes 1179656 | tf_op jit(solution)/shard_map/ppermute | solution.py:51
  52.8 6.6 %copy-start.9 = (s32[609]{0:T(1024)S(1)}, s32[609]{0:T(1024)}, u32[]{:S(2)}) copy-start(s32[609]{0:T(1024)} %plan.1.index) | copy-start | bytes 7312
  52.9 28.0 %collective-permute-start.8 = (bf16[16,96,128]{2,1,0:T(8,128)(2,1)}, bf16[16,96,128]{2,1,0:T(8,128)(2,1)}, u32[]{:S(2)}, u32[]{:S(2)}) collective-permute-start(bf16[16,96,128]{2,1,0:T(8,128)(2,1)} %get-tuple-element.57), channel_id=1, source_target_pairs={{0,24},{4,28},{24,0},{28,4},{8,16},{12,20},{16,8},{20,12},{1,25},{... | collective-permute-start | bytes 1179656 | tf_op jit(solution)/shard_map/ppermute | solution.py:661
  54.2 26.8 %collective-permute-start.9 = (bf16[16,96,128]{2,1,0:T(8,128)(2,1)}, bf16[16,96,128]{2,1,0:T(8,128)(2,1)}, u32[]{:S(2)}, u32[]{:S(2)}) collective-permute-start(bf16[16,96,128]{2,1,0:T(8,128)(2,1)} %get-tuple-element.58), channel_id=1, source_target_pairs={{8,0},{12,4},{16,24},{20,28},{9,1},{13,5},{17,25},{21,29},{10,2},{... | collective-permute-start | bytes 1179656 | tf_op jit(solution)/shard_map/ppermute | solution.py:661
  55.5 28.5 %collective-permute-start.11 = (bf16[16,96,128]{2,1,0:T(8,128)(2,1)}, bf16[16,96,128]{2,1,0:T(8,128)(2,1)}, u32[]{:S(2)}, u32[]{:S(2)}) collective-permute-start(bf16[16,96,128]{2,1,0:T(8,128)(2,1)} %get-tuple-element.61), channel_id=1, source_target_pairs={{0,24},{4,28},{24,0},{28,4},{8,16},{12,20},{16,8},{20,12},{1,25},{... | collective-permute-start | bytes 1179656 | tf_op jit(solution)/shard_map/ppermute | solution.py:661
  58.1 31.2 %collective-permute-start.12 = (bf16[16,96,128]{2,1,0:T(8,128)(2,1)}, bf16[16,96,128]{2,1,0:T(8,128)(2,1)}, u32[]{:S(2)}, u32[]{:S(2)}) collective-permute-start(bf16[16,96,128]{2,1,0:T(8,128)(2,1)} %get-tuple-element.62), channel_id=1, source_target_pairs={{8,0},{12,4},{16,24},{20,28},{9,1},{13,5},{17,25},{21,29},{10,2},{... | collective-permute-start | bytes 1179656 | tf_op jit(solution)/shard_map/ppermute | solution.py:661
  67.7 9.3 %copy-start.8 = (f32[192,1]{1,0:T(8,128)S(1)}, f32[192,1]{1,0:T(8,128)}, u32[]{:S(2)}) copy-start(f32[192,1]{1,0:T(8,128)} %copy.19.bias) | copy-start | bytes 2308
  78.9 14.6 %copy-start.40 = (f32[16,192,128]{2,1,0:T(8,128)S(1)}, f32[16,192,128]{2,1,0:T(8,128)}, u32[]{:S(2)}) copy-start(f32[16,192,128]{2,1,0:T(8,128)} %copy-done.39) | copy-start | bytes 4718596
  81.0 12.5 %copy-start.12 = (bf16[192,128,128]{2,1,0:T(8,128)(2,1)S(1)}, bf16[192,128,128]{2,1,0:T(8,128)(2,1)}, u32[]{:S(2)}) copy-start(bf16[192,128,128]{2,1,0:T(8,128)(2,1)} %copy-done.11) | copy-start | bytes 18874372
  82.4 11.1 %collective-permute-start.10 = (bf16[16,96,128]{2,1,0:T(8,128)(2,1)S(1)}, bf16[16,96,128]{2,1,0:T(8,128)(2,1)S(1)}, u32[]{:S(2)}, u32[]{:S(2)}) collective-permute-start(bf16[16,96,128]{2,1,0:T(8,128)(2,1)S(1)} %far.6), channel_id=1, source_target_pairs={{0,4},{4,0},{8,12},{12,8},{16,20},{20,16},{24,28},{28,24},{1,5},{5... | collective-permute-start | bytes 1179656 | tf_op jit(solution)/shard_map/ppermute | solution.py:51
  90.6 11.3 %collective-permute-start.16 = (bf16[16,96,128]{2,1,0:T(8,128)(2,1)S(1)}, bf16[16,96,128]{2,1,0:T(8,128)(2,1)S(1)}, u32[]{:S(2)}, u32[]{:S(2)}) collective-permute-start(bf16[16,96,128]{2,1,0:T(8,128)(2,1)S(1)} %far.7), channel_id=1, source_target_pairs={{0,4},{4,0},{8,12},{12,8},{16,20},{20,16},{24,28},{28,24},{1,5},{5... | collective-permute-start | bytes 1179656 | tf_op jit(solution)/shard_map/ppermute | solution.py:51
  97.4 10.1 %collective-permute-start.14 = (bf16[16,96,128]{2,1,0:T(8,128)(2,1)S(1)}, bf16[16,96,128]{2,1,0:T(8,128)(2,1)S(1)}, u32[]{:S(2)}, u32[]{:S(2)}) collective-permute-start(bf16[16,96,128]{2,1,0:T(8,128)(2,1)S(1)} %aggregate.6.rest_0_), channel_id=1, source_target_pairs={{0,2},{1,3},{2,0},{3,1},{4,6},{5,7},{6,4},{7,5},{8,10},{9,11},{10,... | collective-permute-start | bytes 1179656 | tf_op jit(solution)/shard_map/ppermute | solution.py:56
  105.9 10.4 %collective-permute-start.18 = (bf16[16,96,128]{2,1,0:T(8,128)(2,1)S(1)}, bf16[16,96,128]{2,1,0:T(8,128)(2,1)S(1)}, u32[]{:S(2)}, u32[]{:S(2)}) collective-permute-start(bf16[16,96,128]{2,1,0:T(8,128)(2,1)S(1)} %aggregate.7.rest_0_), channel_id=1, source_target_pairs={{0,2},{1,3},{2,0},{3,1},{4,6},{5,7},{6,4},{7,5},{8,10},{9,11},{10,... | collective-permute-start | bytes 1179656 | tf_op jit(solution)/shard_map/ppermute | solution.py:56
  107.5 8.9 %collective-permute-start.13 = (bf16[16,96,128]{2,1,0:T(8,128)(2,1)S(1)}, bf16[16,96,128]{2,1,0:T(8,128)(2,1)S(1)}, u32[]{:S(2)}, u32[]{:S(2)}) collective-permute-start(bf16[16,96,128]{2,1,0:T(8,128)(2,1)S(1)} %aggregate.6.rest_0_), channel_id=1, source_target_pairs={{0,1},{1,0},{2,3},{3,2},{4,5},{5,4},{6,7},{7,6},{8,9},{9,8},{10,11... | collective-permute-start | bytes 1179656 | tf_op jit(solution)/shard_map/ppermute | solution.py:56
  107.5 8.9 %collective-permute-start.15 = (bf16[16,96,128]{2,1,0:T(8,128)(2,1)S(1)}, bf16[16,96,128]{2,1,0:T(8,128)(2,1)S(1)}, u32[]{:S(2)}, u32[]{:S(2)}) collective-permute-start(bf16[16,96,128]{2,1,0:T(8,128)(2,1)S(1)} %collective-permute-done.14.rest_2_), channel_id=1, source_target_pairs={{0,1},{1,0},{2,3},{3,2},{4,5},{5,4},{6,7},{7,6},{8,9},{9,8},{10,11... | collective-permute-start | bytes 1179656 | tf_op jit(solution)/shard_map/ppermute | solution.py:56
  110.2 7.8 %collective-permute-start.17 = (bf16[16,96,128]{2,1,0:T(8,128)(2,1)S(1)}, bf16[16,96,128]{2,1,0:T(8,128)(2,1)S(1)}, u32[]{:S(2)}, u32[]{:S(2)}) collective-permute-start(bf16[16,96,128]{2,1,0:T(8,128)(2,1)S(1)} %aggregate.7.rest_0_), channel_id=1, source_target_pairs={{0,1},{1,0},{2,3},{3,2},{4,5},{5,4},{6,7},{7,6},{8,9},{9,8},{10,11... | collective-permute-start | bytes 1179656 | tf_op jit(solution)/shard_map/ppermute | solution.py:56
  116.3 1.8 collective-permute-start.19
  120.7 146.3 %all-gather.8.cloned.1.call-start = ((), (), s32[]{:S(2)}) async-start(), calls=%async_computation.2 | async-start | bytes 3932160 | tf_op jit(solution)/shard_map/all_gather | solution.py:706
  120.7 22.1 %collective-permute-start.21 = (bf16[16,192,128]{2,1,0:T(8,128)(2,1)}, bf16[16,192,128]{2,1,0:T(8,128)(2,1)S(1)}, u32[]{:S(2)}, u32[]{:S(2)}) collective-permute-start(bf16[16,192,128]{2,1,0:T(8,128)(2,1)} %update.7.source.own.rest_0_), channel_id=1, source_target_pairs={{8,0},{12,4},{16,8},{20,12},{24,16},{28,20},{9,1},{13,5},{17,9},{2... | collective-permute-start | bytes 2359304 | tf_op jit(solution)/shard_map/ppermute | solution.py:661
  122.0 22.0 %collective-permute-start.20 = (bf16[16,192,128]{2,1,0:T(8,128)(2,1)}, bf16[16,192,128]{2,1,0:T(8,128)(2,1)S(1)}, u32[]{:S(2)}, u32[]{:S(2)}) collective-permute-start(bf16[16,192,128]{2,1,0:T(8,128)(2,1)} %update.7.source.own.rest_0_), channel_id=1, source_target_pairs={{0,8},{4,12},{8,16},{12,20},{16,24},{20,28},{1,9},{5,13},{9,17},{1... | collective-permute-start | bytes 2359304 | tf_op jit(solution)/shard_map/ppermute | solution.py:661
  127.9 11.2 %collective-permute-start.22 = (bf16[8,192,128]{2,1,0:T(8,128)(2,1)S(1)}, bf16[8,192,128]{2,1,0:T(8,128)(2,1)S(1)}, u32[]{:S(2)}, u32[]{:S(2)}) collective-permute-start(bf16[8,192,128]{2,1,0:T(8,128)(2,1)S(1)} %pick.4), channel_id=1, source_target_pairs={{0,4},{4,0},{8,12},{12,8},{16,20},{20,16},{24,28},{28,24},{1,5},{5... | collective-permute-start | bytes 1179656 | tf_op jit(solution)/shard_map/ppermute | solution.py:51
  147.1 10.7 %collective-permute-start.23 = (bf16[8,192,128]{2,1,0:T(8,128)(2,1)}, bf16[8,192,128]{2,1,0:T(8,128)(2,1)}, u32[]{:S(2)}, u32[]{:S(2)}) collective-permute-start(bf16[8,192,128]{2,1,0:T(8,128)(2,1)} %get-tuple-element.70), channel_id=1, source_target_pairs={{0,4},{4,0},{8,12},{12,8},{16,20},{20,16},{24,28},{28,24},{1,5},{5... | collective-permute-start | bytes 1179656 | tf_op jit(solution)/shard_map/ppermute | solution.py:51
  148.3 24.3 %collective-permute-start.24 = (bf16[16,96,128]{2,1,0:T(8,128)(2,1)}, bf16[16,96,128]{2,1,0:T(8,128)(2,1)}, u32[]{:S(2)}, u32[]{:S(2)}) collective-permute-start(bf16[16,96,128]{2,1,0:T(8,128)(2,1)} %copy-done.36), channel_id=1, source_target_pairs={{0,24},{4,28},{24,0},{28,4},{8,16},{12,20},{16,8},{20,12},{1,25},{... | collective-permute-start | bytes 1179656 | tf_op jit(solution)/shard_map/ppermute | solution.py:661
  149.3 28.6 %collective-permute-start.25 = (bf16[16,96,128]{2,1,0:T(8,128)(2,1)}, bf16[16,96,128]{2,1,0:T(8,128)(2,1)}, u32[]{:S(2)}, u32[]{:S(2)}) collective-permute-start(bf16[16,96,128]{2,1,0:T(8,128)(2,1)} %copy-done.35), channel_id=1, source_target_pairs={{8,0},{12,4},{16,24},{20,28},{9,1},{13,5},{17,25},{21,29},{10,2},{... | collective-permute-start | bytes 1179656 | tf_op jit(solution)/shard_map/ppermute | solution.py:661
  150.6 29.4 %collective-permute-start.27 = (bf16[16,96,128]{2,1,0:T(8,128)(2,1)}, bf16[16,96,128]{2,1,0:T(8,128)(2,1)S(1)}, u32[]{:S(2)}, u32[]{:S(2)}) collective-permute-start(bf16[16,96,128]{2,1,0:T(8,128)(2,1)} %copy-done.30), channel_id=1, source_target_pairs={{0,24},{4,28},{24,0},{28,4},{8,16},{12,20},{16,8},{20,12},{1,25},{... | collective-permute-start | bytes 1179656 | tf_op jit(solution)/shard_map/ppermute | solution.py:661
  153.5 32.7 %collective-permute-start.28 = (bf16[16,96,128]{2,1,0:T(8,128)(2,1)}, bf16[16,96,128]{2,1,0:T(8,128)(2,1)}, u32[]{:S(2)}, u32[]{:S(2)}) collective-permute-start(bf16[16,96,128]{2,1,0:T(8,128)(2,1)} %copy-done.29), channel_id=1, source_target_pairs={{8,0},{12,4},{16,24},{20,28},{9,1},{13,5},{17,25},{21,29},{10,2},{... | collective-permute-start | bytes 1179656 | tf_op jit(solution)/shard_map/ppermute | solution.py:661
  179.1 11.1 %copy-start.42 = (f32[16,192,128]{2,1,0:T(8,128)S(1)}, f32[16,192,128]{2,1,0:T(8,128)}, u32[]{:S(2)}) copy-start(f32[16,192,128]{2,1,0:T(8,128)} %copy-done.41) | copy-start | bytes 4718596
  179.1 11.1 %collective-permute-start.26 = (bf16[16,96,128]{2,1,0:T(8,128)(2,1)S(1)}, bf16[16,96,128]{2,1,0:T(8,128)(2,1)S(1)}, u32[]{:S(2)}, u32[]{:S(2)}) collective-permute-start(bf16[16,96,128]{2,1,0:T(8,128)(2,1)S(1)} %far.8), channel_id=1, source_target_pairs={{0,4},{4,0},{8,12},{12,8},{16,20},{20,16},{24,28},{28,24},{1,5},{5... | collective-permute-start | bytes 1179656 | tf_op jit(solution)/shard_map/ppermute | solution.py:51
  187.3 11.2 %collective-permute-start.32 = (bf16[16,96,128]{2,1,0:T(8,128)(2,1)S(1)}, bf16[16,96,128]{2,1,0:T(8,128)(2,1)S(1)}, u32[]{:S(2)}, u32[]{:S(2)}) collective-permute-start(bf16[16,96,128]{2,1,0:T(8,128)(2,1)S(1)} %far.9), channel_id=1, source_target_pairs={{0,4},{4,0},{8,12},{12,8},{16,20},{20,16},{24,28},{28,24},{1,5},{5... | collective-permute-start | bytes 1179656 | tf_op jit(solution)/shard_map/ppermute | solution.py:51
  196.9 12.1 %collective-permute-start.30 = (bf16[16,96,128]{2,1,0:T(8,128)(2,1)S(1)}, bf16[16,96,128]{2,1,0:T(8,128)(2,1)S(1)}, u32[]{:S(2)}, u32[]{:S(2)}) collective-permute-start(bf16[16,96,128]{2,1,0:T(8,128)(2,1)S(1)} %aggregate.8.rest_0_), channel_id=1, source_target_pairs={{0,2},{1,3},{2,0},{3,1},{4,6},{5,7},{6,4},{7,5},{8,10},{9,11},{10,... | collective-permute-start | bytes 1179656 | tf_op jit(solution)/shard_map/ppermute | solution.py:56
  202.4 13.1 %collective-permute-start.34 = (bf16[16,96,128]{2,1,0:T(8,128)(2,1)S(1)}, bf16[16,96,128]{2,1,0:T(8,128)(2,1)S(1)}, u32[]{:S(2)}, u32[]{:S(2)}) collective-permute-start(bf16[16,96,128]{2,1,0:T(8,128)(2,1)S(1)} %aggregate.9.rest_0_), channel_id=1, source_target_pairs={{0,2},{1,3},{2,0},{3,1},{4,6},{5,7},{6,4},{7,5},{8,10},{9,11},{10,... | collective-permute-start | bytes 1179656 | tf_op jit(solution)/shard_map/ppermute | solution.py:56
  203.9 11.5 %collective-permute-start.29 = (bf16[16,96,128]{2,1,0:T(8,128)(2,1)S(1)}, bf16[16,96,128]{2,1,0:T(8,128)(2,1)S(1)}, u32[]{:S(2)}, u32[]{:S(2)}) collective-permute-start(bf16[16,96,128]{2,1,0:T(8,128)(2,1)S(1)} %aggregate.8.rest_0_), channel_id=1, source_target_pairs={{0,1},{1,0},{2,3},{3,2},{4,5},{5,4},{6,7},{7,6},{8,9},{9,8},{10,11... | collective-permute-start | bytes 1179656 | tf_op jit(solution)/shard_map/ppermute | solution.py:56
  209.0 6.4 %collective-permute-start.31 = (bf16[16,96,128]{2,1,0:T(8,128)(2,1)S(1)}, bf16[16,96,128]{2,1,0:T(8,128)(2,1)S(1)}, u32[]{:S(2)}, u32[]{:S(2)}) collective-permute-start(bf16[16,96,128]{2,1,0:T(8,128)(2,1)S(1)} %collective-permute-done.30.rest_2_), channel_id=1, source_target_pairs={{0,1},{1,0},{2,3},{3,2},{4,5},{5,4},{6,7},{7,6},{8,9},{9,8},{10,11... | collective-permute-start | bytes 1179656 | tf_op jit(solution)/shard_map/ppermute | solution.py:56
  209.0 8.1 %collective-permute-start.33 = (bf16[16,96,128]{2,1,0:T(8,128)(2,1)S(1)}, bf16[16,96,128]{2,1,0:T(8,128)(2,1)S(1)}, u32[]{:S(2)}, u32[]{:S(2)}) collective-permute-start(bf16[16,96,128]{2,1,0:T(8,128)(2,1)S(1)} %aggregate.9.rest_0_), channel_id=1, source_target_pairs={{0,1},{1,0},{2,3},{3,2},{4,5},{5,4},{6,7},{7,6},{8,9},{9,8},{10,11... | collective-permute-start | bytes 1179656 | tf_op jit(solution)/shard_map/ppermute | solution.py:56
  215.4 1.8 collective-permute-start.35
  219.8 22.0 %collective-permute-start.37 = (bf16[16,192,128]{2,1,0:T(8,128)(2,1)}, bf16[16,192,128]{2,1,0:T(8,128)(2,1)S(1)}, u32[]{:S(2)}, u32[]{:S(2)}) collective-permute-start(bf16[16,192,128]{2,1,0:T(8,128)(2,1)} %update.9.source.own.rest_0_), channel_id=1, source_target_pairs={{8,0},{12,4},{16,8},{20,12},{24,16},{28,20},{9,1},{13,5},{17,9},{2... | collective-permute-start | bytes 2359304 | tf_op jit(solution)/shard_map/ppermute | solution.py:661
  221.1 22.0 %collective-permute-start.36 = (bf16[16,192,128]{2,1,0:T(8,128)(2,1)}, bf16[16,192,128]{2,1,0:T(8,128)(2,1)S(1)}, u32[]{:S(2)}, u32[]{:S(2)}) collective-permute-start(bf16[16,192,128]{2,1,0:T(8,128)(2,1)} %update.9.source.own.rest_0_), channel_id=1, source_target_pairs={{0,8},{4,12},{8,16},{12,20},{16,24},{20,28},{1,9},{5,13},{9,17},{1... | collective-permute-start | bytes 2359304 | tf_op jit(solution)/shard_map/ppermute | solution.py:661
  227.0 11.1 %collective-permute-start.38 = (bf16[8,192,128]{2,1,0:T(8,128)(2,1)S(1)}, bf16[8,192,128]{2,1,0:T(8,128)(2,1)S(1)}, u32[]{:S(2)}, u32[]{:S(2)}) collective-permute-start(bf16[8,192,128]{2,1,0:T(8,128)(2,1)S(1)} %pick.5), channel_id=1, source_target_pairs={{0,4},{4,0},{8,12},{12,8},{16,20},{20,16},{24,28},{28,24},{1,5},{5... | collective-permute-start | bytes 1179656 | tf_op jit(solution)/shard_map/ppermute | solution.py:51
  245.7 10.7 %collective-permute-start.39 = (bf16[8,192,128]{2,1,0:T(8,128)(2,1)}, bf16[8,192,128]{2,1,0:T(8,128)(2,1)}, u32[]{:S(2)}, u32[]{:S(2)}) collective-permute-start(bf16[8,192,128]{2,1,0:T(8,128)(2,1)} %get-tuple-element.84), channel_id=1, source_target_pairs={{0,4},{4,0},{8,12},{12,8},{16,20},{20,16},{24,28},{28,24},{1,5},{5... | collective-permute-start | bytes 1179656 | tf_op jit(solution)/shard_map/ppermute | solution.py:51
  246.6 24.3 %collective-permute-start.40 = (bf16[16,96,128]{2,1,0:T(8,128)(2,1)}, bf16[16,96,128]{2,1,0:T(8,128)(2,1)}, u32[]{:S(2)}, u32[]{:S(2)}) collective-permute-start(bf16[16,96,128]{2,1,0:T(8,128)(2,1)} %get-tuple-element.85), channel_id=1, source_target_pairs={{0,24},{4,28},{24,0},{28,4},{8,16},{12,20},{16,8},{20,12},{1,25},{... | collective-permute-start | bytes 1179656 | tf_op jit(solution)/shard_map/ppermute | solution.py:661
  247.8 28.2 %collective-permute-start.41 = (bf16[16,96,128]{2,1,0:T(8,128)(2,1)}, bf16[16,96,128]{2,1,0:T(8,128)(2,1)}, u32[]{:S(2)}, u32[]{:S(2)}) collective-permute-start(bf16[16,96,128]{2,1,0:T(8,128)(2,1)} %get-tuple-element.86), channel_id=1, source_target_pairs={{8,0},{12,4},{16,24},{20,28},{9,1},{13,5},{17,25},{21,29},{10,2},{... | collective-permute-start | bytes 1179656 | tf_op jit(solution)/shard_map/ppermute | solution.py:661
  249.1 29.4 %collective-permute-start.43 = (bf16[16,96,128]{2,1,0:T(8,128)(2,1)}, bf16[16,96,128]{2,1,0:T(8,128)(2,1)S(1)}, u32[]{:S(2)}, u32[]{:S(2)}) collective-permute-start(bf16[16,96,128]{2,1,0:T(8,128)(2,1)} %get-tuple-element.89), channel_id=1, source_target_pairs={{0,24},{4,28},{24,0},{28,4},{8,16},{12,20},{16,8},{20,12},{1,25},{... | collective-permute-start | bytes 1179656 | tf_op jit(solution)/shard_map/ppermute | solution.py:661
  251.9 32.3 %collective-permute-start.44 = (bf16[16,96,128]{2,1,0:T(8,128)(2,1)}, bf16[16,96,128]{2,1,0:T(8,128)(2,1)S(1)}, u32[]{:S(2)}, u32[]{:S(2)}) collective-permute-start(bf16[16,96,128]{2,1,0:T(8,128)(2,1)} %copy-done.28), channel_id=1, source_target_pairs={{8,0},{12,4},{16,24},{20,28},{9,1},{13,5},{17,25},{21,29},{10,2},{... | collective-permute-start | bytes 1179656 | tf_op jit(solution)/shard_map/ppermute | solution.py:661
  277.2 11.6 %copy-start.38 = (f32[16,192,128]{2,1,0:T(8,128)S(1)}, f32[16,192,128]{2,1,0:T(8,128)}, u32[]{:S(2)}) copy-start(f32[16,192,128]{2,1,0:T(8,128)} %copy-done.37) | copy-start | bytes 4718596
  277.2 11.6 %collective-permute-start.42 = (bf16[16,96,128]{2,1,0:T(8,128)(2,1)S(1)}, bf16[16,96,128]{2,1,0:T(8,128)(2,1)S(1)}, u32[]{:S(2)}, u32[]{:S(2)}) collective-permute-start(bf16[16,96,128]{2,1,0:T(8,128)(2,1)S(1)} %far.10), channel_id=1, source_target_pairs={{0,4},{4,0},{8,12},{12,8},{16,20},{20,16},{24,28},{28,24},{1,5},{5... | collective-permute-start | bytes 1179656 | tf_op jit(solution)/shard_map/ppermute | solution.py:51
  284.9 12.2 %collective-permute-start.48 = (bf16[16,96,128]{2,1,0:T(8,128)(2,1)S(1)}, bf16[16,96,128]{2,1,0:T(8,128)(2,1)S(1)}, u32[]{:S(2)}, u32[]{:S(2)}) collective-permute-start(bf16[16,96,128]{2,1,0:T(8,128)(2,1)S(1)} %far.11), channel_id=1, source_target_pairs={{0,4},{4,0},{8,12},{12,8},{16,20},{20,16},{24,28},{28,24},{1,5},{5... | collective-permute-start | bytes 1179656 | tf_op jit(solution)/shard_map/ppermute | solution.py:51
  295.4 12.1 %collective-permute-start.46 = (bf16[16,96,128]{2,1,0:T(8,128)(2,1)S(1)}, bf16[16,96,128]{2,1,0:T(8,128)(2,1)S(1)}, u32[]{:S(2)}, u32[]{:S(2)}) collective-permute-start(bf16[16,96,128]{2,1,0:T(8,128)(2,1)S(1)} %aggregate.10.rest_0_), channel_id=1, source_target_pairs={{0,2},{1,3},{2,0},{3,1},{4,6},{5,7},{6,4},{7,5},{8,10},{9,11},{10,... | collective-permute-start | bytes 1179656 | tf_op jit(solution)/shard_map/ppermute | solution.py:56
  300.4 13.0 %collective-permute-start.50 = (bf16[16,96,128]{2,1,0:T(8,128)(2,1)S(1)}, bf16[16,96,128]{2,1,0:T(8,128)(2,1)S(1)}, u32[]{:S(2)}, u32[]{:S(2)}) collective-permute-start(bf16[16,96,128]{2,1,0:T(8,128)(2,1)S(1)} %aggregate.11.rest_0_), channel_id=1, source_target_pairs={{0,2},{1,3},{2,0},{3,1},{4,6},{5,7},{6,4},{7,5},{8,10},{9,11},{10,... | collective-permute-start | bytes 1179656 | tf_op jit(solution)/shard_map/ppermute | solution.py:56
  301.6 11.9 %collective-permute-start.45 = (bf16[16,96,128]{2,1,0:T(8,128)(2,1)S(1)}, bf16[16,96,128]{2,1,0:T(8,128)(2,1)S(1)}, u32[]{:S(2)}, u32[]{:S(2)}) collective-permute-start(bf16[16,96,128]{2,1,0:T(8,128)(2,1)S(1)} %aggregate.10.rest_0_), channel_id=1, source_target_pairs={{0,1},{1,0},{2,3},{3,2},{4,5},{5,4},{6,7},{7,6},{8,9},{9,8},{10,11... | collective-permute-start | bytes 1179656 | tf_op jit(solution)/shard_map/ppermute | solution.py:56
  307.6 5.9 %collective-permute-start.47 = (bf16[16,96,128]{2,1,0:T(8,128)(2,1)S(1)}, bf16[16,96,128]{2,1,0:T(8,128)(2,1)S(1)}, u32[]{:S(2)}, u32[]{:S(2)}) collective-permute-start(bf16[16,96,128]{2,1,0:T(8,128)(2,1)S(1)} %collective-permute-done.46.rest_2_), channel_id=1, source_target_pairs={{0,1},{1,0},{2,3},{3,2},{4,5},{5,4},{6,7},{7,6},{8,9},{9,8},{10,11... | collective-permute-start | bytes 1179656 | tf_op jit(solution)/shard_map/ppermute | solution.py:56
  307.6 7.6 %collective-permute-start.49 = (bf16[16,96,128]{2,1,0:T(8,128)(2,1)S(1)}, bf16[16,96,128]{2,1,0:T(8,128)(2,1)S(1)}, u32[]{:S(2)}, u32[]{:S(2)}) collective-permute-start(bf16[16,96,128]{2,1,0:T(8,128)(2,1)S(1)} %aggregate.11.rest_0_), channel_id=1, source_target_pairs={{0,1},{1,0},{2,3},{3,2},{4,5},{5,4},{6,7},{7,6},{8,9},{9,8},{10,11... | collective-permute-start | bytes 1179656 | tf_op jit(solution)/shard_map/ppermute | solution.py:56
  313.5 1.7 collective-permute-start.51
  (40 other events, 84.4 us)
Sparse Core Ops, SparseCore 0:
  8.9 31.2 all-gather.3
  120.8 26.2 all-gather.5
  219.9 26.1 all-gather.7

commit v3 on v2

--- a/solution.py
+++ b/solution.py
@@ -422,7 +422,7 @@
         out[2 * q + 1] = sums[:, BLK:]
         return 0
 
-    lax.fori_loop(0, blocks // 2, body, 0)
+    lax.fori_loop(0, blocks // 2, body, 0, unroll=True)
 
 
 def update_kernel(weights, before, *rest, count, low, kind):
@@ -444,7 +444,7 @@
             out[2 * q + k] = pre.astype(out.dtype)
         return 0
 
-    lax.fori_loop(0, blocks // 2, body, 0)
+    lax.fori_loop(0, blocks // 2, body, 0, unroll=True)
 
 
 def tie(first, *others):
@@ -591,8 +591,12 @@
             cost_estimate=cost(0.01),
         )(spot, w)
 
-    own_w, nbr_w = turned_weights(w_self, False), turned_weights(w_nbr, True)
     own_bias = lax.dynamic_slice_in_dim(bias, feat_here * cols, cols, 1)[:, :, None]
+
+    def weights(*after):
+        if "own" not in made:
+            made["own"] = turned_weights(tie((w_self,), *after)[0], False)
+            made["nbr"] = turned_weights(tie((w_nbr,), *after)[0], True)
 
     def parts_of(number, rows):
         return jax.ShapeDtypeStruct((number, rows, BLK), jnp.bfloat16)
@@ -641,7 +645,7 @@
             out_shape=pltpu.VMEM((blocks, cols, BLK), jnp.float32),
             compiler_params=params(),
             cost_estimate=cost(2),
-        )(own_w[layer], own_bias[layer], full)
+        )(made["own"][layer], own_bias[layer], full)
 
     def update(weights, before, parts, low, kind):
         shapes = [pltpu.VMEM((blocks, cols, BLK), jnp.float32)]
@@ -660,7 +664,7 @@
     def send(x, pairs):
         return lax.ppermute(x, "dom", pairs)
 
-    def from_line(hidden, state):
+    def from_line(hidden, layer, full):
         up = [(i, i + 2) for i in range(n - 2)]
         down = [(i + 2, i) for i in range(n - 2)]
         mix = [(0, 6), (1, 7), (6, 0), (7, 1), (2, 4), (3, 5), (4, 2), (5, 3)]
@@ -672,10 +676,12 @@
         x_near, *onwards = call(near_kernel, "near", shapes, 2, picks, hidden, below, above)
         degrees(x_near)
         x_near = from_partner(x_near)
+        weights(x_near)
         far = [
             (send(onwards[2 * c], mix), send(onwards[2 * c + 1], outward)) for c in range(chunks)
         ]
         early = sum_early([hidden, below, above, x_own, x_near])
+        state = own_product(layer, full)
         listed = []
         for c, (mixed, onward) in enumerate(far):
             mixed, onward = far[c] = tie((mixed, onward), early, state, listed)
@@ -688,28 +694,30 @@
             x_far = from_partner(listed[c])
             x_far, *_ = tie((x_far,), listed, aggs)
             aggs.append(aggregate(early, [mixed, onward, x_far], c))
-        return aggs
-
-    def from_ring(hidden):
+        return aggs, state
+
+    def from_ring(hidden, layer, full):
         behind, ahead = from_behind(hidden, 2), from_behind(hidden, -2)
         behind_two, ahead_two = from_behind(behind, 2), from_behind(ahead, -2)
         x_own = from_partner(pick(hidden, 0))
         x_near = [from_partner(pick(behind, 1)), from_partner(pick(ahead, depth - 1))]
         degrees()
+        weights()
         odd = me % 2 == 1
         x_two = jnp.where(odd, pick(behind_two, 2), pick(ahead_two, depth - 2))
         early = sum_early([hidden, behind, ahead, x_own, *x_near])
-        return [aggregate(early, [behind_two, ahead_two, from_partner(x_two)], 0)]
+        aggs = [aggregate(early, [behind_two, ahead_two, from_partner(x_two)], 0)]
+        return aggs, own_product(layer, full)
 
     for layer in range(layers):
         last = layer == layers - 1
-        state = own_product(layer, lax.all_gather(hidden, "feat", axis=0, tiled=True))
-        aggs = from_line(hidden, state) if line else from_ring(hidden)
+        full = lax.all_gather(hidden, "feat", axis=0, tiled=True)
+        aggs, state = from_line(hidden, layer, full) if line else from_ring(hidden, layer, full)
         for c, agg in enumerate(aggs):
             other = from_feat(agg, 2)
             parts = [agg, from_feat(agg, 1), other, from_feat(other, 1)]
             kind = "sum" if c < chunks - 1 else "none" if last else "relu"
-            (state,) = update(nbr_w[layer], state, parts, c * feat_size * size, kind)
+            (state,) = update(made["nbr"][layer], state, parts, c * feat_size * size, kind)
         hidden = state
     return hidden.transpose(0, 2, 1).reshape(node_rows, cols)
 

time: 324 us -> 312 us (0.963)
  Pallas kernels: 96 us -> 87.2 us
  local copies, waits for them, and re-layouts: 43.9 us -> 38.1 us
    pallas_call x6, Pallas kernels: 11.9 us -> 5.26 us  [update(): pl.pallas_call(functools.partial(update_kernel, count=len(parts), low=low...]
    unnamed x98 -> x76, local copies, waits for them, and re-layouts: 38.5 us -> 34.6 us
    pallas_call x3, Pallas kernels: 5.93 us -> 2.35 us  [own_product(): pl.pallas_call(functools.partial(self_kernel, feats=feat_size), name='own...]
    ppermute x18, waiting for transfers between devices: 28.4 us -> 31.7 us  [from_feat(): return lax.ppermute(x, 'feat', [(i, i ^ bit) for i in range(n)])]
  transfers between devices with their start and end apart: 55 -> 55, of which waited for: 24 -> 27; matrix products, arithmetic and copies ran while one was open for 1% -> 1% of each run, Pallas kernels for 27% -> 27%
where the time goes in v3:
time: 312 us; the launch traced here: 310 us
  waiting for transfers between devices  102 us (33%)
  Pallas kernels  87.2 us (28%)
  starting transfers between devices  67.2 us (22%)
  local copies, waits for them, and re-layouts  38.1 us (12%)
  between operations  14.5 us (5%)
    pallas_call x22, Pallas kernels, call(): pl.pallas_call(functools.partial(kernel, **static), name=name, in_specs=[...  63.6 us
    ppermute x18, starting transfers between devices, send(): return lax.ppermute(x, 'dom', pairs)  37.7 us
    ppermute x18, waiting for transfers between devices, send(): return lax.ppermute(x, 'dom', pairs)  36 us
    ppermute x13, waiting for transfers between devices, from_partner(): return lax.ppermute(x, 'dom', [(i, i ^ 1) for i in range(n)])  34.6 us
    unnamed x76, local copies, waits for them, and re-layouts  34.6 us
    ppermute x18, waiting for transfers between devices, from_feat(): return lax.ppermute(x, 'feat', [(i, i ^ bit) for i in range(n)])  31.7 us
    ppermute x13, starting transfers between devices, from_partner(): return lax.ppermute(x, 'dom', [(i, i ^ 1) for i in range(n)])  12.2 us
    ppermute x18, starting transfers between devices, from_feat(): return lax.ppermute(x, 'feat', [(i, i ^ bit) for i in range(n)])  11.2 us
  transfers between devices with their start and end apart: 55, of which 27 were waited for; matrix products, arithmetic and copies ran while one was open for 1% of the time, Pallas kernels for 27%

profile of v3, /device:TPU:0, one launch (start us, length us, event | category | flops | bytes accessed | tf_op | source)
XLA Modules:
  0.0 310.2 jit_solution(12934438836815657950)
XLA Ops:
  9.0 5.1 %collective-permute-start.2 = (s32[1,8,9]{2,1,0:T(8,128)S(1)}, s32[1,8,9]{2,1,0:T(8,128)S(1)}, u32[]{:S(2)}, u32[]{:S(2)}) collective-permute-start(s32[1,8,9]{2,1,0:T(8,128)S(1)} %pad_add_fusion.1), channel_id=1, source_target_pairs={{0,24},{4,28},{8,0},{12,4},{16,8},{20,12},{24,16},{28,20},{1,25},{... | collective-permute-start | bytes 872 | tf_op jit(solution)/shard_map/ppermute | solution.py:46
  16.3 5.1 %collective-permute-start.3 = (bf16[16,192,128]{2,1,0:T(8,128)(2,1)}, bf16[16,192,128]{2,1,0:T(8,128)(2,1)S(1)}, u32[]{:S(2)}, u32[]{:S(2)}) collective-permute-start(bf16[16,192,128]{2,1,0:T(8,128)(2,1)} %bitcast_bitcast_fusion.source.own.rest_0_), channel_id=1, source_target_pairs={{0,8},{4,12},{8,16},{12,20},{16,24},{20,28},{1,9},{5,13},{9,17},{1... | collective-permute-start | bytes 2359304 | tf_op jit(solution)/shard_map/ppermute | solution.py:665
  22.8 1.5 collective-permute-start.6
  24.4 1.6 picks.1
  28.5 9.9 %plan.1.index = s32[609]{0:T(1024)} custom-call(s32[2]{0:T(128)} %pad_add_fusion.2.spot, s32[1]{0:T(128)S(6)} %copy.28.count, s32[192]{0:T(256)} %dst.1, s32[192]{0:T(256)} %src.1, s32[4,8,9]{2,1,0:T(8,128)} %copy-done.35, s32[4,8,9]{2,1,0:T(8,128)} %copy-done.37), custom_call_target="tpu_custom_call" | custom-call | flops 5000000000 | bytes 15000000 | tf_op jit(solution)/shard_map/plan/pallas_call | solution.py:549
  38.5 1.8 near.3
  43.5 3.4 %collective-permute-start.8 = (bf16[16,96,128]{2,1,0:T(8,128)(2,1)}, bf16[16,96,128]{2,1,0:T(8,128)(2,1)}, u32[]{:S(2)}, u32[]{:S(2)}) collective-permute-start(bf16[16,96,128]{2,1,0:T(8,128)(2,1)} %copy-done.18), channel_id=1, source_target_pairs={{0,24},{4,28},{24,0},{28,4},{8,16},{12,20},{16,8},{20,12},{1,25},{... | collective-permute-start | bytes 1179656 | tf_op jit(solution)/shard_map/ppermute | solution.py:665
  50.0 2.8 copy-done.2
  52.8 5.8 %degree.1 = (f32[16,8,128]{2,1,0:T(8,128)S(1)}, bf16[192,128,128]{2,1,0:T(8,128)(2,1)S(1)}) custom-call(s32[609]{0:T(1024)S(1)} %copy-done.6, bf16[192,128,128]{2,1,0:T(8,128)(2,1)S(1)} %copy-done.2), custom_call_target="tpu_custom_call" | custom-call | flops 10000000 | bytes 30000 | tf_op jit(solution)/shard_map/degree/pallas_call | solution.py:536
  58.6 2.3 turn_weights.3
  60.9 6.8 %sum_early.3.early = f32[16,192,128]{2,1,0:T(8,128)S(1)} custom-call(s32[609]{0:T(1024)S(1)} %copy-done.6, bf16[192,128,128]{2,1,0:T(8,128)(2,1)S(1)} %get-tuple-element.58.tiles, bf16[16,192,128]{2,1,0:T(8,128)(2,1)S(1)} %copy-done.5, bf16[16,192,128]{2,1,0:T(8,128)(2,1)S(1)} %collective-permute-done.3.below.rest_1_, ...), custom_call_target="tpu_custom_call" | custom-call | flops 6000000000 | bytes 18000000 | tf_op jit(solution)/shard_map/sum_early/pallas_call | solution.py:536
  67.7 2.6 copy-done.8
  71.6 1.9 copy-done.14
  75.8 4.1 %collective-permute-done.12.onward.rest_1_ = bf16[16,96,128]{2,1,0:T(8,128)(2,1)} collective-permute-done((bf16[16,96,128]{2,1,0:T(8,128)(2,1)S(1)}, bf16[16,96,128]{2,1,0:T(8,128)(2,1)}, u32[]{:S(2)}, u32[]{:S(2)}) %collective-permute-start.12) | collective-permute-done | bytes 393248 | tf_op jit(solution)/shard_map/ppermute | solution.py:665
  81.1 1.8 collective-permute-start.16
  84.2 3.4 %aggregate.6.rest_0_ = bf16[16,96,128]{2,1,0:T(8,128)(2,1)S(1)} custom-call(s32[609]{0:T(1024)S(1)} %copy-done.6, bf16[192,128,128]{2,1,0:T(8,128)(2,1)S(1)} %copy-done.9, f32[16,8,128]{2,1,0:T(8,128)S(1)} %get-tuple-element.59.inverse, f32[16,192,128]{2,1,0:T(8,128)S(1)} %copy-done.27, bf16[16,96,128]{2,1,0:T(8,128)(2,1)} %collective-permute-done.8.mixed.rest_0_, ...), custom_call_target="tpu_custom_call" | custom-call | flops 3000000000 | bytes 9000000 | tf_op jit(solution)/shard_map/aggregate/pallas_call | solution.py:536
  87.6 1.6 collective-permute-start.14
  89.2 3.2 %collective-permute-done.16.rest_2_ = bf16[16,96,128]{2,1,0:T(8,128)(2,1)S(1)} collective-permute-done((bf16[16,96,128]{2,1,0:T(8,128)(2,1)S(1)}, bf16[16,96,128]{2,1,0:T(8,128)(2,1)S(1)}, u32[]{:S(2)}, u32[]{:S(2)}) %collective-permute-start.16) | collective-permute-done | bytes 393248 | tf_op jit(solution)/shard_map/ppermute | solution.py:51
  92.4 3.6 %aggregate.7.rest_0_ = bf16[16,96,128]{2,1,0:T(8,128)(2,1)S(1)} custom-call(s32[609]{0:T(1024)S(1)} %copy-done.6, bf16[192,128,128]{2,1,0:T(8,128)(2,1)S(1)} %copy-done.9, f32[16,8,128]{2,1,0:T(8,128)S(1)} %get-tuple-element.59.inverse, f32[16,192,128]{2,1,0:T(8,128)S(1)} %copy-done.27, bf16[16,96,128]{2,1,0:T(8,128)(2,1)} %collective-permute-done.11.mixed.rest_0_, ...), custom_call_target="tpu_custom_call" | custom-call | flops 3000000000 | bytes 9000000 | tf_op jit(solution)/shard_map/aggregate/pallas_call | solution.py:536
  96.0 1.6 collective-permute-start.18
  98.1 2.3 turn_weights.2
  100.5 6.1 %collective-permute-done.18.rest_2_ = bf16[16,96,128]{2,1,0:T(8,128)(2,1)S(1)} collective-permute-done((bf16[16,96,128]{2,1,0:T(8,128)(2,1)S(1)}, bf16[16,96,128]{2,1,0:T(8,128)(2,1)S(1)}, u32[]{:S(2)}, u32[]{:S(2)}) %collective-permute-start.18) | collective-permute-done | bytes 393248 | tf_op jit(solution)/shard_map/ppermute | solution.py:56
  108.3 1.5 update.7.source.own.rest_0_
  111.1 4.6 %collective-permute-start.20 = (bf16[16,192,128]{2,1,0:T(8,128)(2,1)}, bf16[16,192,128]{2,1,0:T(8,128)(2,1)S(1)}, u32[]{:S(2)}, u32[]{:S(2)}) collective-permute-start(bf16[16,192,128]{2,1,0:T(8,128)(2,1)} %update.7.source.own.rest_0_), channel_id=1, source_target_pairs={{0,8},{4,12},{8,16},{12,20},{16,24},{20,28},{1,9},{5,13},{9,17},{1... | collective-permute-start | bytes 2359304 | tf_op jit(solution)/shard_map/ppermute | solution.py:665
  117.0 1.4 collective-permute-start.22
  118.4 9.3 %collective-permute-done.22.rest_3_ = bf16[8,192,128]{2,1,0:T(8,128)(2,1)S(1)} collective-permute-done((bf16[8,192,128]{2,1,0:T(8,128)(2,1)S(1)}, bf16[8,192,128]{2,1,0:T(8,128)(2,1)S(1)}, u32[]{:S(2)}, u32[]{:S(2)}) %collective-permute-start.22) | collective-permute-done | bytes 393248 | tf_op jit(solution)/shard_map/ppermute | solution.py:51
  128.4 3.1 collective-permute-done.21.above.rest_2_
  132.8 2.5 near.4
  136.0 1.6 collective-permute-start.23
  137.8 3.3 %collective-permute-start.24 = (bf16[16,96,128]{2,1,0:T(8,128)(2,1)}, bf16[16,96,128]{2,1,0:T(8,128)(2,1)}, u32[]{:S(2)}, u32[]{:S(2)}) collective-permute-start(bf16[16,96,128]{2,1,0:T(8,128)(2,1)} %get-tuple-element.75), channel_id=1, source_target_pairs={{0,24},{4,28},{24,0},{28,4},{8,16},{12,20},{16,8},{20,12},{1,25},{... | collective-permute-start | bytes 1179656 | tf_op jit(solution)/shard_map/ppermute | solution.py:665
  144.3 2.2 collective-permute-done.23.rest_4_
  146.5 2.8 copy-done.10
  150.3 7.1 %sum_early.4.early = f32[16,192,128]{2,1,0:T(8,128)S(1)} custom-call(s32[609]{0:T(1024)S(1)} %copy-done.6, bf16[192,128,128]{2,1,0:T(8,128)(2,1)S(1)} %copy-done.10, bf16[16,192,128]{2,1,0:T(8,128)(2,1)} %update.7.source.own.rest_0_, bf16[16,192,128]{2,1,0:T(8,128)(2,1)S(1)} %collective-permute-done.20.below.rest_1_, ...), custom_call_target="tpu_custom_call" | custom-call | flops 6000000000 | bytes 18000000 | tf_op jit(solution)/shard_map/sum_early/pallas_call | solution.py:536
  158.6 1.9 copy-done.15
  161.3 5.7 %collective-permute-done.25.onward.rest_1_ = bf16[16,96,128]{2,1,0:T(8,128)(2,1)} collective-permute-done((bf16[16,96,128]{2,1,0:T(8,128)(2,1)}, bf16[16,96,128]{2,1,0:T(8,128)(2,1)}, u32[]{:S(2)}, u32[]{:S(2)}) %collective-permute-start.25) | collective-permute-done | bytes 393248 | tf_op jit(solution)/shard_map/ppermute | solution.py:665
  169.4 6.0 %collective-permute-done.28.onward.rest_1_ = bf16[16,96,128]{2,1,0:T(8,128)(2,1)} collective-permute-done((bf16[16,96,128]{2,1,0:T(8,128)(2,1)}, bf16[16,96,128]{2,1,0:T(8,128)(2,1)}, u32[]{:S(2)}, u32[]{:S(2)}) %collective-permute-start.28) | collective-permute-done | bytes 393248 | tf_op jit(solution)/shard_map/ppermute | solution.py:665
  177.6 1.8 collective-permute-done.26.rest_2_
  179.4 2.8 copy-done.11
  182.1 3.4 %aggregate.8.rest_0_ = bf16[16,96,128]{2,1,0:T(8,128)(2,1)S(1)} custom-call(s32[609]{0:T(1024)S(1)} %copy-done.6, bf16[192,128,128]{2,1,0:T(8,128)(2,1)S(1)} %copy-done.11, f32[16,8,128]{2,1,0:T(8,128)S(1)} %get-tuple-element.59.inverse, f32[16,192,128]{2,1,0:T(8,128)S(1)} %copy-done.31, bf16[16,96,128]{2,1,0:T(8,128)(2,1)} %collective-permute-done.24.mixed.rest_0_, ...), custom_call_target="tpu_custom_call" | custom-call | flops 3000000000 | bytes 9000000 | tf_op jit(solution)/shard_map/aggregate/pallas_call | solution.py:536
  185.5 1.6 collective-permute-start.30
  187.7 3.3 %aggregate.9.rest_0_ = bf16[16,96,128]{2,1,0:T(8,128)(2,1)S(1)} custom-call(s32[609]{0:T(1024)S(1)} %copy-done.6, bf16[192,128,128]{2,1,0:T(8,128)(2,1)S(1)} %copy-done.11, f32[16,8,128]{2,1,0:T(8,128)S(1)} %get-tuple-element.59.inverse, f32[16,192,128]{2,1,0:T(8,128)S(1)} %copy-done.31, bf16[16,96,128]{2,1,0:T(8,128)(2,1)S(1)} %collective-permute-done.27.mixed.rest_0_, ...), custom_call_target="tpu_custom_call" | custom-call | flops 3000000000 | bytes 9000000 | tf_op jit(solution)/shard_map/aggregate/pallas_call | solution.py:536
  191.0 1.6 collective-permute-start.34
  192.6 5.1 %collective-permute-done.30.rest_2_ = bf16[16,96,128]{2,1,0:T(8,128)(2,1)S(1)} collective-permute-done((bf16[16,96,128]{2,1,0:T(8,128)(2,1)S(1)}, bf16[16,96,128]{2,1,0:T(8,128)(2,1)S(1)}, u32[]{:S(2)}, u32[]{:S(2)}) %collective-permute-start.30) | collective-permute-done | bytes 393248 | tf_op jit(solution)/shard_map/ppermute | solution.py:56
  198.2 5.9 %collective-permute-done.34.rest_2_ = bf16[16,96,128]{2,1,0:T(8,128)(2,1)S(1)} collective-permute-done((bf16[16,96,128]{2,1,0:T(8,128)(2,1)S(1)}, bf16[16,96,128]{2,1,0:T(8,128)(2,1)S(1)}, u32[]{:S(2)}, u32[]{:S(2)}) %collective-permute-start.34) | collective-permute-done | bytes 393248 | tf_op jit(solution)/shard_map/ppermute | solution.py:56
  205.8 1.5 update.9.source.own.rest_0_
  208.6 4.6 %collective-permute-start.36 = (bf16[16,192,128]{2,1,0:T(8,128)(2,1)}, bf16[16,192,128]{2,1,0:T(8,128)(2,1)S(1)}, u32[]{:S(2)}, u32[]{:S(2)}) collective-permute-start(bf16[16,192,128]{2,1,0:T(8,128)(2,1)} %update.9.source.own.rest_0_), channel_id=1, source_target_pairs={{0,8},{4,12},{8,16},{12,20},{16,24},{20,28},{1,9},{5,13},{9,17},{1... | collective-permute-start | bytes 2359304 | tf_op jit(solution)/shard_map/ppermute | solution.py:665
  214.5 10.5 %collective-permute-done.38.rest_3_ = bf16[8,192,128]{2,1,0:T(8,128)(2,1)S(1)} collective-permute-done((bf16[8,192,128]{2,1,0:T(8,128)(2,1)S(1)}, bf16[8,192,128]{2,1,0:T(8,128)(2,1)S(1)}, u32[]{:S(2)}, u32[]{:S(2)}) %collective-permute-start.38) | collective-permute-done | bytes 393248 | tf_op jit(solution)/shard_map/ppermute | solution.py:51
  225.8 3.2 %collective-permute-done.37.above.rest_2_ = bf16[16,192,128]{2,1,0:T(8,128)(2,1)S(1)} collective-permute-done((bf16[16,192,128]{2,1,0:T(8,128)(2,1)}, bf16[16,192,128]{2,1,0:T(8,128)(2,1)S(1)}, u32[]{:S(2)}, u32[]{:S(2)}) %collective-permute-start.37) | collective-permute-done | bytes 786464 | tf_op jit(solution)/shard_map/ppermute | solution.py:665
  230.2 2.6 near.5
  233.7 3.8 %collective-permute-start.40 = (bf16[16,96,128]{2,1,0:T(8,128)(2,1)}, bf16[16,96,128]{2,1,0:T(8,128)(2,1)}, u32[]{:S(2)}, u32[]{:S(2)}) collective-permute-start(bf16[16,96,128]{2,1,0:T(8,128)(2,1)} %get-tuple-element.89), channel_id=1, source_target_pairs={{0,24},{4,28},{24,0},{28,4},{8,16},{12,20},{16,8},{20,12},{1,25},{... | collective-permute-start | bytes 1179656 | tf_op jit(solution)/shard_map/ppermute | solution.py:665
  240.3 2.9 collective-permute-done.39.rest_4_
  243.2 2.8 copy-done.12
  247.0 7.0 %sum_early.5.early = f32[16,192,128]{2,1,0:T(8,128)S(1)} custom-call(s32[609]{0:T(1024)S(1)} %copy-done.6, bf16[192,128,128]{2,1,0:T(8,128)(2,1)S(1)} %copy-done.12, bf16[16,192,128]{2,1,0:T(8,128)(2,1)} %update.9.source.own.rest_0_, bf16[16,192,128]{2,1,0:T(8,128)(2,1)S(1)} %collective-permute-done.36.below.rest_1_, ...), custom_call_target="tpu_custom_call" | custom-call | flops 6000000000 | bytes 18000000 | tf_op jit(solution)/shard_map/sum_early/pallas_call | solution.py:536
  255.1 1.9 copy-done.16
  257.8 5.5 %collective-permute-done.41.onward.rest_1_ = bf16[16,96,128]{2,1,0:T(8,128)(2,1)} collective-permute-done((bf16[16,96,128]{2,1,0:T(8,128)(2,1)}, bf16[16,96,128]{2,1,0:T(8,128)(2,1)}, u32[]{:S(2)}, u32[]{:S(2)}) %collective-permute-start.41) | collective-permute-done | bytes 393248 | tf_op jit(solution)/shard_map/ppermute | solution.py:665
  265.7 5.9 %collective-permute-done.44.onward.rest_1_ = bf16[16,96,128]{2,1,0:T(8,128)(2,1)S(1)} collective-permute-done((bf16[16,96,128]{2,1,0:T(8,128)(2,1)}, bf16[16,96,128]{2,1,0:T(8,128)(2,1)S(1)}, u32[]{:S(2)}, u32[]{:S(2)}) %collective-permute-start.44) | collective-permute-done | bytes 393248 | tf_op jit(solution)/shard_map/ppermute | solution.py:665
  273.3 2.8 collective-permute-done.42.rest_2_
  276.1 2.8 copy-done.13
  278.9 3.4 %aggregate.10.rest_0_ = bf16[16,96,128]{2,1,0:T(8,128)(2,1)S(1)} custom-call(s32[609]{0:T(1024)S(1)} %copy-done.6, bf16[192,128,128]{2,1,0:T(8,128)(2,1)S(1)} %copy-done.13, f32[16,8,128]{2,1,0:T(8,128)S(1)} %get-tuple-element.59.inverse, f32[16,192,128]{2,1,0:T(8,128)S(1)} %copy-done.29, bf16[16,96,128]{2,1,0:T(8,128)(2,1)} %collective-permute-done.40.mixed.rest_0_, ...), custom_call_target="tpu_custom_call" | custom-call | flops 3000000000 | bytes 9000000 | tf_op jit(solution)/shard_map/aggregate/pallas_call | solution.py:536
  282.3 1.6 collective-permute-start.46
  284.0 2.9 aggregate.11.rest_0_
  286.8 1.6 collective-permute-start.50
  288.4 6.0 %collective-permute-done.46.rest_2_ = bf16[16,96,128]{2,1,0:T(8,128)(2,1)S(1)} collective-permute-done((bf16[16,96,128]{2,1,0:T(8,128)(2,1)S(1)}, bf16[16,96,128]{2,1,0:T(8,128)(2,1)S(1)}, u32[]{:S(2)}, u32[]{:S(2)}) %collective-permute-start.46) | collective-permute-done | bytes 393248 | tf_op jit(solution)/shard_map/ppermute | solution.py:56
  295.0 5.4 %collective-permute-done.50.rest_2_ = bf16[16,96,128]{2,1,0:T(8,128)(2,1)S(1)} collective-permute-done((bf16[16,96,128]{2,1,0:T(8,128)(2,1)S(1)}, bf16[16,96,128]{2,1,0:T(8,128)(2,1)S(1)}, u32[]{:S(2)}, u32[]{:S(2)}) %collective-permute-start.50) | collective-permute-done | bytes 393248 | tf_op jit(solution)/shard_map/ppermute | solution.py:56
  (172 shorter events, 60.9 us)
Async XLA Ops:
  6.5 65.0 %all-gather.4.cloned.1.call-start = ((), (), s32[]{:S(2)}) async-start(), calls=%async_computation | async-start | bytes 3932160 | tf_op jit(solution)/shard_map/all_gather | solution.py:714
  8.8 149.9 %all-gather.6.cloned.1.call-start = ((), (), s32[]{:S(2)}) async-start(), calls=%async_computation.1 | async-start | bytes 3932160 | tf_op jit(solution)/shard_map/all_gather | solution.py:714
  9.0 13.7 %collective-permute-start.2 = (s32[1,8,9]{2,1,0:T(8,128)S(1)}, s32[1,8,9]{2,1,0:T(8,128)S(1)}, u32[]{:S(2)}, u32[]{:S(2)}) collective-permute-start(s32[1,8,9]{2,1,0:T(8,128)S(1)} %pad_add_fusion.1), channel_id=1, source_target_pairs={{0,24},{4,28},{8,0},{12,4},{16,8},{20,12},{24,16},{28,20},{1,25},{... | collective-permute-start | bytes 872 | tf_op jit(solution)/shard_map/ppermute | solution.py:46
  14.1 8.7 %collective-permute-start.1 = (s32[1,8,9]{2,1,0:T(8,128)S(1)}, s32[1,8,9]{2,1,0:T(8,128)S(1)}, u32[]{:S(2)}, u32[]{:S(2)}) collective-permute-start(s32[1,8,9]{2,1,0:T(8,128)S(1)} %pad_add_fusion.1), channel_id=1, source_target_pairs={{0,16},{4,20},{8,24},{12,28},{16,0},{20,4},{24,8},{28,12},{1,17},{... | collective-permute-start | bytes 872 | tf_op jit(solution)/shard_map/ppermute | solution.py:46
  14.1 8.7 %collective-permute-start = (s32[1,8,9]{2,1,0:T(8,128)S(1)}, s32[1,8,9]{2,1,0:T(8,128)S(1)}, u32[]{:S(2)}, u32[]{:S(2)}) collective-permute-start(s32[1,8,9]{2,1,0:T(8,128)S(1)} %pad_add_fusion.1), channel_id=1, source_target_pairs={{0,8},{4,12},{8,16},{12,20},{16,24},{20,28},{24,0},{28,4},{1,9},{5... | collective-permute-start | bytes 872 | tf_op jit(solution)/shard_map/ppermute | solution.py:46
  15.1 23.4 %collective-permute-start.4 = (bf16[16,192,128]{2,1,0:T(8,128)(2,1)}, bf16[16,192,128]{2,1,0:T(8,128)(2,1)S(1)}, u32[]{:S(2)}, u32[]{:S(2)}) collective-permute-start(bf16[16,192,128]{2,1,0:T(8,128)(2,1)} %bitcast_bitcast_fusion.source.own.rest_0_), channel_id=1, source_target_pairs={{8,0},{12,4},{16,8},{20,12},{24,16},{28,20},{9,1},{13,5},{17,9},{2... | collective-permute-start | bytes 2359304 | tf_op jit(solution)/shard_map/ppermute | solution.py:665
  16.3 22.1 %collective-permute-start.3 = (bf16[16,192,128]{2,1,0:T(8,128)(2,1)}, bf16[16,192,128]{2,1,0:T(8,128)(2,1)S(1)}, u32[]{:S(2)}, u32[]{:S(2)}) collective-permute-start(bf16[16,192,128]{2,1,0:T(8,128)(2,1)} %bitcast_bitcast_fusion.source.own.rest_0_), channel_id=1, source_target_pairs={{0,8},{4,12},{8,16},{12,20},{16,24},{20,28},{1,9},{5,13},{9,17},{1... | collective-permute-start | bytes 2359304 | tf_op jit(solution)/shard_map/ppermute | solution.py:665
  22.8 3.1 %copy-start.5 = (bf16[16,192,128]{2,1,0:T(8,128)(2,1)S(1)}, bf16[16,192,128]{2,1,0:T(8,128)(2,1)}, u32[]{:S(2)}) copy-start(bf16[16,192,128]{2,1,0:T(8,128)(2,1)} %bitcast_bitcast_fusion.source.own.rest_0_) | copy-start | bytes 2359300
  22.8 5.1 %collective-permute-start.6 = (s32[4,8,9]{2,1,0:T(8,128)S(1)}, s32[4,8,9]{2,1,0:T(8,128)S(1)}, u32[]{:S(2)}, u32[]{:S(2)}) collective-permute-start(s32[4,8,9]{2,1,0:T(8,128)S(1)} %pad_add_fusion.mine), channel_id=1, source_target_pairs={{0,4},{4,0},{8,12},{12,8},{16,20},{20,16},{24,28},{28,24},{1,5},{5... | collective-permute-start | bytes 3464 | tf_op jit(solution)/shard_map/ppermute | solution.py:51
  27.3 11.1 %collective-permute-start.5 = (bf16[8,192,128]{2,1,0:T(8,128)(2,1)S(1)}, bf16[8,192,128]{2,1,0:T(8,128)(2,1)S(1)}, u32[]{:S(2)}, u32[]{:S(2)}) collective-permute-start(bf16[8,192,128]{2,1,0:T(8,128)(2,1)S(1)} %pick.3), channel_id=1, source_target_pairs={{0,4},{4,0},{8,12},{12,8},{16,20},{20,16},{24,28},{28,24},{1,5},{5... | collective-permute-start | bytes 1179656 | tf_op jit(solution)/shard_map/ppermute | solution.py:51
  38.4 11.6 %copy-start.6 = (s32[609]{0:T(1024)S(1)}, s32[609]{0:T(1024)}, u32[]{:S(2)}) copy-start(s32[609]{0:T(1024)} %plan.1.index) | copy-start | bytes 7312
  41.8 16.8 %collective-permute-start.7 = (bf16[8,192,128]{2,1,0:T(8,128)(2,1)}, bf16[8,192,128]{2,1,0:T(8,128)(2,1)}, u32[]{:S(2)}, u32[]{:S(2)}) collective-permute-start(bf16[8,192,128]{2,1,0:T(8,128)(2,1)} %get-tuple-element.54), channel_id=1, source_target_pairs={{0,4},{4,0},{8,12},{12,8},{16,20},{20,16},{24,28},{28,24},{1,5},{5... | collective-permute-start | bytes 1179656 | tf_op jit(solution)/shard_map/ppermute | solution.py:51
  43.5 30.8 %collective-permute-start.8 = (bf16[16,96,128]{2,1,0:T(8,128)(2,1)}, bf16[16,96,128]{2,1,0:T(8,128)(2,1)}, u32[]{:S(2)}, u32[]{:S(2)}) collective-permute-start(bf16[16,96,128]{2,1,0:T(8,128)(2,1)} %copy-done.18), channel_id=1, source_target_pairs={{0,24},{4,28},{24,0},{28,4},{8,16},{12,20},{16,8},{20,12},{1,25},{... | collective-permute-start | bytes 1179656 | tf_op jit(solution)/shard_map/ppermute | solution.py:665
  46.8 27.5 %collective-permute-start.9 = (bf16[16,96,128]{2,1,0:T(8,128)(2,1)}, bf16[16,96,128]{2,1,0:T(8,128)(2,1)}, u32[]{:S(2)}, u32[]{:S(2)}) collective-permute-start(bf16[16,96,128]{2,1,0:T(8,128)(2,1)} %copy-done.17), channel_id=1, source_target_pairs={{8,0},{12,4},{16,24},{20,28},{9,1},{13,5},{17,25},{21,29},{10,2},{... | collective-permute-start | bytes 1179656 | tf_op jit(solution)/shard_map/ppermute | solution.py:665
  48.1 27.7 %collective-permute-start.11 = (bf16[16,96,128]{2,1,0:T(8,128)(2,1)}, bf16[16,96,128]{2,1,0:T(8,128)(2,1)}, u32[]{:S(2)}, u32[]{:S(2)}) collective-permute-start(bf16[16,96,128]{2,1,0:T(8,128)(2,1)} %get-tuple-element.65), channel_id=1, source_target_pairs={{0,24},{4,28},{24,0},{28,4},{8,16},{12,20},{16,8},{20,12},{1,25},{... | collective-permute-start | bytes 1179656 | tf_op jit(solution)/shard_map/ppermute | solution.py:665
  48.7 31.1 %collective-permute-start.12 = (bf16[16,96,128]{2,1,0:T(8,128)(2,1)S(1)}, bf16[16,96,128]{2,1,0:T(8,128)(2,1)}, u32[]{:S(2)}, u32[]{:S(2)}) collective-permute-start(bf16[16,96,128]{2,1,0:T(8,128)(2,1)S(1)} %get-tuple-element.66), channel_id=1, source_target_pairs={{8,0},{12,4},{16,24},{20,28},{9,1},{13,5},{17,25},{21,29},{10,2},{... | collective-permute-start | bytes 1179656 | tf_op jit(solution)/shard_map/ppermute | solution.py:665
  52.8 5.8 %copy-start.3 = (bf16[3,768,768]{2,1,0:T(8,128)(2,1)S(1)}, bf16[3,768,768]{2,1,0:T(8,128)(2,1)}, u32[]{:S(2)}) copy-start(bf16[3,768,768]{2,1,0:T(8,128)(2,1)} %w.1) | copy-start | bytes 10616836
  52.8 5.8 %copy-start.7 = (s32[2]{0:T(128)S(1)}, s32[2]{0:T(128)}, u32[]{:S(2)}) copy-start(s32[2]{0:T(128)} %pad_add_fusion.2.spot) | copy-start | bytes 28
  73.5 10.7 %copy-start.27 = (f32[16,192,128]{2,1,0:T(8,128)S(1)}, f32[16,192,128]{2,1,0:T(8,128)}, u32[]{:S(2)}) copy-start(f32[16,192,128]{2,1,0:T(8,128)} %copy-done.26) | copy-start | bytes 4718596
  74.3 9.9 %copy-start.9 = (bf16[192,128,128]{2,1,0:T(8,128)(2,1)S(1)}, bf16[192,128,128]{2,1,0:T(8,128)(2,1)}, u32[]{:S(2)}) copy-start(bf16[192,128,128]{2,1,0:T(8,128)(2,1)} %copy-done.8) | copy-start | bytes 18874372
  75.7 8.5 %collective-permute-start.10 = (bf16[16,96,128]{2,1,0:T(8,128)(2,1)S(1)}, bf16[16,96,128]{2,1,0:T(8,128)(2,1)S(1)}, u32[]{:S(2)}, u32[]{:S(2)}) collective-permute-start(bf16[16,96,128]{2,1,0:T(8,128)(2,1)S(1)} %far.6), channel_id=1, source_target_pairs={{0,4},{4,0},{8,12},{12,8},{16,20},{20,16},{24,28},{28,24},{1,5},{5... | collective-permute-start | bytes 1179656 | tf_op jit(solution)/shard_map/ppermute | solution.py:51
  81.1 11.4 %collective-permute-start.16 = (bf16[16,96,128]{2,1,0:T(8,128)(2,1)S(1)}, bf16[16,96,128]{2,1,0:T(8,128)(2,1)S(1)}, u32[]{:S(2)}, u32[]{:S(2)}) collective-permute-start(bf16[16,96,128]{2,1,0:T(8,128)(2,1)S(1)} %far.7), channel_id=1, source_target_pairs={{0,4},{4,0},{8,12},{12,8},{16,20},{20,16},{24,28},{28,24},{1,5},{5... | collective-permute-start | bytes 1179656 | tf_op jit(solution)/shard_map/ppermute | solution.py:51
  87.6 9.9 %collective-permute-start.14 = (bf16[16,96,128]{2,1,0:T(8,128)(2,1)S(1)}, bf16[16,96,128]{2,1,0:T(8,128)(2,1)S(1)}, u32[]{:S(2)}, u32[]{:S(2)}) collective-permute-start(bf16[16,96,128]{2,1,0:T(8,128)(2,1)S(1)} %aggregate.6.rest_0_), channel_id=1, source_target_pairs={{0,2},{1,3},{2,0},{3,1},{4,6},{5,7},{6,4},{7,5},{8,10},{9,11},{10,... | collective-permute-start | bytes 1179656 | tf_op jit(solution)/shard_map/ppermute | solution.py:56
  92.4 5.7 %copy-start.4 = (bf16[3,768,768]{2,1,0:T(8,128)(2,1)S(1)}, bf16[3,768,768]{2,1,0:T(8,128)(2,1)}, u32[]{:S(2)}) copy-start(bf16[3,768,768]{2,1,0:T(8,128)(2,1)} %w) | copy-start | bytes 10616836
  96.0 10.5 %collective-permute-start.18 = (bf16[16,96,128]{2,1,0:T(8,128)(2,1)S(1)}, bf16[16,96,128]{2,1,0:T(8,128)(2,1)S(1)}, u32[]{:S(2)}, u32[]{:S(2)}) collective-permute-start(bf16[16,96,128]{2,1,0:T(8,128)(2,1)S(1)} %aggregate.7.rest_0_), channel_id=1, source_target_pairs={{0,2},{1,3},{2,0},{3,1},{4,6},{5,7},{6,4},{7,5},{8,10},{9,11},{10,... | collective-permute-start | bytes 1179656 | tf_op jit(solution)/shard_map/ppermute | solution.py:56
  97.6 9.0 %collective-permute-start.13 = (bf16[16,96,128]{2,1,0:T(8,128)(2,1)S(1)}, bf16[16,96,128]{2,1,0:T(8,128)(2,1)S(1)}, u32[]{:S(2)}, u32[]{:S(2)}) collective-permute-start(bf16[16,96,128]{2,1,0:T(8,128)(2,1)S(1)} %aggregate.6.rest_0_), channel_id=1, source_target_pairs={{0,1},{1,0},{2,3},{3,2},{4,5},{5,4},{6,7},{7,6},{8,9},{9,8},{10,11... | collective-permute-start | bytes 1179656 | tf_op jit(solution)/shard_map/ppermute | solution.py:56
  97.6 9.0 %collective-permute-start.15 = (bf16[16,96,128]{2,1,0:T(8,128)(2,1)S(1)}, bf16[16,96,128]{2,1,0:T(8,128)(2,1)S(1)}, u32[]{:S(2)}, u32[]{:S(2)}) collective-permute-start(bf16[16,96,128]{2,1,0:T(8,128)(2,1)S(1)} %collective-permute-done.14.rest_2_), channel_id=1, source_target_pairs={{0,1},{1,0},{2,3},{3,2},{4,5},{5,4},{6,7},{7,6},{8,9},{9,8},{10,11... | collective-permute-start | bytes 1179656 | tf_op jit(solution)/shard_map/ppermute | solution.py:56
  100.4 6.9 %collective-permute-start.17 = (bf16[16,96,128]{2,1,0:T(8,128)(2,1)S(1)}, bf16[16,96,128]{2,1,0:T(8,128)(2,1)S(1)}, u32[]{:S(2)}, u32[]{:S(2)}) collective-permute-start(bf16[16,96,128]{2,1,0:T(8,128)(2,1)S(1)} %aggregate.7.rest_0_), channel_id=1, source_target_pairs={{0,1},{1,0},{2,3},{3,2},{4,5},{5,4},{6,7},{7,6},{8,9},{9,8},{10,11... | collective-permute-start | bytes 1179656 | tf_op jit(solution)/shard_map/ppermute | solution.py:56
  106.6 1.7 collective-permute-start.19
  109.8 145.3 %all-gather.8.cloned.1.call-start = ((), (), s32[]{:S(2)}) async-start(), calls=%async_computation.2 | async-start | bytes 3932160 | tf_op jit(solution)/shard_map/all_gather | solution.py:714
  109.8 21.7 %collective-permute-start.21 = (bf16[16,192,128]{2,1,0:T(8,128)(2,1)}, bf16[16,192,128]{2,1,0:T(8,128)(2,1)S(1)}, u32[]{:S(2)}, u32[]{:S(2)}) collective-permute-start(bf16[16,192,128]{2,1,0:T(8,128)(2,1)} %update.7.source.own.rest_0_), channel_id=1, source_target_pairs={{8,0},{12,4},{16,8},{20,12},{24,16},{28,20},{9,1},{13,5},{17,9},{2... | collective-permute-start | bytes 2359304 | tf_op jit(solution)/shard_map/ppermute | solution.py:665
  111.1 21.7 %collective-permute-start.20 = (bf16[16,192,128]{2,1,0:T(8,128)(2,1)}, bf16[16,192,128]{2,1,0:T(8,128)(2,1)S(1)}, u32[]{:S(2)}, u32[]{:S(2)}) collective-permute-start(bf16[16,192,128]{2,1,0:T(8,128)(2,1)} %update.7.source.own.rest_0_), channel_id=1, source_target_pairs={{0,8},{4,12},{8,16},{12,20},{16,24},{20,28},{1,9},{5,13},{9,17},{1... | collective-permute-start | bytes 2359304 | tf_op jit(solution)/shard_map/ppermute | solution.py:665
  117.0 10.7 %collective-permute-start.22 = (bf16[8,192,128]{2,1,0:T(8,128)(2,1)S(1)}, bf16[8,192,128]{2,1,0:T(8,128)(2,1)S(1)}, u32[]{:S(2)}, u32[]{:S(2)}) collective-permute-start(bf16[8,192,128]{2,1,0:T(8,128)(2,1)S(1)} %pick.4), channel_id=1, source_target_pairs={{0,4},{4,0},{8,12},{12,8},{16,20},{20,16},{24,28},{28,24},{1,5},{5... | collective-permute-start | bytes 1179656 | tf_op jit(solution)/shard_map/ppermute | solution.py:51
  136.0 10.5 %collective-permute-start.23 = (bf16[8,192,128]{2,1,0:T(8,128)(2,1)}, bf16[8,192,128]{2,1,0:T(8,128)(2,1)}, u32[]{:S(2)}, u32[]{:S(2)}) collective-permute-start(bf16[8,192,128]{2,1,0:T(8,128)(2,1)} %get-tuple-element.74), channel_id=1, source_target_pairs={{0,4},{4,0},{8,12},{12,8},{16,20},{20,16},{24,28},{28,24},{1,5},{5... | collective-permute-start | bytes 1179656 | tf_op jit(solution)/shard_map/ppermute | solution.py:51
  137.8 23.5 %collective-permute-start.24 = (bf16[16,96,128]{2,1,0:T(8,128)(2,1)}, bf16[16,96,128]{2,1,0:T(8,128)(2,1)}, u32[]{:S(2)}, u32[]{:S(2)}) collective-permute-start(bf16[16,96,128]{2,1,0:T(8,128)(2,1)} %get-tuple-element.75), channel_id=1, source_target_pairs={{0,24},{4,28},{24,0},{28,4},{8,16},{12,20},{16,8},{20,12},{1,25},{... | collective-permute-start | bytes 1179656 | tf_op jit(solution)/shard_map/ppermute | solution.py:665
  141.1 25.9 %collective-permute-start.25 = (bf16[16,96,128]{2,1,0:T(8,128)(2,1)}, bf16[16,96,128]{2,1,0:T(8,128)(2,1)}, u32[]{:S(2)}, u32[]{:S(2)}) collective-permute-start(bf16[16,96,128]{2,1,0:T(8,128)(2,1)} %get-tuple-element.76), channel_id=1, source_target_pairs={{8,0},{12,4},{16,24},{20,28},{9,1},{13,5},{17,25},{21,29},{10,2},{... | collective-permute-start | bytes 1179656 | tf_op jit(solution)/shard_map/ppermute | solution.py:665
  142.4 27.0 %collective-permute-start.27 = (bf16[16,96,128]{2,1,0:T(8,128)(2,1)}, bf16[16,96,128]{2,1,0:T(8,128)(2,1)S(1)}, u32[]{:S(2)}, u32[]{:S(2)}) collective-permute-start(bf16[16,96,128]{2,1,0:T(8,128)(2,1)} %copy-done.21), channel_id=1, source_target_pairs={{0,24},{4,28},{24,0},{28,4},{8,16},{12,20},{16,8},{20,12},{1,25},{... | collective-permute-start | bytes 1179656 | tf_op jit(solution)/shard_map/ppermute | solution.py:665
  143.0 32.3 %collective-permute-start.28 = (bf16[16,96,128]{2,1,0:T(8,128)(2,1)}, bf16[16,96,128]{2,1,0:T(8,128)(2,1)}, u32[]{:S(2)}, u32[]{:S(2)}) collective-permute-start(bf16[16,96,128]{2,1,0:T(8,128)(2,1)} %copy-done.20), channel_id=1, source_target_pairs={{8,0},{12,4},{16,24},{20,28},{9,1},{13,5},{17,25},{21,29},{10,2},{... | collective-permute-start | bytes 1179656 | tf_op jit(solution)/shard_map/ppermute | solution.py:665
  168.3 11.1 %copy-start.31 = (f32[16,192,128]{2,1,0:T(8,128)S(1)}, f32[16,192,128]{2,1,0:T(8,128)}, u32[]{:S(2)}) copy-start(f32[16,192,128]{2,1,0:T(8,128)} %copy-done.30) | copy-start | bytes 4718596
  168.3 11.1 %collective-permute-start.26 = (bf16[16,96,128]{2,1,0:T(8,128)(2,1)S(1)}, bf16[16,96,128]{2,1,0:T(8,128)(2,1)S(1)}, u32[]{:S(2)}, u32[]{:S(2)}) collective-permute-start(bf16[16,96,128]{2,1,0:T(8,128)(2,1)S(1)} %far.8), channel_id=1, source_target_pairs={{0,4},{4,0},{8,12},{12,8},{16,20},{20,16},{24,28},{28,24},{1,5},{5... | collective-permute-start | bytes 1179656 | tf_op jit(solution)/shard_map/ppermute | solution.py:51
  176.5 11.2 %collective-permute-start.32 = (bf16[16,96,128]{2,1,0:T(8,128)(2,1)S(1)}, bf16[16,96,128]{2,1,0:T(8,128)(2,1)S(1)}, u32[]{:S(2)}, u32[]{:S(2)}) collective-permute-start(bf16[16,96,128]{2,1,0:T(8,128)(2,1)S(1)} %far.9), channel_id=1, source_target_pairs={{0,4},{4,0},{8,12},{12,8},{16,20},{20,16},{24,28},{28,24},{1,5},{5... | collective-permute-start | bytes 1179656 | tf_op jit(solution)/shard_map/ppermute | solution.py:51
  185.5 12.1 %collective-permute-start.30 = (bf16[16,96,128]{2,1,0:T(8,128)(2,1)S(1)}, bf16[16,96,128]{2,1,0:T(8,128)(2,1)S(1)}, u32[]{:S(2)}, u32[]{:S(2)}) collective-permute-start(bf16[16,96,128]{2,1,0:T(8,128)(2,1)S(1)} %aggregate.8.rest_0_), channel_id=1, source_target_pairs={{0,2},{1,3},{2,0},{3,1},{4,6},{5,7},{6,4},{7,5},{8,10},{9,11},{10,... | collective-permute-start | bytes 1179656 | tf_op jit(solution)/shard_map/ppermute | solution.py:56
  191.0 13.1 %collective-permute-start.34 = (bf16[16,96,128]{2,1,0:T(8,128)(2,1)S(1)}, bf16[16,96,128]{2,1,0:T(8,128)(2,1)S(1)}, u32[]{:S(2)}, u32[]{:S(2)}) collective-permute-start(bf16[16,96,128]{2,1,0:T(8,128)(2,1)S(1)} %aggregate.9.rest_0_), channel_id=1, source_target_pairs={{0,2},{1,3},{2,0},{3,1},{4,6},{5,7},{6,4},{7,5},{8,10},{9,11},{10,... | collective-permute-start | bytes 1179656 | tf_op jit(solution)/shard_map/ppermute | solution.py:56
  192.6 11.5 %collective-permute-start.29 = (bf16[16,96,128]{2,1,0:T(8,128)(2,1)S(1)}, bf16[16,96,128]{2,1,0:T(8,128)(2,1)S(1)}, u32[]{:S(2)}, u32[]{:S(2)}) collective-permute-start(bf16[16,96,128]{2,1,0:T(8,128)(2,1)S(1)} %aggregate.8.rest_0_), channel_id=1, source_target_pairs={{0,1},{1,0},{2,3},{3,2},{4,5},{5,4},{6,7},{7,6},{8,9},{9,8},{10,11... | collective-permute-start | bytes 1179656 | tf_op jit(solution)/shard_map/ppermute | solution.py:56
  197.7 6.4 %collective-permute-start.31 = (bf16[16,96,128]{2,1,0:T(8,128)(2,1)S(1)}, bf16[16,96,128]{2,1,0:T(8,128)(2,1)S(1)}, u32[]{:S(2)}, u32[]{:S(2)}) collective-permute-start(bf16[16,96,128]{2,1,0:T(8,128)(2,1)S(1)} %collective-permute-done.30.rest_2_), channel_id=1, source_target_pairs={{0,1},{1,0},{2,3},{3,2},{4,5},{5,4},{6,7},{7,6},{8,9},{9,8},{10,11... | collective-permute-start | bytes 1179656 | tf_op jit(solution)/shard_map/ppermute | solution.py:56
  197.7 7.0 %collective-permute-start.33 = (bf16[16,96,128]{2,1,0:T(8,128)(2,1)S(1)}, bf16[16,96,128]{2,1,0:T(8,128)(2,1)S(1)}, u32[]{:S(2)}, u32[]{:S(2)}) collective-permute-start(bf16[16,96,128]{2,1,0:T(8,128)(2,1)S(1)} %aggregate.9.rest_0_), channel_id=1, source_target_pairs={{0,1},{1,0},{2,3},{3,2},{4,5},{5,4},{6,7},{7,6},{8,9},{9,8},{10,11... | collective-permute-start | bytes 1179656 | tf_op jit(solution)/shard_map/ppermute | solution.py:56
  204.1 1.7 collective-permute-start.35
  207.3 21.7 %collective-permute-start.37 = (bf16[16,192,128]{2,1,0:T(8,128)(2,1)}, bf16[16,192,128]{2,1,0:T(8,128)(2,1)S(1)}, u32[]{:S(2)}, u32[]{:S(2)}) collective-permute-start(bf16[16,192,128]{2,1,0:T(8,128)(2,1)} %update.9.source.own.rest_0_), channel_id=1, source_target_pairs={{8,0},{12,4},{16,8},{20,12},{24,16},{28,20},{9,1},{13,5},{17,9},{2... | collective-permute-start | bytes 2359304 | tf_op jit(solution)/shard_map/ppermute | solution.py:665
  208.6 21.7 %collective-permute-start.36 = (bf16[16,192,128]{2,1,0:T(8,128)(2,1)}, bf16[16,192,128]{2,1,0:T(8,128)(2,1)S(1)}, u32[]{:S(2)}, u32[]{:S(2)}) collective-permute-start(bf16[16,192,128]{2,1,0:T(8,128)(2,1)} %update.9.source.own.rest_0_), channel_id=1, source_target_pairs={{0,8},{4,12},{8,16},{12,20},{16,24},{20,28},{1,9},{5,13},{9,17},{1... | collective-permute-start | bytes 2359304 | tf_op jit(solution)/shard_map/ppermute | solution.py:665
  214.5 10.6 %collective-permute-start.38 = (bf16[8,192,128]{2,1,0:T(8,128)(2,1)S(1)}, bf16[8,192,128]{2,1,0:T(8,128)(2,1)S(1)}, u32[]{:S(2)}, u32[]{:S(2)}) collective-permute-start(bf16[8,192,128]{2,1,0:T(8,128)(2,1)S(1)} %pick.5), channel_id=1, source_target_pairs={{0,4},{4,0},{8,12},{12,8},{16,20},{20,16},{24,28},{28,24},{1,5},{5... | collective-permute-start | bytes 1179656 | tf_op jit(solution)/shard_map/ppermute | solution.py:51
  232.9 10.3 %collective-permute-start.39 = (bf16[8,192,128]{2,1,0:T(8,128)(2,1)}, bf16[8,192,128]{2,1,0:T(8,128)(2,1)}, u32[]{:S(2)}, u32[]{:S(2)}) collective-permute-start(bf16[8,192,128]{2,1,0:T(8,128)(2,1)} %get-tuple-element.88), channel_id=1, source_target_pairs={{0,4},{4,0},{8,12},{12,8},{16,20},{20,16},{24,28},{28,24},{1,5},{5... | collective-permute-start | bytes 1179656 | tf_op jit(solution)/shard_map/ppermute | solution.py:51
  233.7 24.0 %collective-permute-start.40 = (bf16[16,96,128]{2,1,0:T(8,128)(2,1)}, bf16[16,96,128]{2,1,0:T(8,128)(2,1)}, u32[]{:S(2)}, u32[]{:S(2)}) collective-permute-start(bf16[16,96,128]{2,1,0:T(8,128)(2,1)} %get-tuple-element.89), channel_id=1, source_target_pairs={{0,24},{4,28},{24,0},{28,4},{8,16},{12,20},{16,8},{20,12},{1,25},{... | collective-permute-start | bytes 1179656 | tf_op jit(solution)/shard_map/ppermute | solution.py:665
  237.5 25.8 %collective-permute-start.41 = (bf16[16,96,128]{2,1,0:T(8,128)(2,1)}, bf16[16,96,128]{2,1,0:T(8,128)(2,1)}, u32[]{:S(2)}, u32[]{:S(2)}) collective-permute-start(bf16[16,96,128]{2,1,0:T(8,128)(2,1)} %get-tuple-element.90), channel_id=1, source_target_pairs={{8,0},{12,4},{16,24},{20,28},{9,1},{13,5},{17,25},{21,29},{10,2},{... | collective-permute-start | bytes 1179656 | tf_op jit(solution)/shard_map/ppermute | solution.py:665
  238.8 26.8 %collective-permute-start.43 = (bf16[16,96,128]{2,1,0:T(8,128)(2,1)}, bf16[16,96,128]{2,1,0:T(8,128)(2,1)S(1)}, u32[]{:S(2)}, u32[]{:S(2)}) collective-permute-start(bf16[16,96,128]{2,1,0:T(8,128)(2,1)} %get-tuple-element.93), channel_id=1, source_target_pairs={{0,24},{4,28},{24,0},{28,4},{8,16},{12,20},{16,8},{20,12},{1,25},{... | collective-permute-start | bytes 1179656 | tf_op jit(solution)/shard_map/ppermute | solution.py:665
  239.0 32.6 %collective-permute-start.44 = (bf16[16,96,128]{2,1,0:T(8,128)(2,1)}, bf16[16,96,128]{2,1,0:T(8,128)(2,1)S(1)}, u32[]{:S(2)}, u32[]{:S(2)}) collective-permute-start(bf16[16,96,128]{2,1,0:T(8,128)(2,1)} %copy-done.19), channel_id=1, source_target_pairs={{8,0},{12,4},{16,24},{20,28},{9,1},{13,5},{17,25},{21,29},{10,2},{... | collective-permute-start | bytes 1179656 | tf_op jit(solution)/shard_map/ppermute | solution.py:665
  264.5 11.6 %copy-start.29 = (f32[16,192,128]{2,1,0:T(8,128)S(1)}, f32[16,192,128]{2,1,0:T(8,128)}, u32[]{:S(2)}) copy-start(f32[16,192,128]{2,1,0:T(8,128)} %copy-done.28) | copy-start | bytes 4718596
  264.5 11.6 %collective-permute-start.42 = (bf16[16,96,128]{2,1,0:T(8,128)(2,1)S(1)}, bf16[16,96,128]{2,1,0:T(8,128)(2,1)S(1)}, u32[]{:S(2)}, u32[]{:S(2)}) collective-permute-start(bf16[16,96,128]{2,1,0:T(8,128)(2,1)S(1)} %far.10), channel_id=1, source_target_pairs={{0,4},{4,0},{8,12},{12,8},{16,20},{20,16},{24,28},{28,24},{1,5},{5... | collective-permute-start | bytes 1179656 | tf_op jit(solution)/shard_map/ppermute | solution.py:51
  272.2 11.7 %collective-permute-start.48 = (bf16[16,96,128]{2,1,0:T(8,128)(2,1)S(1)}, bf16[16,96,128]{2,1,0:T(8,128)(2,1)S(1)}, u32[]{:S(2)}, u32[]{:S(2)}) collective-permute-start(bf16[16,96,128]{2,1,0:T(8,128)(2,1)S(1)} %far.11), channel_id=1, source_target_pairs={{0,4},{4,0},{8,12},{12,8},{16,20},{20,16},{24,28},{28,24},{1,5},{5... | collective-permute-start | bytes 1179656 | tf_op jit(solution)/shard_map/ppermute | solution.py:51
  282.3 12.1 %collective-permute-start.46 = (bf16[16,96,128]{2,1,0:T(8,128)(2,1)S(1)}, bf16[16,96,128]{2,1,0:T(8,128)(2,1)S(1)}, u32[]{:S(2)}, u32[]{:S(2)}) collective-permute-start(bf16[16,96,128]{2,1,0:T(8,128)(2,1)S(1)} %aggregate.10.rest_0_), channel_id=1, source_target_pairs={{0,2},{1,3},{2,0},{3,1},{4,6},{5,7},{6,4},{7,5},{8,10},{9,11},{10,... | collective-permute-start | bytes 1179656 | tf_op jit(solution)/shard_map/ppermute | solution.py:56
  286.8 13.5 %collective-permute-start.50 = (bf16[16,96,128]{2,1,0:T(8,128)(2,1)S(1)}, bf16[16,96,128]{2,1,0:T(8,128)(2,1)S(1)}, u32[]{:S(2)}, u32[]{:S(2)}) collective-permute-start(bf16[16,96,128]{2,1,0:T(8,128)(2,1)S(1)} %aggregate.11.rest_0_), channel_id=1, source_target_pairs={{0,2},{1,3},{2,0},{3,1},{4,6},{5,7},{6,4},{7,5},{8,10},{9,11},{10,... | collective-permute-start | bytes 1179656 | tf_op jit(solution)/shard_map/ppermute | solution.py:56
  288.4 11.9 %collective-permute-start.45 = (bf16[16,96,128]{2,1,0:T(8,128)(2,1)S(1)}, bf16[16,96,128]{2,1,0:T(8,128)(2,1)S(1)}, u32[]{:S(2)}, u32[]{:S(2)}) collective-permute-start(bf16[16,96,128]{2,1,0:T(8,128)(2,1)S(1)} %aggregate.10.rest_0_), channel_id=1, source_target_pairs={{0,1},{1,0},{2,3},{3,2},{4,5},{5,4},{6,7},{7,6},{8,9},{9,8},{10,11... | collective-permute-start | bytes 1179656 | tf_op jit(solution)/shard_map/ppermute | solution.py:56
  294.4 5.9 %collective-permute-start.47 = (bf16[16,96,128]{2,1,0:T(8,128)(2,1)S(1)}, bf16[16,96,128]{2,1,0:T(8,128)(2,1)S(1)}, u32[]{:S(2)}, u32[]{:S(2)}) collective-permute-start(bf16[16,96,128]{2,1,0:T(8,128)(2,1)S(1)} %collective-permute-done.46.rest_2_), channel_id=1, source_target_pairs={{0,1},{1,0},{2,3},{3,2},{4,5},{5,4},{6,7},{7,6},{8,9},{9,8},{10,11... | collective-permute-start | bytes 1179656 | tf_op jit(solution)/shard_map/ppermute | solution.py:56
  294.4 6.5 %collective-permute-start.49 = (bf16[16,96,128]{2,1,0:T(8,128)(2,1)S(1)}, bf16[16,96,128]{2,1,0:T(8,128)(2,1)S(1)}, u32[]{:S(2)}, u32[]{:S(2)}) collective-permute-start(bf16[16,96,128]{2,1,0:T(8,128)(2,1)S(1)} %aggregate.11.rest_0_), channel_id=1, source_target_pairs={{0,1},{1,0},{2,3},{3,2},{4,5},{5,4},{6,7},{7,6},{8,9},{9,8},{10,11... | collective-permute-start | bytes 1179656 | tf_op jit(solution)/shard_map/ppermute | solution.py:56
  300.3 1.7 collective-permute-start.51
  (29 other events, 44.8 us)
Sparse Core Ops, SparseCore 0:
  8.9 31.2 all-gather.3
  109.9 28.3 all-gather.5
  207.4 29.1 all-gather.7

commit v4 on v3

--- a/solution.py
+++ b/solution.py
@@ -228,7 +228,7 @@
             kept[4 * t + k] = tiles[4 * t + k]
         return 0
 
-    lax.fori_loop(0, tiles.shape[0] // 4, keep, 0)
+    lax.fori_loop(0, tiles.shape[0] // 4, keep, 0, unroll=4)
 
     def product(at, inside):
         ones = [
@@ -259,7 +259,7 @@
                 held[base + 4 * i + k] = ref[4 * i + k]
             return 0
 
-        lax.fori_loop(0, ref.shape[0] // 4, copy, 0)
+        lax.fori_loop(0, ref.shape[0] // 4, copy, 0, unroll=True)
         base += ref.shape[0]
     held[base] = jnp.zeros(held.shape[1:], held.dtype)
     return base
@@ -332,7 +332,7 @@
         out[s] = source[picks[row, s]]
         return 0
 
-    lax.fori_loop(0, out.shape[0], copy, 0)
+    lax.fori_loop(0, out.shape[0], copy, 0, unroll=True)
 
 
 def near_kernel(picks, own, below, above, x_out, *outs):
@@ -346,7 +346,7 @@
         x_out[s] = jnp.where(layer_here == 0, above[picks[3, s]], below[picks[1, s]])
         return 0
 
-    lax.fori_loop(0, slots, copy, 0)
+    lax.fori_loop(0, slots, copy, 0, unroll=True)
 
     @pl.when((layer_here == 0) | (layer_here == 3))
     def _():
@@ -356,7 +356,7 @@
                 mixed[c][slots + s] = own[picks[5, s], cut]
             return 0
 
-        lax.fori_loop(0, slots, copy, 0)
+        lax.fori_loop(0, slots, copy, 0, unroll=True)
 
     def relay(through, back):
         def copy(i, _):
@@ -366,7 +366,7 @@
                     onward[c][2 * i + k] = back[2 * i + k, cut]
             return 0
 
-        lax.fori_loop(0, blocks // 2, copy, 0)
+        lax.fori_loop(0, blocks // 2, copy, 0, unroll=True)
 
     @pl.when(layer_here == 1)
     def _():
@@ -390,7 +390,7 @@
             out[slots + s] = mixed[s]
             return 0
 
-        lax.fori_loop(0, slots, copy, 0)
+        lax.fori_loop(0, slots, copy, 0, unroll=True)
 
     @pl.when(jnp.logical_not(end))
     def _():
@@ -399,7 +399,7 @@
             out[slots + s] = mixed[picks[2, s]]
             return 0
 
-        lax.fori_loop(0, slots, copy, 0)
+        lax.fori_loop(0, slots, copy, 0, unroll=True)
 
 
 def pair_of(ref, b):

time: 312 us -> 312 us (level)
  Pallas kernels: 87.2 us -> 70.9 us
  waiting for transfers between devices: 102 us -> 115 us
    pallas_call x22, Pallas kernels: 63.6 us -> 49.7 us  [call(): pl.pallas_call(functools.partial(kernel, **static), name=name, in_specs=[...]
    ppermute x18, waiting for transfers between devices: 36 us -> 46.1 us  [send(): return lax.ppermute(x, 'dom', pairs)]
  transfers between devices with their start and end apart: 55 -> 55, of which waited for: 27 -> 30; matrix products, arithmetic and copies ran while one was open for 1% -> 1% of each run, Pallas kernels for 27% -> 22%
where the time goes in v4:
time: 312 us; the launch traced here: 310 us
  waiting for transfers between devices  115 us (37%)
  Pallas kernels  70.9 us (23%)
  starting transfers between devices  70.2 us (22%)
  local copies, waits for them, and re-layouts  37.8 us (12%)
  between operations  14.4 us (5%)
    pallas_call x22, Pallas kernels, call(): pl.pallas_call(functools.partial(kernel, **static), name=name, in_specs=[...  49.7 us
    ppermute x18, waiting for transfers between devices, send(): return lax.ppermute(x, 'dom', pairs)  46.1 us
    ppermute x18, starting transfers between devices, send(): return lax.ppermute(x, 'dom', pairs)  39 us
    ppermute x13, waiting for transfers between devices, from_partner(): return lax.ppermute(x, 'dom', [(i, i ^ 1) for i in range(n)])  37.6 us
    unnamed x76, local copies, waits for them, and re-layouts  34.3 us
    ppermute x18, waiting for transfers between devices, from_feat(): return lax.ppermute(x, 'feat', [(i, i ^ bit) for i in range(n)])  31.6 us
    ppermute x13, starting transfers between devices, from_partner(): return lax.ppermute(x, 'dom', [(i, i ^ 1) for i in range(n)])  14 us
    ppermute x18, starting transfers between devices, from_feat(): return lax.ppermute(x, 'feat', [(i, i ^ bit) for i in range(n)])  11.1 us
  transfers between devices with their start and end apart: 55, of which 30 were waited for; matrix products, arithmetic and copies ran while one was open for 1% of the time, Pallas kernels for 22%

profile of v4, /device:TPU:0, one launch (start us, length us, event | category | flops | bytes accessed | tf_op | source)
XLA Modules:
  0.0 309.6 jit_solution(3287044962832489816)
XLA Ops:
  9.0 5.1 %collective-permute-start.2 = (s32[1,8,9]{2,1,0:T(8,128)S(1)}, s32[1,8,9]{2,1,0:T(8,128)S(1)}, u32[]{:S(2)}, u32[]{:S(2)}) collective-permute-start(s32[1,8,9]{2,1,0:T(8,128)S(1)} %pad_add_fusion.1), channel_id=1, source_target_pairs={{0,24},{4,28},{8,0},{12,4},{16,8},{20,12},{24,16},{28,20},{1,25},{... | collective-permute-start | bytes 872 | tf_op jit(solution)/shard_map/ppermute | solution.py:46
  16.3 5.1 %collective-permute-start.3 = (bf16[16,192,128]{2,1,0:T(8,128)(2,1)}, bf16[16,192,128]{2,1,0:T(8,128)(2,1)S(1)}, u32[]{:S(2)}, u32[]{:S(2)}) collective-permute-start(bf16[16,192,128]{2,1,0:T(8,128)(2,1)} %bitcast_bitcast_fusion.source.own.rest_0_), channel_id=1, source_target_pairs={{0,8},{4,12},{8,16},{12,20},{16,24},{20,28},{1,9},{5,13},{9,17},{1... | collective-permute-start | bytes 2359304 | tf_op jit(solution)/shard_map/ppermute | solution.py:665
  22.8 1.5 collective-permute-start.6
  24.4 1.6 picks.1
  28.5 7.5 %plan.1.index = s32[609]{0:T(1024)} custom-call(s32[2]{0:T(128)} %pad_add_fusion.2.spot, s32[1]{0:T(128)S(6)} %copy.28.count, s32[192]{0:T(256)} %dst.1, s32[192]{0:T(256)} %src.1, s32[4,8,9]{2,1,0:T(8,128)} %copy-done.35, s32[4,8,9]{2,1,0:T(8,128)} %copy-done.37), custom_call_target="tpu_custom_call" | custom-call | flops 5000000000 | bytes 15000000 | tf_op jit(solution)/shard_map/plan/pallas_call | solution.py:549
  37.6 1.7 near.3
  40.8 2.2 collective-permute-start.7
  44.0 2.7 collective-permute-start.8
  50.6 2.8 copy-done.2
  53.4 3.8 %degree.1 = (f32[16,8,128]{2,1,0:T(8,128)S(1)}, bf16[192,128,128]{2,1,0:T(8,128)(2,1)S(1)}) custom-call(s32[609]{0:T(1024)S(1)} %copy-done.6, bf16[192,128,128]{2,1,0:T(8,128)(2,1)S(1)} %copy-done.2), custom_call_target="tpu_custom_call" | custom-call | flops 10000000 | bytes 30000 | tf_op jit(solution)/shard_map/degree/pallas_call | solution.py:536
  57.2 2.3 turn_weights.3
  59.5 4.2 %sum_early.3.early = f32[16,192,128]{2,1,0:T(8,128)S(1)} custom-call(s32[609]{0:T(1024)S(1)} %copy-done.6, bf16[192,128,128]{2,1,0:T(8,128)(2,1)S(1)} %get-tuple-element.58.tiles, bf16[16,192,128]{2,1,0:T(8,128)(2,1)S(1)} %copy-done.5, bf16[16,192,128]{2,1,0:T(8,128)(2,1)S(1)} %collective-permute-done.3.below.rest_1_, ...), custom_call_target="tpu_custom_call" | custom-call | flops 6000000000 | bytes 18000000 | tf_op jit(solution)/shard_map/sum_early/pallas_call | solution.py:536
  63.7 2.6 copy-done.8
  67.5 1.9 copy-done.14
  70.2 1.9 collective-permute-done.9.onward.rest_1_
  73.5 2.3 collective-permute-start.10
  75.8 4.7 %collective-permute-done.12.onward.rest_1_ = bf16[16,96,128]{2,1,0:T(8,128)(2,1)} collective-permute-done((bf16[16,96,128]{2,1,0:T(8,128)(2,1)S(1)}, bf16[16,96,128]{2,1,0:T(8,128)(2,1)}, u32[]{:S(2)}, u32[]{:S(2)}) %collective-permute-start.12) | collective-permute-done | bytes 393248 | tf_op jit(solution)/shard_map/ppermute | solution.py:665
  82.0 2.6 collective-permute-done.10.rest_2_
  84.6 2.9 aggregate.6.rest_0_
  87.5 1.6 collective-permute-start.14
  89.1 3.8 %collective-permute-done.16.rest_2_ = bf16[16,96,128]{2,1,0:T(8,128)(2,1)S(1)} collective-permute-done((bf16[16,96,128]{2,1,0:T(8,128)(2,1)S(1)}, bf16[16,96,128]{2,1,0:T(8,128)(2,1)S(1)}, u32[]{:S(2)}, u32[]{:S(2)}) %collective-permute-start.16) | collective-permute-done | bytes 393248 | tf_op jit(solution)/shard_map/ppermute | solution.py:51
  92.9 3.0 aggregate.7.rest_0_
  96.0 1.6 collective-permute-start.18
  98.1 2.3 turn_weights.2
  100.4 6.0 %collective-permute-done.18.rest_2_ = bf16[16,96,128]{2,1,0:T(8,128)(2,1)S(1)} collective-permute-done((bf16[16,96,128]{2,1,0:T(8,128)(2,1)S(1)}, bf16[16,96,128]{2,1,0:T(8,128)(2,1)S(1)}, u32[]{:S(2)}, u32[]{:S(2)}) %collective-permute-start.18) | collective-permute-done | bytes 393248 | tf_op jit(solution)/shard_map/ppermute | solution.py:56
  110.9 4.6 %collective-permute-start.20 = (bf16[16,192,128]{2,1,0:T(8,128)(2,1)}, bf16[16,192,128]{2,1,0:T(8,128)(2,1)S(1)}, u32[]{:S(2)}, u32[]{:S(2)}) collective-permute-start(bf16[16,192,128]{2,1,0:T(8,128)(2,1)} %update.7.source.own.rest_0_), channel_id=1, source_target_pairs={{0,8},{4,12},{8,16},{12,20},{16,24},{20,28},{1,9},{5,13},{9,17},{1... | collective-permute-start | bytes 2359304 | tf_op jit(solution)/shard_map/ppermute | solution.py:665
  117.1 10.4 %collective-permute-done.22.rest_3_ = bf16[8,192,128]{2,1,0:T(8,128)(2,1)S(1)} collective-permute-done((bf16[8,192,128]{2,1,0:T(8,128)(2,1)S(1)}, bf16[8,192,128]{2,1,0:T(8,128)(2,1)S(1)}, u32[]{:S(2)}, u32[]{:S(2)}) %collective-permute-start.22) | collective-permute-done | bytes 393248 | tf_op jit(solution)/shard_map/ppermute | solution.py:51
  128.2 3.1 %collective-permute-done.21.above.rest_2_ = bf16[16,192,128]{2,1,0:T(8,128)(2,1)S(1)} collective-permute-done((bf16[16,192,128]{2,1,0:T(8,128)(2,1)}, bf16[16,192,128]{2,1,0:T(8,128)(2,1)S(1)}, u32[]{:S(2)}, u32[]{:S(2)}) %collective-permute-start.21) | collective-permute-done | bytes 786464 | tf_op jit(solution)/shard_map/ppermute | solution.py:665
  132.6 2.4 near.4
  136.6 5.0 %collective-permute-start.24 = (bf16[16,96,128]{2,1,0:T(8,128)(2,1)}, bf16[16,96,128]{2,1,0:T(8,128)(2,1)}, u32[]{:S(2)}, u32[]{:S(2)}) collective-permute-start(bf16[16,96,128]{2,1,0:T(8,128)(2,1)} %get-tuple-element.75), channel_id=1, source_target_pairs={{0,24},{4,28},{24,0},{28,4},{8,16},{12,20},{16,8},{20,12},{1,25},{... | collective-permute-start | bytes 1179656 | tf_op jit(solution)/shard_map/ppermute | solution.py:665
  143.0 1.5 collective-permute-start.28
  144.5 1.6 collective-permute-done.23.rest_4_
  146.1 2.8 copy-done.10
  149.8 4.4 %sum_early.4.early = f32[16,192,128]{2,1,0:T(8,128)S(1)} custom-call(s32[609]{0:T(1024)S(1)} %copy-done.6, bf16[192,128,128]{2,1,0:T(8,128)(2,1)S(1)} %copy-done.10, bf16[16,192,128]{2,1,0:T(8,128)(2,1)} %update.7.source.own.rest_0_, bf16[16,192,128]{2,1,0:T(8,128)(2,1)S(1)} %collective-permute-done.20.below.rest_1_, ...), custom_call_target="tpu_custom_call" | custom-call | flops 6000000000 | bytes 18000000 | tf_op jit(solution)/shard_map/sum_early/pallas_call | solution.py:536
  155.4 1.9 copy-done.15
  158.1 9.0 %collective-permute-done.25.onward.rest_1_ = bf16[16,96,128]{2,1,0:T(8,128)(2,1)} collective-permute-done((bf16[16,96,128]{2,1,0:T(8,128)(2,1)}, bf16[16,96,128]{2,1,0:T(8,128)(2,1)}, u32[]{:S(2)}, u32[]{:S(2)}) %collective-permute-start.25) | collective-permute-done | bytes 393248 | tf_op jit(solution)/shard_map/ppermute | solution.py:665
  169.4 6.0 %collective-permute-done.28.onward.rest_1_ = bf16[16,96,128]{2,1,0:T(8,128)(2,1)} collective-permute-done((bf16[16,96,128]{2,1,0:T(8,128)(2,1)}, bf16[16,96,128]{2,1,0:T(8,128)(2,1)}, u32[]{:S(2)}, u32[]{:S(2)}) %collective-permute-start.28) | collective-permute-done | bytes 393248 | tf_op jit(solution)/shard_map/ppermute | solution.py:665
  177.6 1.8 collective-permute-done.26.rest_2_
  179.3 2.8 copy-done.11
  182.1 2.9 aggregate.8.rest_0_
  185.0 1.6 collective-permute-start.30
  187.7 2.8 aggregate.9.rest_0_
  190.5 1.6 collective-permute-start.34
  192.1 5.1 %collective-permute-done.30.rest_2_ = bf16[16,96,128]{2,1,0:T(8,128)(2,1)S(1)} collective-permute-done((bf16[16,96,128]{2,1,0:T(8,128)(2,1)S(1)}, bf16[16,96,128]{2,1,0:T(8,128)(2,1)S(1)}, u32[]{:S(2)}, u32[]{:S(2)}) %collective-permute-start.30) | collective-permute-done | bytes 393248 | tf_op jit(solution)/shard_map/ppermute | solution.py:56
  197.6 5.9 %collective-permute-done.34.rest_2_ = bf16[16,96,128]{2,1,0:T(8,128)(2,1)S(1)} collective-permute-done((bf16[16,96,128]{2,1,0:T(8,128)(2,1)S(1)}, bf16[16,96,128]{2,1,0:T(8,128)(2,1)S(1)}, u32[]{:S(2)}, u32[]{:S(2)}) %collective-permute-start.34) | collective-permute-done | bytes 393248 | tf_op jit(solution)/shard_map/ppermute | solution.py:56
  208.0 4.6 %collective-permute-start.36 = (bf16[16,192,128]{2,1,0:T(8,128)(2,1)}, bf16[16,192,128]{2,1,0:T(8,128)(2,1)S(1)}, u32[]{:S(2)}, u32[]{:S(2)}) collective-permute-start(bf16[16,192,128]{2,1,0:T(8,128)(2,1)} %update.9.source.own.rest_0_), channel_id=1, source_target_pairs={{0,8},{4,12},{8,16},{12,20},{16,24},{20,28},{1,9},{5,13},{9,17},{1... | collective-permute-start | bytes 2359304 | tf_op jit(solution)/shard_map/ppermute | solution.py:665
  214.9 9.6 %collective-permute-done.38.rest_3_ = bf16[8,192,128]{2,1,0:T(8,128)(2,1)S(1)} collective-permute-done((bf16[8,192,128]{2,1,0:T(8,128)(2,1)S(1)}, bf16[8,192,128]{2,1,0:T(8,128)(2,1)S(1)}, u32[]{:S(2)}, u32[]{:S(2)}) %collective-permute-start.38) | collective-permute-done | bytes 393248 | tf_op jit(solution)/shard_map/ppermute | solution.py:51
  225.2 3.2 %collective-permute-done.37.above.rest_2_ = bf16[16,192,128]{2,1,0:T(8,128)(2,1)S(1)} collective-permute-done((bf16[16,192,128]{2,1,0:T(8,128)(2,1)}, bf16[16,192,128]{2,1,0:T(8,128)(2,1)S(1)}, u32[]{:S(2)}, u32[]{:S(2)}) %collective-permute-start.37) | collective-permute-done | bytes 786464 | tf_op jit(solution)/shard_map/ppermute | solution.py:665
  229.7 2.5 near.5
  233.3 3.9 %collective-permute-start.40 = (bf16[16,96,128]{2,1,0:T(8,128)(2,1)}, bf16[16,96,128]{2,1,0:T(8,128)(2,1)}, u32[]{:S(2)}, u32[]{:S(2)}) collective-permute-start(bf16[16,96,128]{2,1,0:T(8,128)(2,1)} %get-tuple-element.89), channel_id=1, source_target_pairs={{0,24},{4,28},{24,0},{28,4},{8,16},{12,20},{16,8},{20,12},{1,25},{... | collective-permute-start | bytes 1179656 | tf_op jit(solution)/shard_map/ppermute | solution.py:665
  239.9 2.6 collective-permute-done.39.rest_4_
  242.5 2.8 copy-done.12
  246.3 4.4 %sum_early.5.early = f32[16,192,128]{2,1,0:T(8,128)S(1)} custom-call(s32[609]{0:T(1024)S(1)} %copy-done.6, bf16[192,128,128]{2,1,0:T(8,128)(2,1)S(1)} %copy-done.12, bf16[16,192,128]{2,1,0:T(8,128)(2,1)} %update.9.source.own.rest_0_, bf16[16,192,128]{2,1,0:T(8,128)(2,1)S(1)} %collective-permute-done.36.below.rest_1_, ...), custom_call_target="tpu_custom_call" | custom-call | flops 6000000000 | bytes 18000000 | tf_op jit(solution)/shard_map/sum_early/pallas_call | solution.py:536
  251.9 1.9 copy-done.16
  254.6 8.7 %collective-permute-done.41.onward.rest_1_ = bf16[16,96,128]{2,1,0:T(8,128)(2,1)} collective-permute-done((bf16[16,96,128]{2,1,0:T(8,128)(2,1)}, bf16[16,96,128]{2,1,0:T(8,128)(2,1)}, u32[]{:S(2)}, u32[]{:S(2)}) %collective-permute-start.41) | collective-permute-done | bytes 393248 | tf_op jit(solution)/shard_map/ppermute | solution.py:665
  265.5 6.0 %collective-permute-done.44.onward.rest_1_ = bf16[16,96,128]{2,1,0:T(8,128)(2,1)S(1)} collective-permute-done((bf16[16,96,128]{2,1,0:T(8,128)(2,1)}, bf16[16,96,128]{2,1,0:T(8,128)(2,1)S(1)}, u32[]{:S(2)}, u32[]{:S(2)}) %collective-permute-start.44) | collective-permute-done | bytes 393248 | tf_op jit(solution)/shard_map/ppermute | solution.py:665
  273.2 2.8 collective-permute-done.42.rest_2_
  276.1 2.8 copy-done.13
  278.8 2.9 aggregate.10.rest_0_
  281.7 1.6 collective-permute-start.46
  283.9 2.3 aggregate.11.rest_0_
  286.3 1.6 collective-permute-start.50
  287.8 6.0 %collective-permute-done.46.rest_2_ = bf16[16,96,128]{2,1,0:T(8,128)(2,1)S(1)} collective-permute-done((bf16[16,96,128]{2,1,0:T(8,128)(2,1)S(1)}, bf16[16,96,128]{2,1,0:T(8,128)(2,1)S(1)}, u32[]{:S(2)}, u32[]{:S(2)}) %collective-permute-start.46) | collective-permute-done | bytes 393248 | tf_op jit(solution)/shard_map/ppermute | solution.py:56
  294.4 5.4 %collective-permute-done.50.rest_2_ = bf16[16,96,128]{2,1,0:T(8,128)(2,1)S(1)} collective-permute-done((bf16[16,96,128]{2,1,0:T(8,128)(2,1)S(1)}, bf16[16,96,128]{2,1,0:T(8,128)(2,1)S(1)}, u32[]{:S(2)}, u32[]{:S(2)}) %collective-permute-start.50) | collective-permute-done | bytes 393248 | tf_op jit(solution)/shard_map/ppermute | solution.py:56
  (172 shorter events, 65.3 us)
Async XLA Ops:
  6.5 61.0 %all-gather.4.cloned.1.call-start = ((), (), s32[]{:S(2)}) async-start(), calls=%async_computation | async-start | bytes 3932160 | tf_op jit(solution)/shard_map/all_gather | solution.py:714
  8.8 146.6 %all-gather.6.cloned.1.call-start = ((), (), s32[]{:S(2)}) async-start(), calls=%async_computation.1 | async-start | bytes 3932160 | tf_op jit(solution)/shard_map/all_gather | solution.py:714
  9.0 13.7 %collective-permute-start.2 = (s32[1,8,9]{2,1,0:T(8,128)S(1)}, s32[1,8,9]{2,1,0:T(8,128)S(1)}, u32[]{:S(2)}, u32[]{:S(2)}) collective-permute-start(s32[1,8,9]{2,1,0:T(8,128)S(1)} %pad_add_fusion.1), channel_id=1, source_target_pairs={{0,24},{4,28},{8,0},{12,4},{16,8},{20,12},{24,16},{28,20},{1,25},{... | collective-permute-start | bytes 872 | tf_op jit(solution)/shard_map/ppermute | solution.py:46
  14.1 8.7 %collective-permute-start.1 = (s32[1,8,9]{2,1,0:T(8,128)S(1)}, s32[1,8,9]{2,1,0:T(8,128)S(1)}, u32[]{:S(2)}, u32[]{:S(2)}) collective-permute-start(s32[1,8,9]{2,1,0:T(8,128)S(1)} %pad_add_fusion.1), channel_id=1, source_target_pairs={{0,16},{4,20},{8,24},{12,28},{16,0},{20,4},{24,8},{28,12},{1,17},{... | collective-permute-start | bytes 872 | tf_op jit(solution)/shard_map/ppermute | solution.py:46
  14.1 8.7 %collective-permute-start = (s32[1,8,9]{2,1,0:T(8,128)S(1)}, s32[1,8,9]{2,1,0:T(8,128)S(1)}, u32[]{:S(2)}, u32[]{:S(2)}) collective-permute-start(s32[1,8,9]{2,1,0:T(8,128)S(1)} %pad_add_fusion.1), channel_id=1, source_target_pairs={{0,8},{4,12},{8,16},{12,20},{16,24},{20,28},{24,0},{28,4},{1,9},{5... | collective-permute-start | bytes 872 | tf_op jit(solution)/shard_map/ppermute | solution.py:46
  15.1 21.7 %collective-permute-start.4 = (bf16[16,192,128]{2,1,0:T(8,128)(2,1)}, bf16[16,192,128]{2,1,0:T(8,128)(2,1)S(1)}, u32[]{:S(2)}, u32[]{:S(2)}) collective-permute-start(bf16[16,192,128]{2,1,0:T(8,128)(2,1)} %bitcast_bitcast_fusion.source.own.rest_0_), channel_id=1, source_target_pairs={{8,0},{12,4},{16,8},{20,12},{24,16},{28,20},{9,1},{13,5},{17,9},{2... | collective-permute-start | bytes 2359304 | tf_op jit(solution)/shard_map/ppermute | solution.py:665
  16.3 21.3 %collective-permute-start.3 = (bf16[16,192,128]{2,1,0:T(8,128)(2,1)}, bf16[16,192,128]{2,1,0:T(8,128)(2,1)S(1)}, u32[]{:S(2)}, u32[]{:S(2)}) collective-permute-start(bf16[16,192,128]{2,1,0:T(8,128)(2,1)} %bitcast_bitcast_fusion.source.own.rest_0_), channel_id=1, source_target_pairs={{0,8},{4,12},{8,16},{12,20},{16,24},{20,28},{1,9},{5,13},{9,17},{1... | collective-permute-start | bytes 2359304 | tf_op jit(solution)/shard_map/ppermute | solution.py:665
  22.8 3.1 %copy-start.5 = (bf16[16,192,128]{2,1,0:T(8,128)(2,1)S(1)}, bf16[16,192,128]{2,1,0:T(8,128)(2,1)}, u32[]{:S(2)}) copy-start(bf16[16,192,128]{2,1,0:T(8,128)(2,1)} %bitcast_bitcast_fusion.source.own.rest_0_) | copy-start | bytes 2359300
  22.8 5.1 %collective-permute-start.6 = (s32[4,8,9]{2,1,0:T(8,128)S(1)}, s32[4,8,9]{2,1,0:T(8,128)S(1)}, u32[]{:S(2)}, u32[]{:S(2)}) collective-permute-start(s32[4,8,9]{2,1,0:T(8,128)S(1)} %pad_add_fusion.mine), channel_id=1, source_target_pairs={{0,4},{4,0},{8,12},{12,8},{16,20},{20,16},{24,28},{28,24},{1,5},{5... | collective-permute-start | bytes 3464 | tf_op jit(solution)/shard_map/ppermute | solution.py:51
  27.3 9.5 %collective-permute-start.5 = (bf16[8,192,128]{2,1,0:T(8,128)(2,1)S(1)}, bf16[8,192,128]{2,1,0:T(8,128)(2,1)S(1)}, u32[]{:S(2)}, u32[]{:S(2)}) collective-permute-start(bf16[8,192,128]{2,1,0:T(8,128)(2,1)S(1)} %pick.3), channel_id=1, source_target_pairs={{0,4},{4,0},{8,12},{12,8},{16,20},{20,16},{24,28},{28,24},{1,5},{5... | collective-permute-start | bytes 1179656 | tf_op jit(solution)/shard_map/ppermute | solution.py:51
  36.0 14.6 %copy-start.6 = (s32[609]{0:T(1024)S(1)}, s32[609]{0:T(1024)}, u32[]{:S(2)}) copy-start(s32[609]{0:T(1024)} %plan.1.index) | copy-start | bytes 7312
  40.8 16.3 %collective-permute-start.7 = (bf16[8,192,128]{2,1,0:T(8,128)(2,1)}, bf16[8,192,128]{2,1,0:T(8,128)(2,1)}, u32[]{:S(2)}, u32[]{:S(2)}) collective-permute-start(bf16[8,192,128]{2,1,0:T(8,128)(2,1)} %get-tuple-element.54), channel_id=1, source_target_pairs={{0,4},{4,0},{8,12},{12,8},{16,20},{20,16},{24,28},{28,24},{1,5},{5... | collective-permute-start | bytes 1179656 | tf_op jit(solution)/shard_map/ppermute | solution.py:51
  44.0 26.2 %collective-permute-start.8 = (bf16[16,96,128]{2,1,0:T(8,128)(2,1)}, bf16[16,96,128]{2,1,0:T(8,128)(2,1)}, u32[]{:S(2)}, u32[]{:S(2)}) collective-permute-start(bf16[16,96,128]{2,1,0:T(8,128)(2,1)} %copy-done.18), channel_id=1, source_target_pairs={{0,24},{4,28},{24,0},{28,4},{8,16},{12,20},{16,8},{20,12},{1,25},{... | collective-permute-start | bytes 1179656 | tf_op jit(solution)/shard_map/ppermute | solution.py:665
  46.7 25.5 %collective-permute-start.9 = (bf16[16,96,128]{2,1,0:T(8,128)(2,1)}, bf16[16,96,128]{2,1,0:T(8,128)(2,1)}, u32[]{:S(2)}, u32[]{:S(2)}) collective-permute-start(bf16[16,96,128]{2,1,0:T(8,128)(2,1)} %copy-done.17), channel_id=1, source_target_pairs={{8,0},{12,4},{16,24},{20,28},{9,1},{13,5},{17,25},{21,29},{10,2},{... | collective-permute-start | bytes 1179656 | tf_op jit(solution)/shard_map/ppermute | solution.py:665
  48.0 27.8 %collective-permute-start.11 = (bf16[16,96,128]{2,1,0:T(8,128)(2,1)}, bf16[16,96,128]{2,1,0:T(8,128)(2,1)}, u32[]{:S(2)}, u32[]{:S(2)}) collective-permute-start(bf16[16,96,128]{2,1,0:T(8,128)(2,1)} %get-tuple-element.65), channel_id=1, source_target_pairs={{0,24},{4,28},{24,0},{28,4},{8,16},{12,20},{16,8},{20,12},{1,25},{... | collective-permute-start | bytes 1179656 | tf_op jit(solution)/shard_map/ppermute | solution.py:665
  49.3 31.2 %collective-permute-start.12 = (bf16[16,96,128]{2,1,0:T(8,128)(2,1)S(1)}, bf16[16,96,128]{2,1,0:T(8,128)(2,1)}, u32[]{:S(2)}, u32[]{:S(2)}) collective-permute-start(bf16[16,96,128]{2,1,0:T(8,128)(2,1)S(1)} %get-tuple-element.66), channel_id=1, source_target_pairs={{8,0},{12,4},{16,24},{20,28},{9,1},{13,5},{17,25},{21,29},{10,2},{... | collective-permute-start | bytes 1179656 | tf_op jit(solution)/shard_map/ppermute | solution.py:665
  53.4 3.8 %copy-start.3 = (bf16[3,768,768]{2,1,0:T(8,128)(2,1)S(1)}, bf16[3,768,768]{2,1,0:T(8,128)(2,1)}, u32[]{:S(2)}) copy-start(bf16[3,768,768]{2,1,0:T(8,128)(2,1)} %w.1) | copy-start | bytes 10616836
  53.4 3.8 %copy-start.7 = (s32[2]{0:T(128)S(1)}, s32[2]{0:T(128)}, u32[]{:S(2)}) copy-start(s32[2]{0:T(128)} %pad_add_fusion.2.spot) | copy-start | bytes 28
  69.4 15.2 %copy-start.27 = (f32[16,192,128]{2,1,0:T(8,128)S(1)}, f32[16,192,128]{2,1,0:T(8,128)}, u32[]{:S(2)}) copy-start(f32[16,192,128]{2,1,0:T(8,128)} %copy-done.26) | copy-start | bytes 4718596
  72.2 12.4 %copy-start.9 = (bf16[192,128,128]{2,1,0:T(8,128)(2,1)S(1)}, bf16[192,128,128]{2,1,0:T(8,128)(2,1)}, u32[]{:S(2)}) copy-start(bf16[192,128,128]{2,1,0:T(8,128)(2,1)} %copy-done.8) | copy-start | bytes 18874372
  73.5 11.1 %collective-permute-start.10 = (bf16[16,96,128]{2,1,0:T(8,128)(2,1)S(1)}, bf16[16,96,128]{2,1,0:T(8,128)(2,1)S(1)}, u32[]{:S(2)}, u32[]{:S(2)}) collective-permute-start(bf16[16,96,128]{2,1,0:T(8,128)(2,1)S(1)} %far.6), channel_id=1, source_target_pairs={{0,4},{4,0},{8,12},{12,8},{16,20},{20,16},{24,28},{28,24},{1,5},{5... | collective-permute-start | bytes 1179656 | tf_op jit(solution)/shard_map/ppermute | solution.py:51
  81.7 11.3 %collective-permute-start.16 = (bf16[16,96,128]{2,1,0:T(8,128)(2,1)S(1)}, bf16[16,96,128]{2,1,0:T(8,128)(2,1)S(1)}, u32[]{:S(2)}, u32[]{:S(2)}) collective-permute-start(bf16[16,96,128]{2,1,0:T(8,128)(2,1)S(1)} %far.7), channel_id=1, source_target_pairs={{0,4},{4,0},{8,12},{12,8},{16,20},{20,16},{24,28},{28,24},{1,5},{5... | collective-permute-start | bytes 1179656 | tf_op jit(solution)/shard_map/ppermute | solution.py:51
  87.5 10.1 %collective-permute-start.14 = (bf16[16,96,128]{2,1,0:T(8,128)(2,1)S(1)}, bf16[16,96,128]{2,1,0:T(8,128)(2,1)S(1)}, u32[]{:S(2)}, u32[]{:S(2)}) collective-permute-start(bf16[16,96,128]{2,1,0:T(8,128)(2,1)S(1)} %aggregate.6.rest_0_), channel_id=1, source_target_pairs={{0,2},{1,3},{2,0},{3,1},{4,6},{5,7},{6,4},{7,5},{8,10},{9,11},{10,... | collective-permute-start | bytes 1179656 | tf_op jit(solution)/shard_map/ppermute | solution.py:56
  92.9 5.1 %copy-start.4 = (bf16[3,768,768]{2,1,0:T(8,128)(2,1)S(1)}, bf16[3,768,768]{2,1,0:T(8,128)(2,1)}, u32[]{:S(2)}) copy-start(bf16[3,768,768]{2,1,0:T(8,128)(2,1)} %w) | copy-start | bytes 10616836
  96.0 10.4 %collective-permute-start.18 = (bf16[16,96,128]{2,1,0:T(8,128)(2,1)S(1)}, bf16[16,96,128]{2,1,0:T(8,128)(2,1)S(1)}, u32[]{:S(2)}, u32[]{:S(2)}) collective-permute-start(bf16[16,96,128]{2,1,0:T(8,128)(2,1)S(1)} %aggregate.7.rest_0_), channel_id=1, source_target_pairs={{0,2},{1,3},{2,0},{3,1},{4,6},{5,7},{6,4},{7,5},{8,10},{9,11},{10,... | collective-permute-start | bytes 1179656 | tf_op jit(solution)/shard_map/ppermute | solution.py:56
  97.5 8.9 %collective-permute-start.13 = (bf16[16,96,128]{2,1,0:T(8,128)(2,1)S(1)}, bf16[16,96,128]{2,1,0:T(8,128)(2,1)S(1)}, u32[]{:S(2)}, u32[]{:S(2)}) collective-permute-start(bf16[16,96,128]{2,1,0:T(8,128)(2,1)S(1)} %aggregate.6.rest_0_), channel_id=1, source_target_pairs={{0,1},{1,0},{2,3},{3,2},{4,5},{5,4},{6,7},{7,6},{8,9},{9,8},{10,11... | collective-permute-start | bytes 1179656 | tf_op jit(solution)/shard_map/ppermute | solution.py:56
  97.6 8.9 %collective-permute-start.15 = (bf16[16,96,128]{2,1,0:T(8,128)(2,1)S(1)}, bf16[16,96,128]{2,1,0:T(8,128)(2,1)S(1)}, u32[]{:S(2)}, u32[]{:S(2)}) collective-permute-start(bf16[16,96,128]{2,1,0:T(8,128)(2,1)S(1)} %collective-permute-done.14.rest_2_), channel_id=1, source_target_pairs={{0,1},{1,0},{2,3},{3,2},{4,5},{5,4},{6,7},{7,6},{8,9},{9,8},{10,11... | collective-permute-start | bytes 1179656 | tf_op jit(solution)/shard_map/ppermute | solution.py:56
  100.3 6.7 %collective-permute-start.17 = (bf16[16,96,128]{2,1,0:T(8,128)(2,1)S(1)}, bf16[16,96,128]{2,1,0:T(8,128)(2,1)S(1)}, u32[]{:S(2)}, u32[]{:S(2)}) collective-permute-start(bf16[16,96,128]{2,1,0:T(8,128)(2,1)S(1)} %aggregate.7.rest_0_), channel_id=1, source_target_pairs={{0,1},{1,0},{2,3},{3,2},{4,5},{5,4},{6,7},{7,6},{8,9},{9,8},{10,11... | collective-permute-start | bytes 1179656 | tf_op jit(solution)/shard_map/ppermute | solution.py:56
  106.4 1.7 collective-permute-start.19
  109.6 142.3 %all-gather.8.cloned.1.call-start = ((), (), s32[]{:S(2)}) async-start(), calls=%async_computation.2 | async-start | bytes 3932160 | tf_op jit(solution)/shard_map/all_gather | solution.py:714
  109.6 21.7 %collective-permute-start.21 = (bf16[16,192,128]{2,1,0:T(8,128)(2,1)}, bf16[16,192,128]{2,1,0:T(8,128)(2,1)S(1)}, u32[]{:S(2)}, u32[]{:S(2)}) collective-permute-start(bf16[16,192,128]{2,1,0:T(8,128)(2,1)} %update.7.source.own.rest_0_), channel_id=1, source_target_pairs={{8,0},{12,4},{16,8},{20,12},{24,16},{28,20},{9,1},{13,5},{17,9},{2... | collective-permute-start | bytes 2359304 | tf_op jit(solution)/shard_map/ppermute | solution.py:665
  110.9 21.7 %collective-permute-start.20 = (bf16[16,192,128]{2,1,0:T(8,128)(2,1)}, bf16[16,192,128]{2,1,0:T(8,128)(2,1)S(1)}, u32[]{:S(2)}, u32[]{:S(2)}) collective-permute-start(bf16[16,192,128]{2,1,0:T(8,128)(2,1)} %update.7.source.own.rest_0_), channel_id=1, source_target_pairs={{0,8},{4,12},{8,16},{12,20},{16,24},{20,28},{1,9},{5,13},{9,17},{1... | collective-permute-start | bytes 2359304 | tf_op jit(solution)/shard_map/ppermute | solution.py:665
  116.8 10.7 %collective-permute-start.22 = (bf16[8,192,128]{2,1,0:T(8,128)(2,1)S(1)}, bf16[8,192,128]{2,1,0:T(8,128)(2,1)S(1)}, u32[]{:S(2)}, u32[]{:S(2)}) collective-permute-start(bf16[8,192,128]{2,1,0:T(8,128)(2,1)S(1)} %pick.4), channel_id=1, source_target_pairs={{0,4},{4,0},{8,12},{12,8},{16,20},{20,16},{24,28},{28,24},{1,5},{5... | collective-permute-start | bytes 1179656 | tf_op jit(solution)/shard_map/ppermute | solution.py:51
  135.7 10.3 %collective-permute-start.23 = (bf16[8,192,128]{2,1,0:T(8,128)(2,1)}, bf16[8,192,128]{2,1,0:T(8,128)(2,1)}, u32[]{:S(2)}, u32[]{:S(2)}) collective-permute-start(bf16[8,192,128]{2,1,0:T(8,128)(2,1)} %get-tuple-element.74), channel_id=1, source_target_pairs={{0,4},{4,0},{8,12},{12,8},{16,20},{20,16},{24,28},{28,24},{1,5},{5... | collective-permute-start | bytes 1179656 | tf_op jit(solution)/shard_map/ppermute | solution.py:51
  136.6 21.5 %collective-permute-start.24 = (bf16[16,96,128]{2,1,0:T(8,128)(2,1)}, bf16[16,96,128]{2,1,0:T(8,128)(2,1)}, u32[]{:S(2)}, u32[]{:S(2)}) collective-permute-start(bf16[16,96,128]{2,1,0:T(8,128)(2,1)} %get-tuple-element.75), channel_id=1, source_target_pairs={{0,24},{4,28},{24,0},{28,4},{8,16},{12,20},{16,8},{20,12},{1,25},{... | collective-permute-start | bytes 1179656 | tf_op jit(solution)/shard_map/ppermute | solution.py:665
  141.6 25.5 %collective-permute-start.25 = (bf16[16,96,128]{2,1,0:T(8,128)(2,1)}, bf16[16,96,128]{2,1,0:T(8,128)(2,1)}, u32[]{:S(2)}, u32[]{:S(2)}) collective-permute-start(bf16[16,96,128]{2,1,0:T(8,128)(2,1)} %get-tuple-element.76), channel_id=1, source_target_pairs={{8,0},{12,4},{16,24},{20,28},{9,1},{13,5},{17,25},{21,29},{10,2},{... | collective-permute-start | bytes 1179656 | tf_op jit(solution)/shard_map/ppermute | solution.py:665
  142.9 26.5 %collective-permute-start.27 = (bf16[16,96,128]{2,1,0:T(8,128)(2,1)}, bf16[16,96,128]{2,1,0:T(8,128)(2,1)S(1)}, u32[]{:S(2)}, u32[]{:S(2)}) collective-permute-start(bf16[16,96,128]{2,1,0:T(8,128)(2,1)} %copy-done.21), channel_id=1, source_target_pairs={{0,24},{4,28},{24,0},{28,4},{8,16},{12,20},{16,8},{20,12},{1,25},{... | collective-permute-start | bytes 1179656 | tf_op jit(solution)/shard_map/ppermute | solution.py:665
  143.0 32.4 %collective-permute-start.28 = (bf16[16,96,128]{2,1,0:T(8,128)(2,1)}, bf16[16,96,128]{2,1,0:T(8,128)(2,1)}, u32[]{:S(2)}, u32[]{:S(2)}) collective-permute-start(bf16[16,96,128]{2,1,0:T(8,128)(2,1)} %copy-done.20), channel_id=1, source_target_pairs={{8,0},{12,4},{16,24},{20,28},{9,1},{13,5},{17,25},{21,29},{10,2},{... | collective-permute-start | bytes 1179656 | tf_op jit(solution)/shard_map/ppermute | solution.py:665
  168.3 11.1 %copy-start.31 = (f32[16,192,128]{2,1,0:T(8,128)S(1)}, f32[16,192,128]{2,1,0:T(8,128)}, u32[]{:S(2)}) copy-start(f32[16,192,128]{2,1,0:T(8,128)} %copy-done.30) | copy-start | bytes 4718596
  168.3 11.1 %collective-permute-start.26 = (bf16[16,96,128]{2,1,0:T(8,128)(2,1)S(1)}, bf16[16,96,128]{2,1,0:T(8,128)(2,1)S(1)}, u32[]{:S(2)}, u32[]{:S(2)}) collective-permute-start(bf16[16,96,128]{2,1,0:T(8,128)(2,1)S(1)} %far.8), channel_id=1, source_target_pairs={{0,4},{4,0},{8,12},{12,8},{16,20},{20,16},{24,28},{28,24},{1,5},{5... | collective-permute-start | bytes 1179656 | tf_op jit(solution)/shard_map/ppermute | solution.py:51
  176.5 11.2 %collective-permute-start.32 = (bf16[16,96,128]{2,1,0:T(8,128)(2,1)S(1)}, bf16[16,96,128]{2,1,0:T(8,128)(2,1)S(1)}, u32[]{:S(2)}, u32[]{:S(2)}) collective-permute-start(bf16[16,96,128]{2,1,0:T(8,128)(2,1)S(1)} %far.9), channel_id=1, source_target_pairs={{0,4},{4,0},{8,12},{12,8},{16,20},{20,16},{24,28},{28,24},{1,5},{5... | collective-permute-start | bytes 1179656 | tf_op jit(solution)/shard_map/ppermute | solution.py:51
  185.0 12.1 %collective-permute-start.30 = (bf16[16,96,128]{2,1,0:T(8,128)(2,1)S(1)}, bf16[16,96,128]{2,1,0:T(8,128)(2,1)S(1)}, u32[]{:S(2)}, u32[]{:S(2)}) collective-permute-start(bf16[16,96,128]{2,1,0:T(8,128)(2,1)S(1)} %aggregate.8.rest_0_), channel_id=1, source_target_pairs={{0,2},{1,3},{2,0},{3,1},{4,6},{5,7},{6,4},{7,5},{8,10},{9,11},{10,... | collective-permute-start | bytes 1179656 | tf_op jit(solution)/shard_map/ppermute | solution.py:56
  190.5 13.1 %collective-permute-start.34 = (bf16[16,96,128]{2,1,0:T(8,128)(2,1)S(1)}, bf16[16,96,128]{2,1,0:T(8,128)(2,1)S(1)}, u32[]{:S(2)}, u32[]{:S(2)}) collective-permute-start(bf16[16,96,128]{2,1,0:T(8,128)(2,1)S(1)} %aggregate.9.rest_0_), channel_id=1, source_target_pairs={{0,2},{1,3},{2,0},{3,1},{4,6},{5,7},{6,4},{7,5},{8,10},{9,11},{10,... | collective-permute-start | bytes 1179656 | tf_op jit(solution)/shard_map/ppermute | solution.py:56
  192.1 11.5 %collective-permute-start.29 = (bf16[16,96,128]{2,1,0:T(8,128)(2,1)S(1)}, bf16[16,96,128]{2,1,0:T(8,128)(2,1)S(1)}, u32[]{:S(2)}, u32[]{:S(2)}) collective-permute-start(bf16[16,96,128]{2,1,0:T(8,128)(2,1)S(1)} %aggregate.8.rest_0_), channel_id=1, source_target_pairs={{0,1},{1,0},{2,3},{3,2},{4,5},{5,4},{6,7},{7,6},{8,9},{9,8},{10,11... | collective-permute-start | bytes 1179656 | tf_op jit(solution)/shard_map/ppermute | solution.py:56
  197.1 6.4 %collective-permute-start.31 = (bf16[16,96,128]{2,1,0:T(8,128)(2,1)S(1)}, bf16[16,96,128]{2,1,0:T(8,128)(2,1)S(1)}, u32[]{:S(2)}, u32[]{:S(2)}) collective-permute-start(bf16[16,96,128]{2,1,0:T(8,128)(2,1)S(1)} %collective-permute-done.30.rest_2_), channel_id=1, source_target_pairs={{0,1},{1,0},{2,3},{3,2},{4,5},{5,4},{6,7},{7,6},{8,9},{9,8},{10,11... | collective-permute-start | bytes 1179656 | tf_op jit(solution)/shard_map/ppermute | solution.py:56
  197.1 7.0 %collective-permute-start.33 = (bf16[16,96,128]{2,1,0:T(8,128)(2,1)S(1)}, bf16[16,96,128]{2,1,0:T(8,128)(2,1)S(1)}, u32[]{:S(2)}, u32[]{:S(2)}) collective-permute-start(bf16[16,96,128]{2,1,0:T(8,128)(2,1)S(1)} %aggregate.9.rest_0_), channel_id=1, source_target_pairs={{0,1},{1,0},{2,3},{3,2},{4,5},{5,4},{6,7},{7,6},{8,9},{9,8},{10,11... | collective-permute-start | bytes 1179656 | tf_op jit(solution)/shard_map/ppermute | solution.py:56
  203.5 1.7 collective-permute-start.35
  206.7 21.7 %collective-permute-start.37 = (bf16[16,192,128]{2,1,0:T(8,128)(2,1)}, bf16[16,192,128]{2,1,0:T(8,128)(2,1)S(1)}, u32[]{:S(2)}, u32[]{:S(2)}) collective-permute-start(bf16[16,192,128]{2,1,0:T(8,128)(2,1)} %update.9.source.own.rest_0_), channel_id=1, source_target_pairs={{8,0},{12,4},{16,8},{20,12},{24,16},{28,20},{9,1},{13,5},{17,9},{2... | collective-permute-start | bytes 2359304 | tf_op jit(solution)/shard_map/ppermute | solution.py:665
  208.0 21.7 %collective-permute-start.36 = (bf16[16,192,128]{2,1,0:T(8,128)(2,1)}, bf16[16,192,128]{2,1,0:T(8,128)(2,1)S(1)}, u32[]{:S(2)}, u32[]{:S(2)}) collective-permute-start(bf16[16,192,128]{2,1,0:T(8,128)(2,1)} %update.9.source.own.rest_0_), channel_id=1, source_target_pairs={{0,8},{4,12},{8,16},{12,20},{16,24},{20,28},{1,9},{5,13},{9,17},{1... | collective-permute-start | bytes 2359304 | tf_op jit(solution)/shard_map/ppermute | solution.py:665
  213.9 10.6 %collective-permute-start.38 = (bf16[8,192,128]{2,1,0:T(8,128)(2,1)S(1)}, bf16[8,192,128]{2,1,0:T(8,128)(2,1)S(1)}, u32[]{:S(2)}, u32[]{:S(2)}) collective-permute-start(bf16[8,192,128]{2,1,0:T(8,128)(2,1)S(1)} %pick.5), channel_id=1, source_target_pairs={{0,4},{4,0},{8,12},{12,8},{16,20},{20,16},{24,28},{28,24},{1,5},{5... | collective-permute-start | bytes 1179656 | tf_op jit(solution)/shard_map/ppermute | solution.py:51
  232.2 10.3 %collective-permute-start.39 = (bf16[8,192,128]{2,1,0:T(8,128)(2,1)}, bf16[8,192,128]{2,1,0:T(8,128)(2,1)}, u32[]{:S(2)}, u32[]{:S(2)}) collective-permute-start(bf16[8,192,128]{2,1,0:T(8,128)(2,1)} %get-tuple-element.88), channel_id=1, source_target_pairs={{0,4},{4,0},{8,12},{12,8},{16,20},{20,16},{24,28},{28,24},{1,5},{5... | collective-permute-start | bytes 1179656 | tf_op jit(solution)/shard_map/ppermute | solution.py:51
  233.3 21.2 %collective-permute-start.40 = (bf16[16,96,128]{2,1,0:T(8,128)(2,1)}, bf16[16,96,128]{2,1,0:T(8,128)(2,1)}, u32[]{:S(2)}, u32[]{:S(2)}) collective-permute-start(bf16[16,96,128]{2,1,0:T(8,128)(2,1)} %get-tuple-element.89), channel_id=1, source_target_pairs={{0,24},{4,28},{24,0},{28,4},{8,16},{12,20},{16,8},{20,12},{1,25},{... | collective-permute-start | bytes 1179656 | tf_op jit(solution)/shard_map/ppermute | solution.py:665
  237.2 26.1 %collective-permute-start.41 = (bf16[16,96,128]{2,1,0:T(8,128)(2,1)}, bf16[16,96,128]{2,1,0:T(8,128)(2,1)}, u32[]{:S(2)}, u32[]{:S(2)}) collective-permute-start(bf16[16,96,128]{2,1,0:T(8,128)(2,1)} %get-tuple-element.90), channel_id=1, source_target_pairs={{8,0},{12,4},{16,24},{20,28},{9,1},{13,5},{17,25},{21,29},{10,2},{... | collective-permute-start | bytes 1179656 | tf_op jit(solution)/shard_map/ppermute | solution.py:665
  238.5 27.0 %collective-permute-start.43 = (bf16[16,96,128]{2,1,0:T(8,128)(2,1)}, bf16[16,96,128]{2,1,0:T(8,128)(2,1)S(1)}, u32[]{:S(2)}, u32[]{:S(2)}) collective-permute-start(bf16[16,96,128]{2,1,0:T(8,128)(2,1)} %get-tuple-element.93), channel_id=1, source_target_pairs={{0,24},{4,28},{24,0},{28,4},{8,16},{12,20},{16,8},{20,12},{1,25},{... | collective-permute-start | bytes 1179656 | tf_op jit(solution)/shard_map/ppermute | solution.py:665
  238.6 32.9 %collective-permute-start.44 = (bf16[16,96,128]{2,1,0:T(8,128)(2,1)}, bf16[16,96,128]{2,1,0:T(8,128)(2,1)S(1)}, u32[]{:S(2)}, u32[]{:S(2)}) collective-permute-start(bf16[16,96,128]{2,1,0:T(8,128)(2,1)} %copy-done.19), channel_id=1, source_target_pairs={{8,0},{12,4},{16,24},{20,28},{9,1},{13,5},{17,25},{21,29},{10,2},{... | collective-permute-start | bytes 1179656 | tf_op jit(solution)/shard_map/ppermute | solution.py:665
  264.5 11.6 %copy-start.29 = (f32[16,192,128]{2,1,0:T(8,128)S(1)}, f32[16,192,128]{2,1,0:T(8,128)}, u32[]{:S(2)}) copy-start(f32[16,192,128]{2,1,0:T(8,128)} %copy-done.28) | copy-start | bytes 4718596
  264.5 11.6 %collective-permute-start.42 = (bf16[16,96,128]{2,1,0:T(8,128)(2,1)S(1)}, bf16[16,96,128]{2,1,0:T(8,128)(2,1)S(1)}, u32[]{:S(2)}, u32[]{:S(2)}) collective-permute-start(bf16[16,96,128]{2,1,0:T(8,128)(2,1)S(1)} %far.10), channel_id=1, source_target_pairs={{0,4},{4,0},{8,12},{12,8},{16,20},{20,16},{24,28},{28,24},{1,5},{5... | collective-permute-start | bytes 1179656 | tf_op jit(solution)/shard_map/ppermute | solution.py:51
  272.2 11.7 %collective-permute-start.48 = (bf16[16,96,128]{2,1,0:T(8,128)(2,1)S(1)}, bf16[16,96,128]{2,1,0:T(8,128)(2,1)S(1)}, u32[]{:S(2)}, u32[]{:S(2)}) collective-permute-start(bf16[16,96,128]{2,1,0:T(8,128)(2,1)S(1)} %far.11), channel_id=1, source_target_pairs={{0,4},{4,0},{8,12},{12,8},{16,20},{20,16},{24,28},{28,24},{1,5},{5... | collective-permute-start | bytes 1179656 | tf_op jit(solution)/shard_map/ppermute | solution.py:51
  281.7 12.1 %collective-permute-start.46 = (bf16[16,96,128]{2,1,0:T(8,128)(2,1)S(1)}, bf16[16,96,128]{2,1,0:T(8,128)(2,1)S(1)}, u32[]{:S(2)}, u32[]{:S(2)}) collective-permute-start(bf16[16,96,128]{2,1,0:T(8,128)(2,1)S(1)} %aggregate.10.rest_0_), channel_id=1, source_target_pairs={{0,2},{1,3},{2,0},{3,1},{4,6},{5,7},{6,4},{7,5},{8,10},{9,11},{10,... | collective-permute-start | bytes 1179656 | tf_op jit(solution)/shard_map/ppermute | solution.py:56
  286.3 13.5 %collective-permute-start.50 = (bf16[16,96,128]{2,1,0:T(8,128)(2,1)S(1)}, bf16[16,96,128]{2,1,0:T(8,128)(2,1)S(1)}, u32[]{:S(2)}, u32[]{:S(2)}) collective-permute-start(bf16[16,96,128]{2,1,0:T(8,128)(2,1)S(1)} %aggregate.11.rest_0_), channel_id=1, source_target_pairs={{0,2},{1,3},{2,0},{3,1},{4,6},{5,7},{6,4},{7,5},{8,10},{9,11},{10,... | collective-permute-start | bytes 1179656 | tf_op jit(solution)/shard_map/ppermute | solution.py:56
  287.8 11.9 %collective-permute-start.45 = (bf16[16,96,128]{2,1,0:T(8,128)(2,1)S(1)}, bf16[16,96,128]{2,1,0:T(8,128)(2,1)S(1)}, u32[]{:S(2)}, u32[]{:S(2)}) collective-permute-start(bf16[16,96,128]{2,1,0:T(8,128)(2,1)S(1)} %aggregate.10.rest_0_), channel_id=1, source_target_pairs={{0,1},{1,0},{2,3},{3,2},{4,5},{5,4},{6,7},{7,6},{8,9},{9,8},{10,11... | collective-permute-start | bytes 1179656 | tf_op jit(solution)/shard_map/ppermute | solution.py:56
  293.9 5.9 %collective-permute-start.47 = (bf16[16,96,128]{2,1,0:T(8,128)(2,1)S(1)}, bf16[16,96,128]{2,1,0:T(8,128)(2,1)S(1)}, u32[]{:S(2)}, u32[]{:S(2)}) collective-permute-start(bf16[16,96,128]{2,1,0:T(8,128)(2,1)S(1)} %collective-permute-done.46.rest_2_), channel_id=1, source_target_pairs={{0,1},{1,0},{2,3},{3,2},{4,5},{5,4},{6,7},{7,6},{8,9},{9,8},{10,11... | collective-permute-start | bytes 1179656 | tf_op jit(solution)/shard_map/ppermute | solution.py:56
  293.9 6.5 %collective-permute-start.49 = (bf16[16,96,128]{2,1,0:T(8,128)(2,1)S(1)}, bf16[16,96,128]{2,1,0:T(8,128)(2,1)S(1)}, u32[]{:S(2)}, u32[]{:S(2)}) collective-permute-start(bf16[16,96,128]{2,1,0:T(8,128)(2,1)S(1)} %aggregate.11.rest_0_), channel_id=1, source_target_pairs={{0,1},{1,0},{2,3},{3,2},{4,5},{5,4},{6,7},{7,6},{8,9},{9,8},{10,11... | collective-permute-start | bytes 1179656 | tf_op jit(solution)/shard_map/ppermute | solution.py:56
  299.7 1.7 collective-permute-start.51
  (29 other events, 46.2 us)
Sparse Core Ops, SparseCore 0:
  8.9 31.2 all-gather.3
  109.7 28.5 all-gather.5
  206.9 29.2 all-gather.7
